TPU v7x, 128 devices: a whole 4x4x4 slice. The times are simulated.
128 devices in a mesh: seq: 32 (over z_lo, x, y), head: 4 (over z_hi, core).
Axes of the slice: x: 4, y: 4, z: 4 (z_hi: 2, z_lo: 2; z = z_hi * 2 + z_lo), core: 2. Of those that a mesh axis runs over, the one named last changes fastest.
Arguments:
- tokens: bfloat16 [8192, 2048], P('seq'), may hold values from -6 to 6
- segment_ids: int32 [8192], P('seq'), may hold values from 0 to 2, as said below
- cotangent: bfloat16 [8192, 2048], P('seq'), may hold values from -6 to 6
- norm1_gain: float32 [2048], replicated, may hold values from 0.5 to 1.5
- x_weight: bfloat16 [2048, 3072], P(None, 'head'), may hold values from -0.125 to 0.125
- z_weight: bfloat16 [2048, 3072], P(None, 'head'), may hold values from -0.125 to 0.125
- bc_weight: bfloat16 [2048, 512], replicated, may hold values from -0.125 to 0.125
- dt_weight: bfloat16 [2048, 48], P(None, 'head'), may hold values from -0.125 to 0.125
- x_conv: float32 [4, 3072], P(None, 'head'), may hold values from -3 to 3
- bc_conv: float32 [4, 512], replicated, may hold values from -0.6 to 0.6
- dt_bias: float32 [48], P('head'), may hold values from -1 to 1
- decay_rate: float32 [48], P('head'), may hold values from 0.00012207031 to 0.2
- skip_gain: float32 [48], P('head'), may hold values from 0.5 to 1.5
- out_weight: bfloat16 [3072, 2048], P('head'), may hold values from -0.0546875 to 0.0546875
- query_weight: bfloat16 [2048, 1024], P(None, 'head'), may hold values from -0.125 to 0.125
- kv_weight: bfloat16 [2048, 512], replicated, may hold values from -0.125 to 0.125
- attn_weight: bfloat16 [1024, 2048], P('head'), may hold values from -1.5 to 1.5
- norm2_gain: float32 [2048], replicated, may hold values from 0.5 to 1.5
- gate_weight: bfloat16 [2048, 4096], P(None, 'head'), may hold values from -0.125 to 0.125
- up_weight: bfloat16 [2048, 4096], P(None, 'head'), may hold values from -0.125 to 0.125
- down_weight: bfloat16 [4096, 2048], P('head'), may hold values from -0.09375 to 0.09375
Outputs:
- output: bfloat16 [8192, 2048], P('seq')
- grad_tokens: float32 [8192, 2048], P('seq')
- grad_norm1_gain: float32 [2048], replicated
- grad_x_weight: float32 [2048, 3072], P('seq', 'head')
- grad_z_weight: float32 [2048, 3072], P('seq', 'head')
- grad_bc_weight: float32 [2048, 512], replicated
- grad_dt_weight: float32 [2048, 48], P('seq', 'head')
- grad_x_conv: float32 [4, 3072], replicated
- grad_bc_conv: float32 [4, 512], replicated
- grad_dt_bias: float32 [48], replicated
- grad_decay_rate: float32 [48], replicated
- grad_skip_gain: float32 [48], replicated
- grad_out_weight: float32 [3072, 2048], P('head', 'seq')
- grad_query_weight: float32 [2048, 1024], P('seq', 'head')
- grad_kv_weight: float32 [2048, 512], replicated
- grad_attn_weight: float32 [1024, 2048], P('head', 'seq')
- grad_norm2_gain: float32 [2048], replicated
- grad_gate_weight: float32 [2048, 4096], P('seq', 'head')
- grad_up_weight: float32 [2048, 4096], P('seq', 'head')
- grad_down_weight: float32 [4096, 2048], P('head', 'seq')
Inputs may be any that keep to these rules, and one draw needn't show every extreme that they name: `segment_ids`: never decreasing; document 1 begins within the first 256 tokens and document 2 within the last 256.
All inputs are finite; a program needn't handle non-finite values.
Results may differ from a plain program's by a relative error of at most 0.03.
Values may be sent and summed in bfloat16 or wider, within the bound.
A program may use at most 256 MiB of HBM per device.

v0:
```python
import math

import jax
import jax.numpy as jnp
from jax import lax
from jax.sharding import Mesh
from jax.sharding import PartitionSpec as P

SSM_HEADS = 48
SSM_DIM = 64
STATE = 256
CONV = 4
QHEADS = 8
KVHEADS = 2
HEAD_DIM = 128
SEQ = ("seq_0", "seq_1", "seq_2")
SEQ_HEAD = ("seq_0", "seq_1", "seq_2", "head")


EPSILON = 1e-05
ROPE_BASE = 100000000000.0
HIGHEST = lax.Precision.HIGHEST


def passed_along(array, axis, by):
    devices = lax.axis_size(axis)
    pairs = [(i, i + by) for i in range(devices) if 0 <= i + by < devices]
    return lax.ppermute(array, axis, pairs)


def nothing_yet(array, identity):
    return jax.tree.map(
        lambda a, e: jnp.broadcast_to(jnp.asarray(e, a.dtype), a.shape), array, identity
    )


def carried_in(array, axes, combine, identity):
    before = start = nothing_yet(array, identity)
    subtotal = array
    for axis in reversed(axes):
        devices, index = (lax.axis_size(axis), lax.axis_index(axis))
        pieces = jax.tree.map(
            lambda part, kind: lax.all_gather(part.astype(kind), axis),
            subtotal,
            (jnp.bfloat16, jnp.bfloat16),
        )
        inside, subtotal = (start, start)
        for k in range(devices):
            passed = k < index
            subtotal = combine(
                subtotal, jax.tree.map(lambda part, own: part[k].astype(own.dtype), pieces, array)
            )
            inside = jax.tree.map(lambda new, old: jnp.where(passed, new, old), subtotal, inside)
        before = combine(inside, before)
    return before


def side_by_side(arrays, axis, dim, along):
    widths = [math.prod(a.shape[along:]) for a in arrays]
    both = jnp.concatenate(
        [a.reshape(*a.shape[:along], w) for a, w in zip(arrays, widths)], axis=along
    )
    whole = lax.all_gather(both, axis, axis=dim, tiled=True)
    tiles = jnp.split(whole, [sum(widths[:k]) for k in range(1, len(widths))], axis=along)
    return tuple((b.reshape(*whole.shape[:along], *a.shape[along:]) for a, b in zip(arrays, tiles)))


def entering(array, axes, combine, identity):
    before = start = nothing_yet(array, identity)
    subtotal = array
    for axis in reversed(axes):
        devices, index = (lax.axis_size(axis), lax.axis_index(axis))
        pieces = jax.tree.map(lambda part: lax.all_gather(part, axis), subtotal)
        inside, subtotal = (start, start)
        for k in reversed(range(devices)):
            passed = k > index
            subtotal = combine(subtotal, jax.tree.map(lambda part: part[k], pieces))
            inside = jax.tree.map(lambda new, old: jnp.where(passed, new, old), subtotal, inside)
        before = combine(inside, before)
    return before


def together(arrays, axis):
    line, at, finished = (jnp.concatenate([a.reshape(-1) for a in arrays]), 0, [])
    subtotal = lax.psum(line, axis)
    for a in arrays:
        finished.append(subtotal[at : at + a.size].reshape(a.shape))
        at += a.size
    return tuple(finished)


def in_one_piece(arrays, axis, dim, along):
    ends, at = ([], 0)
    for a in arrays[:-1]:
        at += a.shape[along]
        ends.append(at)
    both = jnp.concatenate(arrays, axis=along)
    return tuple(
        jnp.split(lax.psum_scatter(both, axis, scatter_dimension=dim, tiled=True), ends, axis=along)
    )


def plain_dot(left_side, right_side):
    return jnp.dot(left_side, right_side, preferred_element_type=jnp.float32)


def dot_across(left_side, right_side):
    return lax.dot_general(
        left_side, right_side, (((0,), (0,)), ((), ())), preferred_element_type=jnp.float32
    )


def dot_back(left_side, right_side):
    return lax.dot_general(
        left_side, right_side, (((1,), (1,)), ((), ())), preferred_element_type=jnp.float32
    )


def rms_norm(values, scales):
    return values * lax.rsqrt(jnp.mean(values * values, -1, keepdims=True) + EPSILON) * scales


def rope_turn(values, positions, direction):
    half_dim = values.shape[-1] // 2
    frequency = ROPE_BASE ** (-(jnp.arange(half_dim).astype(jnp.float32) * 2.0 / values.shape[-1]))
    angles = positions.astype(jnp.float32)[:, None] * frequency[None, :]
    cosine = jnp.cos(angles)[:, None, :]
    sine_part = direction * jnp.sin(angles)[:, None, :]
    first_half = values[..., :half_dim]
    second_half = values[..., half_dim:]
    return jnp.concatenate(
        [
            first_half * cosine - second_half * sine_part,
            second_half * cosine + first_half * sine_part,
        ],
        -1,
    )


def conv_taps(extended, seg_extended, kernel):
    tap_count = kernel.shape[0]
    row_count = extended.shape[0] - tap_count + 1
    own_segment = seg_extended[tap_count - 1 :]
    running_sum = jnp.zeros((row_count, extended.shape[1]), jnp.float32)
    for tap_index in range(tap_count):
        same_doc = seg_extended[tap_index : tap_index + row_count] == own_segment
        running_sum = running_sum + kernel[tap_index] * jnp.where(
            same_doc[:, None], extended[tap_index : tap_index + row_count], 0.0
        )
    return running_sum


def state_part(x_values, step_sizes, b_matrix, rates, segment, seg_before):
    cumulative = jnp.cumsum(-step_sizes * rates, 0)
    carry_weight = (
        jnp.exp(cumulative[-1][None, :] - cumulative)
        * (segment == segment[-1]).astype(jnp.float32)[:, None]
    )
    moved = x_values * (step_sizes * carry_weight)[:, :, None]
    local_state = jnp.einsum("jhp,jn->hpn", moved, b_matrix, precision=HIGHEST)
    through = jnp.exp(cumulative[-1]) * (segment[-1] == seg_before).astype(jnp.float32)
    return (local_state, through)


def output_part(x_values, step_sizes, cb_product, c_matrix, rates, segment, seg_before, state_in):
    cumulative = jnp.cumsum(-step_sizes * rates, 0)
    row_index = jnp.arange(segment.shape[0])
    causal = (row_index[None, :] <= row_index[:, None]) & (segment[None, :] == segment[:, None])
    gaps = jnp.where(causal[:, :, None], cumulative[:, None, :] - cumulative[None, :, :], -jnp.inf)
    mixing = jnp.exp(gaps) * cb_product[:, :, None]
    moved = x_values * step_sizes[:, :, None]
    inner = jnp.einsum("ijh,jhp->ihp", mixing, moved, precision=HIGHEST)
    entry = jnp.exp(cumulative) * (segment == seg_before).astype(jnp.float32)[:, None]
    outer = jnp.einsum("in,hpn->ihp", c_matrix, state_in, precision=HIGHEST) * entry[:, :, None]
    return inner + outer


def combine_states(earlier, later):
    return (earlier[0] * later[0], later[0][:, None, None] * earlier[1] + later[1])


def place_slice(length_shape, piece, start_at, axis_num):
    return lax.dynamic_update_slice_in_dim(
        jnp.zeros(length_shape, jnp.float32), piece, start_at, axis_num
    )


def on_device(
    tokens,
    segment_ids,
    cotangent,
    norm1_gain,
    x_weight,
    z_weight,
    bc_weight,
    dt_weight,
    x_conv,
    bc_conv,
    dt_bias,
    decay_rate,
    skip_gain,
    out_weight,
    query_weight,
    kv_weight,
    attn_weight,
    norm2_gain,
    gate_weight,
    up_weight,
    down_weight,
):
    row_count = tokens.shape[0]
    seq_index = lax.axis_index(SEQ)
    head_index = lax.axis_index("head")
    lead_head = (head_index == 0).astype(jnp.float32)
    edge_rows = CONV - 1
    heads_local = decay_rate.shape[0]
    inner_local = x_weight.shape[1]
    qheads_local = query_weight.shape[1] // HEAD_DIM
    positions = seq_index * row_count + jnp.arange(row_count)
    x_input = tokens.astype(jnp.float32)
    normed_f, norm_back = jax.vjp(rms_norm, x_input, norm1_gain)
    normed = normed_f.astype(jnp.bfloat16)
    x_pre = plain_dot(normed, x_weight).astype(jnp.bfloat16)
    z_val = plain_dot(normed, z_weight)
    bc_pre = plain_dot(normed, bc_weight).astype(jnp.bfloat16)
    dt_raw = plain_dot(normed, dt_weight)
    seg_wire = segment_ids.astype(jnp.bfloat16)
    edge_x, edge_bc, edge_seg = passed_along(
        (x_pre[-edge_rows:], bc_pre[-edge_rows:], seg_wire[-edge_rows:]), SEQ, 1
    )
    seg_extended = jnp.concatenate([edge_seg.astype(jnp.int32), segment_ids])
    seg_before = seg_extended[edge_rows - 1]
    x_extended = jnp.concatenate([edge_x, x_pre]).astype(jnp.float32)
    bc_extended = jnp.concatenate([edge_bc, bc_pre]).astype(jnp.float32)

    def conv_silu(extended, kernel):
        return jax.nn.silu(conv_taps(extended, seg_extended, kernel))

    x_act_f, x_conv_back = jax.vjp(conv_silu, x_extended, x_conv)
    bc_act_f, bc_conv_back = jax.vjp(conv_silu, bc_extended, bc_conv)
    x_flat = lax.optimization_barrier(x_act_f.astype(jnp.bfloat16)).astype(jnp.float32)
    x_heads = x_flat.reshape(row_count, heads_local, SSM_DIM)
    bc_low_act = bc_act_f.astype(jnp.bfloat16)
    bc_act = lax.optimization_barrier(bc_low_act).astype(jnp.float32)
    b_matrix = bc_act[:, :STATE]
    c_matrix = bc_act[:, STATE:]
    cb_product = dot_back(bc_low_act[:, STATE:], bc_low_act[:, :STATE])
    dt_pre = dt_raw + dt_bias
    step_sizes = jax.nn.softplus(dt_pre)

    def state_fn(x_values, step_vals, b_vals, rate_vals):
        return state_part(x_values, step_vals, b_vals, rate_vals, segment_ids, seg_before)

    (local_state, through), state_part_back = jax.vjp(
        state_fn, x_heads, step_sizes, b_matrix, decay_rate
    )
    start_value = (jnp.ones_like(through), jnp.zeros_like(local_state))
    _, state_in = carried_in((through, local_state), SEQ, combine_states, start_value)

    def output_fn(x_values, step_vals, cb_vals, c_vals, rate_vals, entry_state):
        return output_part(
            x_values, step_vals, cb_vals, c_vals, rate_vals, segment_ids, seg_before, entry_state
        )

    ssm_core, output_back = jax.vjp(
        output_fn, x_heads, step_sizes, cb_product, c_matrix, decay_rate, state_in
    )
    ssm_out = (ssm_core + skip_gain[None, :, None] * x_heads).reshape(row_count, inner_local)
    z_gate = jax.nn.silu(z_val)
    gated_out = (ssm_out * z_gate).astype(jnp.bfloat16)
    group_size = QHEADS // KVHEADS
    kv_index = head_index * qheads_local // group_size
    key_cols = lax.dynamic_slice_in_dim(kv_weight, kv_index * HEAD_DIM, HEAD_DIM, 1)
    value_cols = lax.dynamic_slice_in_dim(kv_weight, (KVHEADS + kv_index) * HEAD_DIM, HEAD_DIM, 1)
    query_raw = plain_dot(normed, query_weight).reshape(row_count, qheads_local, HEAD_DIM)
    queries = rope_turn(query_raw, positions, 1.0).astype(jnp.bfloat16)
    key_own = rope_turn(plain_dot(normed, key_cols)[:, None, :], positions, 1.0)[:, 0, :].astype(
        jnp.bfloat16
    )
    value_own = plain_dot(normed, value_cols).astype(jnp.bfloat16)
    all_keys, all_values, all_segs = side_by_side((key_own, value_own, seg_wire), SEQ, 0, 1)
    key_positions = jnp.arange(all_keys.shape[0])
    visible = (key_positions[None, :] <= positions[:, None]) & (
        all_segs.astype(jnp.int32)[None, :] == segment_ids[:, None]
    )
    score_scale = HEAD_DIM ** (-0.5)
    scores = (
        jnp.einsum("ihd,jd->hij", queries, all_keys, preferred_element_type=jnp.float32)
        * score_scale
    )
    scores = jnp.where(visible[None], scores, -1e30)
    row_max = jnp.max(scores, -1, keepdims=True)
    exp_scores = jnp.exp(scores - row_max)
    attn_probs = exp_scores / jnp.sum(exp_scores, -1, keepdims=True)
    probs_low = attn_probs.astype(jnp.bfloat16)
    attended = jnp.einsum("hij,jd->ihd", probs_low, all_values, preferred_element_type=jnp.float32)
    attended_low = attended.reshape(row_count, qheads_local * HEAD_DIM).astype(jnp.bfloat16)
    mixer_part = plain_dot(gated_out, out_weight) + plain_dot(attended_low, attn_weight)
    mixer_sum = lax.psum(mixer_part, "head")
    hidden_in = x_input + mixer_sum
    normed_two_f, norm_two_back = jax.vjp(rms_norm, hidden_in, norm2_gain)
    normed_two = normed_two_f.astype(jnp.bfloat16)
    gate_val = plain_dot(normed_two, gate_weight)
    up_val = plain_dot(normed_two, up_weight)
    gate_act = jax.nn.silu(gate_val)
    hidden = (gate_act * up_val).astype(jnp.bfloat16)
    ffn_total = lax.psum(plain_dot(hidden, down_weight).astype(jnp.bfloat16), "head").astype(
        jnp.float32
    )
    output = (hidden_in + ffn_total).astype(jnp.bfloat16)
    grad_hidden = dot_back(cotangent, down_weight)
    gate_sig = jax.nn.sigmoid(gate_val)
    grad_gate = (grad_hidden * up_val * gate_sig * (1.0 + gate_val * (1.0 - gate_sig))).astype(
        jnp.bfloat16
    )
    grad_up = (grad_hidden * gate_act).astype(jnp.bfloat16)
    grad_down_w = dot_across(hidden, cotangent)
    grad_gate_w = dot_across(normed_two, grad_gate)
    grad_up_w = dot_across(normed_two, grad_up)
    grad_normed_two = lax.psum(
        (dot_back(grad_gate, gate_weight) + dot_back(grad_up, up_weight)).astype(jnp.bfloat16),
        "head",
    ).astype(jnp.float32)
    grad_from_two, grad_gain_two = norm_two_back(grad_normed_two)
    grad_hidden_in = grad_from_two + cotangent.astype(jnp.float32)
    grad_mix = grad_hidden_in.astype(jnp.bfloat16)
    grad_gated = dot_back(grad_mix, out_weight)
    grad_out_w = dot_across(gated_out, grad_mix)
    grad_attended = (
        dot_back(grad_mix, attn_weight)
        .astype(jnp.bfloat16)
        .reshape(row_count, qheads_local, HEAD_DIM)
    )
    grad_attn_w = dot_across(attended_low, grad_mix)
    z_sig = jax.nn.sigmoid(z_val)
    grad_z = (grad_gated * ssm_out * z_sig * (1.0 + z_val * (1.0 - z_sig))).astype(jnp.bfloat16)
    grad_ssm = (grad_gated * z_gate).reshape(row_count, heads_local, SSM_DIM)
    grad_skip = jnp.sum(grad_ssm * x_heads, (0, 2))
    out_grads = output_back(grad_ssm)
    _, state_grad = entering((through, out_grads[5]), SEQ, combine_states, start_value)
    grad_through = jnp.sum(state_grad * state_in, (1, 2))
    state_grads = state_part_back((state_grad, grad_through))
    grad_cb = out_grads[2]
    grad_b_total = state_grads[2] + jnp.dot(grad_cb.T, c_matrix, precision=HIGHEST)
    grad_c_total = out_grads[3] + jnp.dot(grad_cb, b_matrix, precision=HIGHEST)
    grad_x_heads = out_grads[0] + state_grads[0] + skip_gain[None, :, None] * grad_ssm
    grad_steps = out_grads[1] + state_grads[1]
    grad_bc_act = jnp.concatenate([grad_b_total, grad_c_total], -1)
    grad_rate = out_grads[4] + state_grads[3]
    grad_dt_pre = grad_steps * jax.nn.sigmoid(dt_pre)
    grad_dt_raw = grad_dt_pre.astype(jnp.bfloat16)
    grad_bias = jnp.sum(grad_dt_pre, 0)
    grad_x_ext, grad_x_conv = x_conv_back(grad_x_heads.reshape(row_count, inner_local))
    grad_bc_ext, grad_bc_conv = bc_conv_back(grad_bc_act)
    from_next_x, from_next_bc = passed_along(
        (grad_x_ext[:edge_rows], grad_bc_ext[:edge_rows]), SEQ, -1
    )
    grad_x_pre = grad_x_ext[edge_rows:].at[-edge_rows:].add(from_next_x).astype(jnp.bfloat16)
    grad_bc_part = grad_bc_ext[edge_rows:].at[-edge_rows:].add(from_next_bc)
    grad_probs = jnp.einsum(
        "ihd,jd->hij", grad_attended, all_values, preferred_element_type=jnp.float32
    )
    row_dot = jnp.sum(attn_probs * grad_probs, -1, keepdims=True)
    grad_scores = (attn_probs * (grad_probs - row_dot)).astype(jnp.bfloat16)
    grad_query = (
        jnp.einsum("hij,jd->ihd", grad_scores, all_keys, preferred_element_type=jnp.float32)
        * score_scale
    )
    grad_query_raw = (
        rope_turn(grad_query, positions, -1.0)
        .astype(jnp.bfloat16)
        .reshape(row_count, qheads_local * HEAD_DIM)
    )
    grad_query_w = dot_across(normed, grad_query_raw)
    grad_key = (
        jnp.einsum("hij,ihd->jd", grad_scores, queries, preferred_element_type=jnp.float32)
        * score_scale
    )
    grad_value = jnp.einsum(
        "hij,ihd->jd", probs_low, grad_attended, preferred_element_type=jnp.float32
    )
    grad_kv_own = lax.psum_scatter(
        jnp.concatenate([grad_key, grad_value], -1).astype(jnp.bfloat16),
        SEQ,
        scatter_dimension=0,
        tiled=True,
    ).astype(jnp.float32)
    grad_key_raw = rope_turn(grad_kv_own[:, None, :HEAD_DIM], positions, -1.0)[:, 0, :]
    kv_slots = place_slice(
        (row_count, 2 * KVHEADS * HEAD_DIM), grad_key_raw, kv_index * HEAD_DIM, 1
    )
    kv_slots = lax.dynamic_update_slice_in_dim(
        kv_slots, grad_kv_own[:, HEAD_DIM:], (KVHEADS + kv_index) * HEAD_DIM, 1
    )
    grad_normed_part = (
        dot_back(grad_x_pre, x_weight)
        + dot_back(grad_z, z_weight)
        + dot_back(grad_dt_raw, dt_weight)
        + dot_back(grad_query_raw, query_weight)
    )
    grad_normed_sum, grad_bc_sum, grad_kv_sum = (
        lax.psum(grad_normed_part.astype(jnp.bfloat16), "head").astype(jnp.float32),
        lax.psum(grad_bc_part.astype(jnp.bfloat16), "head").astype(jnp.float32),
        lax.psum(kv_slots.astype(jnp.bfloat16), "head").astype(jnp.float32),
    )
    grad_bc_low = grad_bc_sum.astype(jnp.bfloat16)
    grad_kv_low = grad_kv_sum.astype(jnp.bfloat16)
    grad_normed = (
        grad_normed_sum + dot_back(grad_bc_low, bc_weight) + dot_back(grad_kv_low, kv_weight)
    )
    grad_from_one, grad_gain_one = norm_back(grad_normed)
    grad_tokens = grad_hidden_in + grad_from_one
    grad_x_w = dot_across(normed, grad_x_pre)
    grad_z_w = dot_across(normed, grad_z)
    grad_dt_w = dot_across(normed, grad_dt_raw)
    grad_bc_w = dot_across(normed, grad_bc_low) * lead_head
    grad_kv_w = dot_across(normed, grad_kv_low) * lead_head
    conv_full = place_slice((CONV, SSM_HEADS * SSM_DIM), grad_x_conv, head_index * inner_local, 1)
    bias_full = place_slice((SSM_HEADS,), grad_bias, head_index * heads_local, 0)
    rate_full = place_slice((SSM_HEADS,), grad_rate, head_index * heads_local, 0)
    skip_full = place_slice((SSM_HEADS,), grad_skip, head_index * heads_local, 0)
    (
        bc_w_sum,
        kv_w_sum,
        bc_conv_sum,
        x_conv_sum,
        bias_sum,
        rate_sum,
        skip_sum,
        gain_one_sum,
        gain_two_sum,
    ) = together(
        (
            grad_bc_w,
            grad_kv_w,
            grad_bc_conv,
            conv_full,
            bias_full,
            rate_full,
            skip_full,
            grad_gain_one * lead_head,
            grad_gain_two * lead_head,
        ),
        SEQ_HEAD,
    )
    (
        x_w_sum,
        z_w_sum,
        dt_w_sum,
        query_w_sum,
        out_w_sum,
        attn_w_sum,
        gate_w_sum,
        up_w_sum,
        down_w_sum,
    ) = (
        *tuple(
            (
                part.astype(jnp.float32)
                for part in in_one_piece(
                    (
                        grad_x_w.astype(jnp.bfloat16),
                        grad_z_w.astype(jnp.bfloat16),
                        grad_dt_w.astype(jnp.bfloat16),
                        grad_query_w.astype(jnp.bfloat16),
                    ),
                    SEQ,
                    0,
                    1,
                )
            )
        ),
        *tuple(
            (
                part.astype(jnp.float32)
                for part in in_one_piece(
                    (grad_out_w.astype(jnp.bfloat16), grad_attn_w.astype(jnp.bfloat16)), SEQ, 1, 0
                )
            )
        ),
        *tuple(
            (
                part.astype(jnp.float32)
                for part in in_one_piece(
                    (grad_gate_w.astype(jnp.bfloat16), grad_up_w.astype(jnp.bfloat16)), SEQ, 0, 1
                )
            )
        ),
        lax.psum_scatter(
            grad_down_w.astype(jnp.bfloat16), SEQ, scatter_dimension=1, tiled=True
        ).astype(jnp.float32),
    )
    return (
        output,
        grad_tokens,
        gain_one_sum,
        x_w_sum,
        z_w_sum,
        bc_w_sum,
        dt_w_sum,
        x_conv_sum,
        bc_conv_sum,
        bias_sum,
        rate_sum,
        skip_sum,
        out_w_sum,
        query_w_sum,
        kv_w_sum,
        attn_w_sum,
        gain_two_sum,
        gate_w_sum,
        up_w_sum,
        down_w_sum,
    )


def solution(mesh):
    split = Mesh(
        mesh.devices.reshape(2, 4, 4, mesh.shape["head"]), ("seq_0", "seq_1", "seq_2", "head")
    )
    return jax.shard_map(
        on_device,
        mesh=split,
        in_specs=(
            P(SEQ, None),
            P(SEQ),
            P(SEQ, None),
            P(),
            P(None, "head"),
            P(None, "head"),
            P(),
            P(None, "head"),
            P(None, "head"),
            P(),
            P("head"),
            P("head"),
            P("head"),
            P("head", None),
            P(None, "head"),
            P(),
            P("head", None),
            P(),
            P(None, "head"),
            P(None, "head"),
            P("head", None),
        ),
        out_specs=(
            P(SEQ, None),
            P(SEQ, None),
            P(),
            P(SEQ, "head"),
            P(SEQ, "head"),
            P(),
            P(SEQ, "head"),
            P(),
            P(),
            P(),
            P(),
            P(),
            P("head", SEQ),
            P(SEQ, "head"),
            P(),
            P("head", SEQ),
            P(),
            P(SEQ, "head"),
            P(SEQ, "head"),
            P("head", SEQ),
        ),
        check_vma=False,
    )
```

profile of v0, /device:TPU:0, one launch (start us, length us, event | category | flops | bytes accessed | tf_op | source)
XLA Modules:
  0.0 1710.3 jit_solution(16617190447288188408)
XLA Ops:
  8.2 3.8 collective-permute-start
  16.9 3.6 collective-permute-start.2
  21.6 3.2 collective-permute-start.1
  40.7 9.8 all-gather.2
  50.5 10.0 all-gather.3
  61.1 7.8 all-gather.23.cloned.1.call-done
  90.7 4.3 all-gather.4
  100.5 11.6 all_gather.61
  114.7 5.0 fusion.58
  122.0 4.5 multiply_convert_fusion.5
  126.5 136.7 %all-gather.17.cloned.1.call-done = bf16[8192,257]{1,0:T(8,128)(2,1)} async-done(((bf16[256,257]{1,0:T(8,128)(2,1)}), bf16[8192,257]{1,0:T(8,128)(2,1)}) %all-gather.17.cloned.1.call-update) | async-done | bytes 4210704 | tf_op jit(solution)/shard_map/all_gather | solution.py:63
  266.0 4.5 fusion.7
  270.5 9.0 bitcast_select_fusion
  279.5 19.1 %fusion.328 = (f32[2,256]{1,0:T(2,128)S(1)}, f32[2,256,8192]{1,2,0:T(8,128)}) fusion(f32[2,256,8192]{1,2,0:T(8,128)} %bitcast_select_fusion), kind=kOutput, calls=%fused_computation.547 | output fusion | flops 8396799 | bytes 33556480 | tf_op jit(solution)/shard_map/sub | solution.py:293
  298.6 7.8 fusion.63
  310.0 59.6 %all-reduce.24.cloned.1.call-done = f32[256,2048]{1,0:T(8,128)} async-done(((f32[256,2048]{1,0:T(8,128)}), f32[256,2048]{1,0:T(8,128)}) %all-reduce.24.cloned.1.call-update) | async-done | bytes 2097168 | tf_op jit(solution)/shard_map/psum | solution.py:299
  387.9 40.7 %all-reduce.26.cloned.1.call-done = bf16[256,2048]{1,0:T(8,128)(2,1)} async-done(((bf16[256,2048]{1,0:T(8,128)(2,1)}), bf16[256,2048]{1,0:T(8,128)(2,1)}) %all-reduce.26.cloned.1.call-update) | async-done | bytes 1048592 | tf_op jit(solution)/shard_map/psum | solution.py:320
  428.6 3.3 fusion.30
  434.1 3.3 multiply_reduce_fusion.1
  441.1 9.7 all-gather.5
  450.8 9.8 all-gather.6
  462.9 11.8 fusion.1
  474.7 5.8 all-gather.25.cloned.1.call-done
  480.6 3.1 bitcast_add_fusion.6
  483.7 15.7 fusion.3
  499.5 6.8 fusion.5
  506.3 3.7 fusion.6
  510.0 4.2 pad_maximum_fusion.1
  514.9 4.2 all-gather.7
  520.9 4.7 convolution_convert_fusion.8
  530.1 5.1 fusion.36
  535.4 2.9 reduce-window.24
  540.9 7.5 fusion.62
  549.4 4.3 convolution_bitcast_fusion.2
  554.8 3.6 fusion.52
  558.4 3.1 multiply_add_fusion.1
  562.0 3.2 fusion.334
  567.6 127.5 %reduce-scatter.12.cloned.1.call-done = bf16[256,256]{1,0:T(8,128)(2,1)} async-done(((bf16[8192,256]{1,0:T(8,128)(2,1)}), bf16[256,256]{1,0:T(8,128)(2,1)}) %reduce-scatter.12.cloned.1.call-update) | async-done | bytes 131088 | tf_op jit(solution)/shard_map/reduce_scatter | solution.py:382
  696.8 26.5 %all-gather.21.cloned.1.call-done = f32[2,12,64,256]{3,2,1,0:T(8,128)} async-done(((f32[1,12,64,256]{3,2,1,0:T(8,128)}), f32[2,12,64,256]{3,2,1,0:T(8,128)}) %all-gather.21.cloned.1.call-update) | async-done | bytes 1572880 | tf_op jit(solution)/shard_map/all_gather | solution.py:73
  723.4 5.2 convolution_bitcast_fusion.3
  754.6 3.2 collective-permute-done.3
  758.8 5.9 fusion.22
  765.9 3.4 convolution_convert_fusion
  775.6 6.4 copy.253
  783.4 3.3 convolution_convert_fusion.1
  786.7 3.3 convolution_convert_fusion.2
  790.0 8.6 pad_maximum_fusion
  798.6 12.3 copy.255
  814.9 23.4 %all-reduce.30.cloned.1.call-done = (bf16[256,2048]{1,0:T(8,128)(2,1)}, bf16[256,512]{1,0:T(8,128)(2,1)}, bf16[256,2048]{1,0:T(8,128)(2,1)}, bf16[256,512]{1,0:T(8,128)(2,1)}) async-done(((bf16[256,2048]{1,0:T(8,128)(2,1)}, bf16[256,512]{1,0:T(8,128)(2,1)}, bf16[256,2048]{1,0:T(8,128)(2,1)}, bf16[256,512]{1,0:T(8,128)(2,1)}), (bf16[256,2048]{1,0:T(8,128)(2,1)}, bf16[256,512]{1,0:T(8,128)(2,1)}, ...) | async-done | bytes 2621456 | tf_op jit(solution)/shard_map/psum | solution.py:307
  840.2 3.1 copy.271
  844.2 3.1 copy.270
  851.2 72.6 %concatenate.60 = f32[2115728]{0:T(1024)} concatenate(f32[1048576]{0:T(1024)} %bitcast.584, f32[1048576]{0:T(1024)} %bitcast.583, f32[2048]{0:T(1024)} %bitcast.627, f32[12288]{0:T(1024)} %bitcast.616, f32[48]{0:T(128)} %copy-done.212, f32[48]{0:T(128)} %copy-done.210, f32[48]{0:T(128)} %copy-done.211, f32[2048]{0:T(1024)S(1)} %get-tuple-element.261, f32[2048]{0:T(1024)S(1)} %get-tuple-element.260), dimensions={0} | concatenate | bytes 16925824 | tf_op jit(solution)/shard_map/concatenate | solution.py:84
  928.0 80.8 %reduce-scatter.14.cloned.1.call-done = bf16[1024,64]{0,1:T(8,128)(2,1)} async-done(((bf16[1024,2048]{0,1:T(8,128)(2,1)}), bf16[1024,64]{0,1:T(8,128)(2,1)}) %reduce-scatter.14.cloned.1.call-update) | async-done | bytes 131088 | tf_op jit(solution)/shard_map/reduce_scatter | solution.py:489
  1010.5 165.4 %reduce-scatter.18.cloned.1.call-done = bf16[64,1024]{1,0:T(8,128)(2,1)} async-done(((bf16[2048,1024]{1,0:T(8,128)(2,1)}), bf16[64,1024]{1,0:T(8,128)(2,1)}) %reduce-scatter.18.cloned.1.call-update) | async-done | bytes 131088
  1179.8 2.8 convolution_convert_fusion.5
  1182.6 33.6 %concatenate.61 = bf16[2048,1804]{0,1:T(8,128)(2,1)} concatenate(bf16[2048,768]{0,1:T(8,128)(2,1)} %convolution_convert_fusion.5, bf16[2048,768]{0,1:T(8,128)(2,1)} %convolution_convert_fusion.4, bf16[2048,12]{0,1:T(8,128)(2,1)S(1)} %convolution_convert_fusion.9, bf16[2048,256]{0,1:T(8,128)(2,1)S(1)} %convolution_convert_fusion.6), dimensions={1} | concatenate | bytes 14778368 | tf_op jit(solution)/shard_map/concatenate | solution.py:97
  1216.2 10.2 copy.251
  1228.1 5.3 fusion.32
  1233.4 120.5 %reduce-scatter.20.cloned.1.call-done = bf16[64,2048]{1,0:T(8,128)(2,1)} async-done(((bf16[2048,2048]{1,0:T(8,128)(2,1)}), bf16[64,2048]{1,0:T(8,128)(2,1)}) %reduce-scatter.20.cloned.1.call-update) | async-done | bytes 262160
  1356.9 160.5 %all-reduce.28.cloned.1.call-done = f32[2115728]{0:T(1024)} async-done(((f32[2115728]{0:T(1024)}), f32[2115728]{0:T(1024)}) %all-reduce.28.cloned.1.call-update) | async-done | bytes 8462928 | tf_op jit(solution)/shard_map/psum | solution.py:85
  1519.5 7.4 fusion.322
  1526.9 4.9 reshape.807
  1532.5 5.1 reshape.804
  1539.0 158.2 %reduce-scatter.16.cloned.1.call-done = bf16[64,1804]{1,0:T(8,128)(2,1)} async-done(((bf16[2048,1804]{1,0:T(8,128)(2,1)}), bf16[64,1804]{1,0:T(8,128)(2,1)}) %reduce-scatter.16.cloned.1.call-update) | async-done | bytes 230928
  (708 shorter events, 172.0 us)
Async XLA Ops:
  7.2 299.8 %copy-start = (bf16[768,2048]{1,0:T(8,128)(2,1)S(1)}, bf16[768,2048]{1,0:T(8,128)(2,1)}, u32[]{:S(2)}) copy-start(bf16[768,2048]{1,0:T(8,128)(2,1)} %param.38) | copy-start | bytes 9437188
  7.2 13.3 copy-start.79
  7.2 61.7 %all-gather.23.cloned.1.call-start = ((), (), s32[]{:S(2)}) async-start(), calls=%async_computation.14 | async-start | bytes 1966080 | tf_op jit(solution)/shard_map/all_gather | solution.py:43
  7.3 13.3 copy-start.2
  8.2 18.9 %collective-permute-start = (bf16[3]{0:T(256)(128)(2,1)S(1)}, bf16[3]{0:T(256)(128)(2,1)S(1)}, u32[]{:S(2)}, u32[]{:S(2)}) collective-permute-start(bf16[3]{0:T(256)(128)(2,1)S(1)} %slice.340), channel_id=1, source_target_pairs={{0,4},{4,8},{8,12},{12,16},{16,20},{20,24},{24,28},{28,32},{32,36}... | collective-permute-start | bytes 26 | tf_op jit(solution)/shard_map/ppermute | solution.py:28
  16.9 14.9 collective-permute-start.2
  21.6 11.5 collective-permute-start.1
  40.4 57.9 %all-gather.15.cloned.1.call-start = ((), (), s32[]{:S(2)}) async-start(), calls=%async_computation.5 | async-start | bytes 1966080 | tf_op jit(solution)/shard_map/all_gather | solution.py:43
  71.5 191.7 %all-gather.17.cloned.1.call-start = ((), (), s32[]{:S(2)}) async-start(), calls=%async_computation.6 | async-start | bytes 6488064 | tf_op jit(solution)/shard_map/all_gather | solution.py:63
  77.7 291.9 %all-reduce.24.cloned.1.call-start = ((), (), s32[]{:S(2)}) async-start(), calls=%async_computation.7 | async-start | bytes 4194304 | tf_op jit(solution)/shard_map/psum | solution.py:299
  98.3 13.8 copy-start.35
  98.3 13.8 copy-start.36
  98.3 13.8 copy-start.164
  98.3 13.8 copy-start.166
  98.3 13.8 copy-start.172
  98.4 13.8 copy-start.175
  98.4 13.8 copy-start.178
  98.4 13.8 copy-start.180
  98.4 13.8 copy-start.182
  98.4 13.8 copy-start.184
  98.4 13.8 copy-start.201
  98.4 13.8 copy-start.203
  98.4 13.8 copy-start.218
  98.4 13.8 copy-start.220
  309.8 118.8 %all-reduce.26.cloned.1.call-start = ((), (), s32[]{:S(2)}) async-start(), calls=%async_computation.8 | async-start | bytes 2097152 | tf_op jit(solution)/shard_map/psum | solution.py:320
  383.8 96.7 %all-gather.25.cloned.1.call-start = ((), (), s32[]{:S(2)}) async-start(), calls=%async_computation.15 | async-start | bytes 3932160 | tf_op jit(solution)/shard_map/all_gather | solution.py:73
  437.4 23.8 %copy-start.14 = (bf16[256,2048]{1,0:T(8,128)(2,1)S(1)}, bf16[256,2048]{1,0:T(8,128)(2,1)}, u32[]{:S(2)}) copy-start(bf16[256,2048]{1,0:T(8,128)(2,1)} %copy-done.13) | copy-start | bytes 3145732
  437.4 25.5 %copy-start.155 = (f32[2,256]{1,0:T(2,128)S(1)}, f32[2,256]{1,0:T(2,128)}, u32[]{:S(2)}) copy-start(f32[2,256]{1,0:T(2,128)} %copy-done.154) | copy-start | bytes 6148
  441.1 117.3 %all-gather.19.cloned.1.call-start = ((), (), s32[]{:S(2)}) async-start(), calls=%async_computation.9 | async-start | bytes 3932160 | tf_op jit(solution)/shard_map/all_gather | solution.py:73
  450.8 29.7 %copy-start.186 = (f32[12]{0:T(128)}, f32[12]{0:T(128)S(1)}, u32[]{:S(2)}) copy-start(f32[12]{0:T(128)S(1)} %get-tuple-element.230) | copy-start | bytes 148
  450.8 29.7 %copy-start.188 = (f32[12]{0:T(128)}, f32[12]{0:T(128)S(1)}, u32[]{:S(2)}) copy-start(f32[12]{0:T(128)S(1)} %get-tuple-element.231) | copy-start | bytes 148
  450.8 29.7 %copy-start.190 = (f32[12]{0:T(128)}, f32[12]{0:T(128)S(1)}, u32[]{:S(2)}) copy-start(f32[12]{0:T(128)S(1)} %get-tuple-element.232) | copy-start | bytes 148
  461.2 19.4 %copy-start.168 = (f32[12]{0:T(128)}, f32[12]{0:T(128)S(1)}, u32[]{:S(2)}) copy-start(f32[12]{0:T(128)S(1)} %get-tuple-element.227) | copy-start | bytes 148
  483.7 211.4 %reduce-scatter.12.cloned.1.call-start = ((), (), s32[]{:S(2)}) async-start(), calls=%async_computation.11 | async-start | bytes 4325376 | tf_op jit(solution)/shard_map/reduce_scatter | solution.py:382
  483.7 15.8 copy-start.55
  483.7 22.6 %slice-start = ((s8[16777216]{0:T(1024)(128)(4,1)}), s8[4194304]{0:T(1024)(128)(4,1)S(1)}, s32[]{:S(2)}) async-start(s8[16777216]{0:T(1024)(128)(4,1)} %bitcast.581), calls=%async_computation.20 | async-start | bytes 8388608
  483.7 22.6 %slice-start.1 = ((s8[16777216]{0:T(1024)(128)(4,1)}), s8[4194304]{0:T(1024)(128)(4,1)S(1)}, s32[]{:S(2)}) async-start(s8[16777216]{0:T(1024)(128)(4,1)} %bitcast.581), calls=%async_computation.21 | async-start | bytes 8388608
  483.7 22.6 %slice-start.2 = ((s8[16777216]{0:T(1024)(128)(4,1)}), s8[4194304]{0:T(1024)(128)(4,1)S(1)}, s32[]{:S(2)}) async-start(s8[16777216]{0:T(1024)(128)(4,1)} %bitcast.581), calls=%async_computation.22 | async-start | bytes 8388608
  514.3 209.0 %all-gather.21.cloned.1.call-start = ((), (), s32[]{:S(2)}) async-start(), calls=%async_computation.10 | async-start | bytes 2359296 | tf_op jit(solution)/shard_map/all_gather | solution.py:73
  535.3 18.5 %copy-start.59 = (f32[256,256]{1,0:T(8,128)}, f32[256,256]{1,0:T(8,128)S(1)}, u32[]{:S(2)}) copy-start(f32[256,256]{1,0:T(8,128)S(1)} %get-tuple-element.126) | copy-start | bytes 786436
  561.5 276.8 %all-reduce.30.cloned.1.call-start = ((), (), s32[]{:S(2)}) async-start(), calls=%async_computation.19 | async-start | bytes 5242880 | tf_op jit(solution)/shard_map/psum | solution.py:307
  565.2 130.8 %copy-start.143 = (f32[256]{0:T(256)S(1)}, f32[256]{0:T(256)}, u32[]{:S(2)}) copy-start(f32[256]{0:T(256)} %copy-done.142) | copy-start | bytes 3076
  565.2 130.8 %copy-start.162 = (f32[64]{0:T(128)S(1)}, f32[64]{0:T(128)}, u32[]{:S(2)}) copy-start(f32[64]{0:T(128)} %copy-done.161) | copy-start | bytes 772
  565.2 158.1 %copy-start.169 = (f32[12]{0:T(128)S(1)}, f32[12]{0:T(128)}, u32[]{:S(2)}) copy-start(f32[12]{0:T(128)} %copy-done.168) | copy-start | bytes 148
  565.2 158.1 %copy-start.189 = (f32[12]{0:T(128)S(1)}, f32[12]{0:T(128)}, u32[]{:S(2)}) copy-start(f32[12]{0:T(128)} %copy-done.188) | copy-start | bytes 148
  565.2 158.1 %copy-start.191 = (f32[12]{0:T(128)S(1)}, f32[12]{0:T(128)}, u32[]{:S(2)}) copy-start(f32[12]{0:T(128)} %copy-done.190) | copy-start | bytes 148
  565.2 158.1 %copy-start.205 = (f32[12]{0:T(128)S(1)}, f32[12]{0:T(128)}, u32[]{:S(2)}) copy-start(f32[12]{0:T(128)} %get-tuple-element.163) | copy-start | bytes 148
  565.2 158.1 %copy-start.206 = (f32[12]{0:T(128)S(1)}, f32[12]{0:T(128)}, u32[]{:S(2)}) copy-start(f32[12]{0:T(128)} %get-tuple-element.164) | copy-start | bytes 148
  565.2 158.1 %copy-start.207 = (f32[12]{0:T(128)S(1)}, f32[12]{0:T(128)}, u32[]{:S(2)}) copy-start(f32[12]{0:T(128)} %get-tuple-element.244) | copy-start | bytes 148
  565.2 158.1 %copy-start.208 = (f32[12]{0:T(128)S(1)}, f32[12]{0:T(128)}, u32[]{:S(2)}) copy-start(f32[12]{0:T(128)} %get-tuple-element.245) | copy-start | bytes 148
  696.8 26.5 %copy-start.62 = (bf16[256,512]{1,0:T(8,128)(2,1)}, bf16[256,512]{1,0:T(8,128)(2,1)S(1)}, u32[]{:S(2)}) copy-start(bf16[256,512]{1,0:T(8,128)(2,1)S(1)} %slice_dynamic-update-slice_fusion) | copy-start | bytes 786436
  745.5 7.8 collective-permute-start.4
  751.6 6.2 collective-permute-start.3
  764.7 244.2 %reduce-scatter.14.cloned.1.call-start = ((), (), s32[]{:S(2)}) async-start(), calls=%async_computation.13 | async-start | bytes 4325376 | tf_op jit(solution)/shard_map/reduce_scatter | solution.py:489
  769.3 406.6 %reduce-scatter.18.cloned.1.call-start = ((), (), s32[]{:S(2)}) async-start(), calls=%async_computation.17 | async-start | bytes 4325376
  782.0 571.8 %reduce-scatter.20.cloned.1.call-start = ((), (), s32[]{:S(2)}) async-start(), calls=%async_computation.18 | async-start | bytes 8650752
  811.1 27.3 %copy-start.3 = (bf16[256,2048]{1,0:T(8,128)(2,1)S(1)}, bf16[256,2048]{1,0:T(8,128)(2,1)}, u32[]{:S(2)}) copy-start(bf16[256,2048]{1,0:T(8,128)(2,1)} %param.25) | copy-start | bytes 3145732
  811.1 27.3 %copy-start.80 = (f32[2048]{0:T(1024)S(1)}, f32[2048]{0:T(1024)}, u32[]{:S(2)}) copy-start(f32[2048]{0:T(1024)} %param.28) | copy-start | bytes 24580
  811.1 27.2 %copy-start.105 = (f32[256]{0:T(256)S(1)}, f32[256]{0:T(256)}, u32[]{:S(2)}) copy-start(f32[256]{0:T(256)} %copy-done.104) | copy-start | bytes 3076
  811.1 706.3 %all-reduce.28.cloned.1.call-start = ((), (), s32[]{:S(2)}) async-start(), calls=%async_computation.12 | async-start | bytes 16932864 | tf_op jit(solution)/shard_map/psum | solution.py:85
  814.9 25.2 %copy-start.210 = (f32[48]{0:T(128)}, f32[48]{0:T(128)S(1)}, u32[]{:S(2)}) copy-start(f32[48]{0:T(128)S(1)} %add_dynamic-update-slice_fusion.1) | copy-start | bytes 580
  923.8 773.4 %reduce-scatter.16.cloned.1.call-start = ((), (), s32[]{:S(2)}) async-start(), calls=%async_computation.16 | async-start | bytes 8110080
  925.2 254.1 %copy-start.115 = (bf16[256,12]{0,1:T(8,128)(2,1)S(1)}, bf16[256,12]{0,1:T(8,128)(2,1)}, u32[]{:S(2)}) copy-start(bf16[256,12]{0,1:T(8,128)(2,1)} %copy-done.114) | copy-start | bytes 18436
  1532.5 170.7 %copy-start.1 = (bf16[768,2048]{1,0:T(8,128)(2,1)S(1)}, bf16[768,2048]{1,0:T(8,128)(2,1)}, u32[]{:S(2)}) copy-start(bf16[768,2048]{1,0:T(8,128)(2,1)} %param.38) | copy-start | bytes 9437188
  (188 other events, 840.2 us)
Sparse Core Ops, SparseCore 0:
  40.5 28.3 all-gather.22
  71.7 26.6 all-gather.14
  100.5 162.6 all-gather.16
  309.9 59.6 all-reduce.23
  384.0 44.5 all-reduce.25
  441.2 39.3 all-gather.24
  483.8 39.6 all-gather.18
  526.4 168.5 reduce-scatter.11
  696.7 26.4 all-gather.20
  764.8 73.4 all-reduce.29
  840.7 168.1 reduce-scatter.13
  1011.1 164.7 reduce-scatter.17
  1178.3 175.5 reduce-scatter.19
  1358.8 158.5 all-reduce.27
  1519.8 177.2 reduce-scatter.15
where the time goes:
time: 1730 us; the launch traced here: 1710 us
  waiting for transfers between devices  1120 us (65%)
  local copies, waits for them, and re-layouts  220 us (13%)
  matrix products  153 us (9%)
  other arithmetic  127 us (7%)
  blocking collectives  59.4 us (3%)
  between operations  18.9 us (1%)
    unnamed x18, waiting for transfers between devices  444 us
    psum x1, waiting for transfers between devices, together(): subtotal = lax.psum(line, axis)  161 us
    all_gather x1, waiting for transfers between devices, side_by_side(): whole = lax.all_gather(both, axis, axis=dim, tiled=True)  137 us
    reduce_scatter x1, waiting for transfers between devices, on_device(): lax.psum_scatter(jnp.concatenate([grad_key, grad_value], -1).astype(jnp.b...  127 us
    reduce_scatter x1, waiting for transfers between devices, on_device(): lax.psum_scatter(grad_down_w.astype(jnp.bfloat16), SEQ, scatter_dimension...  80.8 us
    concatenate x1, local copies, waits for them, and re-layouts, together(): jnp.concatenate([a.reshape(-1) for a in arrays])  72.6 us
    unnamed x492, local copies, waits for them, and re-layouts  63.1 us
    psum x1, waiting for transfers between devices, on_device(): mixer_sum = lax.psum(mixer_part, 'head')  59.6 us
  transfers between devices with their start and end apart: 20, of which 14 were waited for; matrix products, arithmetic and copies ran while one was open for 22% of the time, Pallas kernels for 0%

commit v1 on v0

v1 whole, which is shorter than its diff:
```python
import functools

import jax
import jax.numpy as jnp
from jax import lax
from jax.experimental import pallas as pl
from jax.experimental.pallas import tpu as pltpu
from jax.sharding import Mesh
from jax.sharding import PartitionSpec as P

SSM_DIM = 64
STATE = 256
CONV = 4
KVHEADS = 2
HEAD_DIM = 128
NZ, NX, NY = 2, 4, 4
BLOCKS = NZ * NX * NY
CHIPS = 2 * BLOCKS
ROWS = 256
MODEL = 2048
SEQ = ("zl", "x", "y")
EPSILON = 1e-05
ROPE_BASE = 100000000000.0
HIGHEST = lax.Precision.HIGHEST
MESH = pl.DeviceIdType.MESH
BF16, F32 = jnp.bfloat16, jnp.float32
MASKED = -1e30
LOG2E = 1.4426950408889634
VMEM_LIMIT = 56 * 2**20


def block_index():
    return (lax.axis_index("zl") * NX + lax.axis_index("x")) * NY + lax.axis_index("y")


def block_at(s):
    return {"zl": s // (NX * NY), "x": (s // NY) % NX, "y": s % NY}


def signal(sem, where):
    pl.semaphore_signal(sem, inc=1, device_id=where, device_id_type=MESH)


def remote(src, dst, send, recv, where):
    return pltpu.make_async_remote_copy(src, dst, send, recv, device_id=where, device_id_type=MESH)


def over(start, stop, body):
    def step(i, carry):
        body(i)
        return carry

    lax.fori_loop(start, stop, step, 0)


def dot(a, b, left=1, right=0):
    return lax.dot_general(
        a, b, (((left,), (right,)), ((), ())), preferred_element_type=F32
    )


def vmem(n):
    return [pl.BlockSpec(memory_space=pltpu.VMEM)] * n


def params(collective_id):
    return pltpu.CompilerParams(
        collective_id=collective_id, has_side_effects=True, vmem_limit_bytes=VMEM_LIMIT
    )


def key_segments(block):
    turned = jnp.transpose(block.astype(F32))
    return jnp.concatenate([turned[:, 0:1], turned[:, 1:2]], 0)


def attention_forward_kernel(
    q_ref, own_ref, qseg_ref, edge_ref, out_ref, lse_ref, kv_ref, edge_out,
    m_ref, l_ref, acc_ref, send_sem, recv_sem, sib_send, sib_recv, edge_sem,
):
    me, c = block_index(), lax.axis_index("c")
    sibling = {"c": 1 - c}
    barrier = pltpu.get_barrier_semaphore()
    over(1, BLOCKS, lambda o: signal(barrier, block_at((me + o) % BLOCKS)))
    signal(barrier, sibling)
    pl.semaphore_wait(barrier, BLOCKS)

    kv_ref[c, 0] = own_ref[...]
    to_sibling = lambda t, src: remote(
        src, kv_ref.at[c, t], sib_send.at[t], sib_recv.at[t], sibling
    )
    from_sibling = lambda t: remote(
        kv_ref.at[1 - c, t], kv_ref.at[1 - c, t], sib_send.at[t], sib_recv.at[t], sibling
    )
    to_block = lambda t: remote(
        own_ref, kv_ref.at[c, t], send_sem.at[t], recv_sem.at[t], block_at((me + t) % BLOCKS)
    )
    edge_copy = remote(
        edge_ref, edge_out, edge_sem.at[0], edge_sem.at[1], block_at((me + 1) % BLOCKS)
    )

    @pl.when(me < BLOCKS - 1)
    def _():
        edge_copy.start()

    to_sibling(0, own_ref).start()
    over(1, BLOCKS - me, lambda t: to_block(t).start())

    scale = LOG2E * HEAD_DIM**-0.5
    queries = q_ref[...]
    qseg = qseg_ref[0:1, :]

    def scores_of(t):
        s = dot(kv_ref[0, t, :ROWS], queries, 1, 1) * scale
        return jnp.where(key_segments(kv_ref[0, t, ROWS:]) == qseg, s, MASKED)

    from_sibling(0).wait_recv()
    row = lax.broadcasted_iota(jnp.int32, (ROWS, 2 * ROWS), 0)
    col = lax.broadcasted_iota(jnp.int32, (ROWS, 2 * ROWS), 1) % ROWS
    s = jnp.where(row <= col, scores_of(0), MASKED)
    m = jnp.max(s, 0, keepdims=True)
    p = jnp.exp2(s - m)
    m_ref[...] = m
    l_ref[...] = jnp.sum(p, 0, keepdims=True)
    acc_ref[...] = dot(kv_ref[1, 0, :ROWS], p.astype(BF16), 0, 0)

    def forward(t):
        to_block(t).wait_recv()
        to_sibling(t, kv_ref.at[c, t]).start()

    @pl.when(me >= 1)
    def _():
        forward(1)

    def step(t):
        @pl.when(t + 1 <= me)
        def _():
            forward(t + 1)

        from_sibling(t).wait_recv()
        s = scores_of(t)
        m_old = m_ref[...]
        m = jnp.maximum(m_old, jnp.max(s, 0, keepdims=True))
        p = jnp.exp2(s - m)
        alpha = jnp.exp2(m_old - m)
        m_ref[...] = m
        l_ref[...] = l_ref[...] * alpha + jnp.sum(p, 0, keepdims=True)
        acc_ref[...] = acc_ref[...] * alpha + dot(kv_ref[1, t, :ROWS], p.astype(BF16), 0, 0)

    over(1, me + 1, step)
    out_ref[...] = jnp.transpose(acc_ref[...] / l_ref[...])
    lse_ref[...] = jnp.broadcast_to(m_ref[...] + jnp.log2(l_ref[...]), lse_ref.shape)

    over(0, me + 1, lambda t: to_sibling(t, own_ref).wait_send())
    over(1, BLOCKS - me, lambda t: to_block(t).wait_send())

    @pl.when(me < BLOCKS - 1)
    def _():
        edge_copy.wait_send()

    @pl.when(me > 0)
    def _():
        edge_copy.wait_recv()

    @pl.when(me == 0)
    def _():
        edge_out[...] = jnp.zeros_like(edge_out)


def attention_forward(queries, own, qseg, edge):
    wide = 2 * ROWS
    return pl.pallas_call(
        attention_forward_kernel,
        name="attention_forward",
        out_shape=(
            jax.ShapeDtypeStruct((wide, HEAD_DIM), F32),
            jax.ShapeDtypeStruct((8, wide), F32),
            jax.ShapeDtypeStruct((2, BLOCKS, *own.shape), BF16),
            jax.ShapeDtypeStruct(edge.shape, edge.dtype),
        ),
        in_specs=vmem(4),
        out_specs=tuple(vmem(4)),
        scratch_shapes=[
            pltpu.VMEM((1, wide), F32),
            pltpu.VMEM((1, wide), F32),
            pltpu.VMEM((HEAD_DIM, wide), F32),
            pltpu.SemaphoreType.DMA((BLOCKS,)),
            pltpu.SemaphoreType.DMA((BLOCKS,)),
            pltpu.SemaphoreType.DMA((BLOCKS,)),
            pltpu.SemaphoreType.DMA((BLOCKS,)),
            pltpu.SemaphoreType.DMA((2,)),
        ],
        compiler_params=params(1),
    )(queries, own, qseg, edge)


def attention_backward_kernel(
    q_ref, do_ref, lse_ref, delta_ref, qseg_ref, kv_ref, edge_ref, dq_ref, own_ref, edge_out,
    dqt_ref, mine, theirs, sib, summed, got, send_sem, recv_sem, sib_send, sib_recv, edge_sem,
):
    me, c = block_index(), lax.axis_index("c")
    sibling = {"c": 1 - c}
    barrier = pltpu.get_barrier_semaphore()
    over(1, BLOCKS, lambda o: signal(barrier, block_at((me + o) % BLOCKS)))
    signal(barrier, sibling)
    pl.semaphore_wait(barrier, BLOCKS)

    to_sibling = lambda t: remote(
        theirs.at[t], sib.at[t], sib_send.at[t], sib_recv.at[t], sibling
    )
    to_owner = lambda t: remote(
        summed.at[t], got.at[t], send_sem.at[t], recv_sem.at[t],
        block_at((me + BLOCKS - t) % BLOCKS),
    )
    edge_copy = remote(
        edge_ref, edge_out, edge_sem.at[0], edge_sem.at[1],
        block_at((me + BLOCKS - 1) % BLOCKS),
    )

    @pl.when(me > 0)
    def _():
        edge_copy.start()

    scale = LOG2E * HEAD_DIM**-0.5
    queries, grads = q_ref[...], do_ref[...]
    lse, delta, qseg = lse_ref[0:1, :], delta_ref[0:1, :], qseg_ref[0:1, :]

    def block(t, own):
        keys = kv_ref[0, t, :ROWS]
        s = dot(keys, queries, 1, 1) * scale
        s = jnp.where(key_segments(kv_ref[0, t, ROWS:]) == qseg, s, MASKED)
        if own:
            row = lax.broadcasted_iota(jnp.int32, (ROWS, 2 * ROWS), 0)
            col = lax.broadcasted_iota(jnp.int32, (ROWS, 2 * ROWS), 1) % ROWS
            s = jnp.where(row <= col, s, MASKED)
        p = jnp.exp2(s - lse)
        ds = (p * (dot(kv_ref[1, t, :ROWS], grads, 1, 1) - delta)).astype(BF16)
        dk = dot(ds, queries)
        dv = dot(p.astype(BF16), grads)
        change = dot(keys, ds, 0, 0)
        dqt_ref[...] = change if own else dqt_ref[...] + change
        mine[t] = jnp.where(c == 0, dk, dv).astype(BF16)
        theirs[t] = jnp.where(c == 0, dv, dk).astype(BF16)
        to_sibling(t).start()

    def pair(t):
        to_sibling(t).wait_recv()
        return mine[t].astype(F32) + sib[t].astype(F32)

    block(0, True)

    def step(t):
        block(t, False)

        @pl.when(t >= 2)
        def _():
            summed[t - 1] = pair(t - 1).astype(BF16)
            to_owner(t - 1).start()

    over(1, me + 1, step)

    @pl.when(me >= 1)
    def _():
        summed[me] = pair(me).astype(BF16)
        to_owner(me).start()

    own_ref[...] = pair(0)
    dq_ref[...] = jnp.transpose(dqt_ref[...])

    def collect(t):
        to_owner(t).wait_recv()
        own_ref[...] += got[t].astype(F32)

    over(1, BLOCKS - me, collect)
    over(0, me + 1, lambda t: to_sibling(t).wait_send())
    over(1, me + 1, lambda t: to_owner(t).wait_send())

    @pl.when(me > 0)
    def _():
        edge_copy.wait_send()

    @pl.when(me < BLOCKS - 1)
    def _():
        edge_copy.wait_recv()

    @pl.when(me == BLOCKS - 1)
    def _():
        edge_out[...] = jnp.zeros_like(edge_out)


def attention_backward(queries, grads, lse, delta, qseg, kv, edge):
    wide = 2 * ROWS
    piece = (BLOCKS, ROWS, HEAD_DIM)
    return pl.pallas_call(
        attention_backward_kernel,
        name="attention_backward",
        out_shape=(
            jax.ShapeDtypeStruct((wide, HEAD_DIM), F32),
            jax.ShapeDtypeStruct((ROWS, HEAD_DIM), F32),
            jax.ShapeDtypeStruct(edge.shape, edge.dtype),
        ),
        in_specs=vmem(7),
        out_specs=tuple(vmem(3)),
        scratch_shapes=[
            pltpu.VMEM((HEAD_DIM, wide), F32),
            *[pltpu.VMEM(piece, BF16)] * 5,
            *[pltpu.SemaphoreType.DMA((BLOCKS,))] * 4,
            pltpu.SemaphoreType.DMA((2,)),
        ],
        compiler_params=params(2),
    )(queries, grads, lse, delta, qseg, kv, edge)


SCAN_ROWS = 24


def scan_kernel(reverse, part_ref, out_ref, got, back, send_sem, recv_sem):
    me = block_index()
    barrier = pltpu.get_barrier_semaphore()
    over(1, BLOCKS, lambda o: signal(barrier, block_at((me + o) % BLOCKS)))
    pl.semaphore_wait(barrier, BLOCKS - 1)

    def there(o):
        d = (me + o) % BLOCKS
        return remote(
            part_ref.at[d], got.at[me], send_sem.at[0, o], recv_sem.at[0, o], block_at(d)
        )

    def arrived(phase, dst, o):
        s = (me + BLOCKS - o) % BLOCKS
        return remote(
            dst.at[s], dst.at[s], send_sem.at[phase, o], recv_sem.at[phase, o], block_at(s)
        )

    over(1, BLOCKS, lambda o: there(o).start())
    got[me] = part_ref[me]
    over(1, BLOCKS, lambda o: arrived(0, got, o).wait_recv())

    at_lane = lax.broadcasted_iota(jnp.int32, (SCAN_ROWS, 128), 1)
    at_row = lax.broadcasted_iota(jnp.int32, (SCAN_ROWS, 128), 0)

    def scan(i, state):
        k = BLOCKS - 1 - i if reverse else i
        message = got[k].astype(F32)
        back[k] = jnp.concatenate([state, jnp.zeros((8, STATE), F32)], 0).astype(BF16)

        @pl.when(k != me)
        def _():
            o = (k + BLOCKS - me) % BLOCKS
            remote(
                back.at[k], out_ref.at[me], send_sem.at[1, o], recv_sem.at[1, o], block_at(k)
            ).start()

        factors = message[SCAN_ROWS : SCAN_ROWS + 1, :128]
        factors += message[SCAN_ROWS + 1 : SCAN_ROWS + 2, :128]
        factors += message[SCAN_ROWS + 2 : SCAN_ROWS + 3, :128]
        through = jnp.sum(jnp.where(at_lane == at_row, factors, 0.0), 1, keepdims=True)
        return through * state + message[:SCAN_ROWS]

    lax.fori_loop(0, BLOCKS, scan, jnp.zeros((SCAN_ROWS, STATE), F32))
    out_ref[me] = back[me]
    over(1, BLOCKS, lambda o: arrived(1, out_ref, o).wait_recv())

    def sent(o):
        there(o).wait_send()
        d = (me + o) % BLOCKS
        remote(
            back.at[d], out_ref.at[me], send_sem.at[1, o], recv_sem.at[1, o], block_at(d)
        ).wait_send()

    over(1, BLOCKS, sent)


def scan_states(state, through, reverse, collective_id):
    heads = state.shape[0]
    per = heads * SSM_DIM // BLOCKS
    rows = state.reshape(BLOCKS, per, STATE).astype(BF16)
    factor = jnp.repeat(through, SSM_DIM).reshape(BLOCKS, per)
    high = factor.astype(BF16)
    rest = factor - high.astype(F32)
    middle = rest.astype(BF16)
    low = (rest - middle.astype(F32)).astype(BF16)
    extra = jnp.stack([high, middle, low], 1)
    extra = jnp.pad(extra, ((0, 0), (0, 5), (0, STATE - per)))
    message = jnp.concatenate([rows, extra], 1)
    out = pl.pallas_call(
        functools.partial(scan_kernel, reverse),
        name="scan_back" if reverse else "scan_ahead",
        out_shape=jax.ShapeDtypeStruct(message.shape, BF16),
        in_specs=vmem(1),
        out_specs=vmem(1)[0],
        scratch_shapes=[
            pltpu.VMEM(message.shape, BF16),
            pltpu.VMEM(message.shape, BF16),
            pltpu.SemaphoreType.DMA((2, BLOCKS)),
            pltpu.SemaphoreType.DMA((2, BLOCKS)),
        ],
        compiler_params=params(collective_id),
    )(message)
    return out[:, :per].reshape(heads, SSM_DIM, STATE).astype(F32)


HEAD_CHUNKS = 4


def head_sum_kernel(x_ref, out_ref, near, pair, far, near_send, near_recv, far_send, far_recv, last_send, last_recv):
    c, zh = lax.axis_index("c"), lax.axis_index("zh")
    sibling, opposite = {"c": 1 - c}, {"zh": 1 - zh}
    barrier = pltpu.get_barrier_semaphore()
    signal(barrier, sibling)
    signal(barrier, opposite)
    pl.semaphore_wait(barrier, 2)
    half = x_ref.shape[0] // 2
    n = half // HEAD_CHUNKS

    def rows(core, k):
        return pl.ds(pl.multiple_of(core * half + k * n, 16), n)

    def local(k):
        return pl.ds(k * n, n)

    first = lambda k: remote(
        x_ref.at[rows(1 - c, k)], near.at[local(k)], near_send.at[k], near_recv.at[k], sibling
    )
    second = lambda k: remote(
        pair.at[local(k)], far.at[local(k)], far_send.at[k], far_recv.at[k], opposite
    )
    third = lambda k, core: remote(
        out_ref.at[rows(core, k)], out_ref.at[rows(core, k)],
        last_send.at[k], last_recv.at[k], sibling,
    )
    for k in range(HEAD_CHUNKS):
        first(k).start()
    for k in range(HEAD_CHUNKS):
        first(k).wait_recv()
        pair[local(k)] = (x_ref[rows(c, k)].astype(F32) + near[local(k)].astype(F32)).astype(BF16)
        second(k).start()
    for k in range(HEAD_CHUNKS):
        second(k).wait_recv()
        out_ref[rows(c, k)] = (pair[local(k)].astype(F32) + far[local(k)].astype(F32)).astype(BF16)
        third(k, c).start()
    for k in range(HEAD_CHUNKS):
        third(k, 1 - c).wait_recv()
    for k in range(HEAD_CHUNKS):
        first(k).wait_send()
        second(k).wait_send()
        third(k, c).wait_send()


def head_sum(x, collective_id):
    half = (x.shape[0] // 2, x.shape[1])
    return pl.pallas_call(
        head_sum_kernel,
        name=f"head_sum_{collective_id}",
        out_shape=jax.ShapeDtypeStruct(x.shape, BF16),
        in_specs=vmem(1),
        out_specs=vmem(1)[0],
        scratch_shapes=[
            *[pltpu.VMEM(half, BF16)] * 3,
            *[pltpu.SemaphoreType.DMA((HEAD_CHUNKS,))] * 6,
        ],
        compiler_params=params(collective_id),
    )(x)


def head_share_kernel(x_ref, out_ref, got, send_sem, recv_sem):
    me = lax.axis_index("zh") * 2 + lax.axis_index("c")
    at = lambda d: {"zh": d // 2, "c": d % 2}
    barrier = pltpu.get_barrier_semaphore()
    for o in range(1, 4):
        signal(barrier, at((me + o) % 4))
    pl.semaphore_wait(barrier, 3)
    copy = lambda o: remote(
        x_ref.at[(me + o) % 4], got.at[o], send_sem.at[o], recv_sem.at[o], at((me + o) % 4)
    )
    for o in range(1, 4):
        copy(o).start()
    total = x_ref[me].astype(F32)
    for o in range(1, 4):
        copy(o).wait_recv()
        total += got[o].astype(F32)
    out_ref[...] = total
    for o in range(1, 4):
        copy(o).wait_send()


def head_share(x, collective_id):
    return pl.pallas_call(
        head_share_kernel,
        name="head_share",
        out_shape=jax.ShapeDtypeStruct(x.shape[1:], F32),
        in_specs=vmem(1),
        out_specs=vmem(1)[0],
        scratch_shapes=[
            pltpu.VMEM(x.shape, BF16),
            pltpu.SemaphoreType.DMA((4,)),
            pltpu.SemaphoreType.DMA((4,)),
        ],
        compiler_params=params(collective_id),
    )(x)


WIDE = 256
LAG = 3


def weight_kernel(
    first_of, l_ref, r_ref, out_ref, lz, rz, part, gx, half, gy,
    lz_send, lz_recv, rz_send, rz_recv, gx_send, gx_recv, gy_send, gy_recv,
):
    n = r_ref.shape[1] // WIDE
    n_left = l_ref.shape[0]
    own = MODEL // NZ
    zl, x, y = (lax.axis_index(a) for a in SEQ)
    other = {"zl": 1 - zl}
    barrier = pltpu.get_barrier_semaphore()
    signal(barrier, other)
    for o in range(1, 4):
        signal(barrier, {"x": (x + o) % NX})
        signal(barrier, {"y": (y + o) % NY})
    pl.semaphore_wait(barrier, 7)

    def columns(c):
        return pl.ds(pl.multiple_of(c * WIDE, WIDE), WIDE)

    def left(g):
        return remote(
            l_ref.at[g, pl.ds(pl.multiple_of((1 - zl) * own, own), own)], lz.at[g],
            lz_send.at[g], lz_recv.at[g], other,
        )

    def right(c):
        return remote(r_ref.at[:, columns(c)], rz.at[c], rz_send.at[c], rz_recv.at[c], other)

    for g in range(n_left):
        left(g).start()
        over(first_of[g], first_of[g + 1], lambda c: right(c).start())

    def spread(c, phase, o):
        along_x = c % 2 == phase
        x_to = jnp.where(along_x, (x + o) % NX, x)
        y_to = jnp.where(along_x, y, (y + o) % NY)
        return {"x": x_to, "y": y_to}, jnp.where(along_x, x_to, y_to)

    def send_first(c, o):
        where, d = spread(c, 0, o)
        return remote(part.at[c, d], gx.at[c, o - 1], gx_send.at[c], gx_recv.at[c], where)

    def send_second(c, o):
        where, d = spread(c, 1, o)
        return remote(half.at[c, d], gy.at[c, o - 1], gy_send.at[c], gy_recv.at[c], where)

    def whole(got, send, recv, c):
        return remote(got.at[c], got.at[c], send.at[c], recv.at[c], other)

    def product(c):
        for g in range(n_left):
            @pl.when(c == first_of[g])
            def _():
                left(g).wait_recv()
        right(c).wait_recv()
        g = sum((c >= first_of[k]).astype(jnp.int32) for k in range(1, n_left)) if n_left > 1 else 0
        mine, theirs = r_ref[:, columns(c)], rz[c]
        even = c % 2 == 0
        for i in range(NX):
            a = l_ref[g, pl.ds(pl.multiple_of(zl * own + i * 256, 256), 256), :]
            b = lz[g, pl.ds(i * 256, 256), :]
            tile = (dot(a, mine) + dot(b, theirs)).astype(BF16)
            for j in range(NY):
                part[c, jnp.where(even, i, j), jnp.where(even, j, i)] = tile[j * 64 : (j + 1) * 64]
        for o in range(1, 4):
            send_first(c, o).start()

    def middle(c):
        whole(gx, gx_send, gx_recv, c).wait_recv()
        mine = jnp.where(c % 2 == 0, x, y)
        for j in range(4):
            total = part[c, mine, j].astype(F32)
            for o in range(3):
                total += gx[c, o, j].astype(F32)
            half[c, j] = total.astype(BF16)
        for o in range(1, 4):
            send_second(c, o).start()

    def last(c):
        whole(gy, gy_send, gy_recv, c).wait_recv()
        mine = jnp.where(c % 2 == 0, y, x)
        total = half[c, mine].astype(F32)
        for o in range(3):
            total += gy[c, o].astype(F32)
        out_ref[:, columns(c)] = total

    def step(i):
        @pl.when(i < n)
        def _():
            product(i)

        @pl.when((i >= LAG) & (i < n + LAG))
        def _():
            middle(i - LAG)

        @pl.when(i >= 2 * LAG)
        def _():
            last(i - 2 * LAG)

    over(0, n + 2 * LAG, step)

    for g in range(n_left):
        left(g).wait_send()

    def sent(c):
        right(c).wait_send()
        whole(gx, gx_send, gx_recv, c).wait_send()
        whole(gy, gy_send, gy_recv, c).wait_send()

    over(0, n, sent)


def weight_gradients(lefts, groups, collective_id, name):
    first_of, at = [0], 0
    flat = []
    for arrays in groups:
        for a in arrays:
            flat.append(a)
            at += a.shape[1]
        first_of.append(at // WIDE)
    left = jnp.stack(lefts)
    right = jnp.concatenate(flat, 1)
    n, n_left = at // WIDE, len(lefts)
    own = MODEL // NZ
    dma = pltpu.SemaphoreType.DMA
    return pl.pallas_call(
        functools.partial(weight_kernel, tuple(first_of)),
        name=name,
        out_shape=jax.ShapeDtypeStruct((own // (NX * NY), at), F32),
        in_specs=vmem(2),
        out_specs=vmem(1)[0],
        scratch_shapes=[
            pltpu.VMEM((n_left, own, ROWS), BF16),
            pltpu.VMEM((n, ROWS, WIDE), BF16),
            pltpu.VMEM((n, 4, 4, 64, WIDE), BF16),
            pltpu.VMEM((n, 3, 4, 64, WIDE), BF16),
            pltpu.VMEM((n, 4, 64, WIDE), BF16),
            pltpu.VMEM((n, 3, 64, WIDE), BF16),
            dma((n_left,)), dma((n_left,)),
            *[dma((n,))] * 6,
        ],
        compiler_params=params(collective_id),
    )(left, right)


SMALL = 8 * 128
TAIL = 80


def gather_kernel(
    w_ref, e_ref, out_ref, got, mine, e_send, e_recv, w_send, w_recv, sib_send, sib_recv
):
    me, c, zh = block_index(), lax.axis_index("c"), lax.axis_index("zh")
    chip = zh * BLOCKS + me
    sibling = {"c": 1 - c}

    def chip_at(p):
        return {"zh": p // BLOCKS, **block_at(p % BLOCKS)}

    barrier = pltpu.get_barrier_semaphore()
    over(1, CHIPS, lambda o: signal(barrier, chip_at((chip + o) % CHIPS)))
    signal(barrier, sibling)
    pl.semaphore_wait(barrier, CHIPS)

    def share(o):
        d = (me + o) % BLOCKS
        return remote(e_ref.at[d], got.at[o], e_send.at[o], e_recv.at[o], block_at(d))

    over(1, BLOCKS, lambda o: share(o).start())
    got[0] = e_ref[me]

    def add(o, total):
        share(o).wait_recv()
        return total + got[o]

    total = lax.fori_loop(1, BLOCKS, add, got[0])
    mine[:64] = w_ref[...].astype(BF16)
    mine[64:] = jnp.zeros((TAIL - 64, 2 * 128), BF16)
    mine[64:, :128] = jnp.concatenate([total, jnp.zeros_like(total)], 0).astype(BF16)
    out_ref[c, chip] = mine[...]

    def spread(o):
        d = (chip + o) % CHIPS
        return remote(mine, out_ref.at[c, chip], w_send.at[o], w_recv.at[o], chip_at(d))

    def arrived(o):
        s = (chip + CHIPS - o) % CHIPS
        return s, remote(mine, out_ref.at[c, s], w_send.at[o], w_recv.at[o], chip_at(s))

    def to_sibling(s, core):
        return remote(
            out_ref.at[core, s], out_ref.at[core, s], sib_send.at[s], sib_recv.at[s], sibling
        )

    over(1, CHIPS, lambda o: spread(o).start())
    to_sibling(chip, c).start()

    def pass_on(o):
        s, copy = arrived(o)
        copy.wait_recv()
        to_sibling(s, c).start()

    over(1, CHIPS, pass_on)
    over(0, CHIPS, lambda s: to_sibling(s, 1 - c).wait_recv())
    over(0, CHIPS, lambda s: to_sibling(s, c).wait_send())
    over(1, CHIPS, lambda o: spread(o).wait_send())
    over(1, BLOCKS, lambda o: share(o).wait_send())


def gather_replicated(weights, small, collective_id):
    dma = pltpu.SemaphoreType.DMA
    return pl.pallas_call(
        gather_kernel,
        name="gather_replicated",
        out_shape=jax.ShapeDtypeStruct((2, CHIPS, TAIL, 256), BF16),
        in_specs=vmem(2),
        out_specs=vmem(1)[0],
        scratch_shapes=[
            pltpu.VMEM((BLOCKS, 8, 128), F32),
            pltpu.VMEM((TAIL, 256), BF16),
            dma((BLOCKS,)), dma((BLOCKS,)),
            *[dma((CHIPS,))] * 4,
        ],
        compiler_params=params(collective_id),
    )(weights, small)


def rms_norm(values, scales):
    return values * lax.rsqrt(jnp.mean(values * values, -1, keepdims=True) + EPSILON) * scales


def rope_turn(values, cosine, sine):
    half = values.shape[-1] // 2
    first, second = values[..., :half], values[..., half:]
    return jnp.concatenate([first * cosine - second * sine, second * cosine + first * sine], -1)


def conv_taps(extended, seg_extended, kernel):
    tap_count = kernel.shape[0]
    row_count = extended.shape[0] - tap_count + 1
    own_segment = seg_extended[tap_count - 1 :]
    running_sum = jnp.zeros((row_count, extended.shape[1]), F32)
    for tap_index in range(tap_count):
        same_doc = seg_extended[tap_index : tap_index + row_count] == own_segment
        running_sum = running_sum + kernel[tap_index] * jnp.where(
            same_doc[:, None], extended[tap_index : tap_index + row_count], 0.0
        )
    return running_sum


def state_part(x_values, step_sizes, b_matrix, rates, segment, seg_before):
    cumulative = jnp.cumsum(-step_sizes * rates, 0)
    carry_weight = (
        jnp.exp(cumulative[-1][None, :] - cumulative)
        * (segment == segment[-1]).astype(F32)[:, None]
    )
    moved = x_values * (step_sizes * carry_weight)[:, :, None]
    local_state = jnp.einsum("jhp,jn->hpn", moved, b_matrix, precision=HIGHEST)
    through = jnp.exp(cumulative[-1]) * (segment[-1] == seg_before).astype(F32)
    return (local_state, through)


def output_part(x_values, step_sizes, cb_product, c_matrix, rates, segment, seg_before, state_in):
    cumulative = jnp.cumsum(-step_sizes * rates, 0)
    row_index = jnp.arange(segment.shape[0])
    causal = (row_index[None, :] <= row_index[:, None]) & (segment[None, :] == segment[:, None])
    gaps = jnp.where(causal[:, :, None], cumulative[:, None, :] - cumulative[None, :, :], -jnp.inf)
    mixing = jnp.exp(gaps) * cb_product[:, :, None]
    moved = x_values * step_sizes[:, :, None]
    inner = jnp.einsum("ijh,jhp->ihp", mixing, moved, precision=HIGHEST)
    entry = jnp.exp(cumulative) * (segment == seg_before).astype(F32)[:, None]
    outer = jnp.einsum("in,hpn->ihp", c_matrix, state_in, precision=HIGHEST) * entry[:, :, None]
    return inner + outer


def on_device(
    tokens, segment_ids, cotangent, norm1_gain, x_weight, z_weight, bc_weight, dt_weight,
    x_conv, bc_conv, dt_bias, decay_rate, skip_gain, out_weight, query_weight, kv_weight,
    attn_weight, norm2_gain, gate_weight, up_weight, down_weight,
):
    edge_rows = CONV - 1
    zh, c = lax.axis_index("zh"), lax.axis_index("c")
    head_index = zh * 2 + c
    heads = decay_rate.shape[0]
    inner = x_weight.shape[1]
    q_heads = query_weight.shape[1] // HEAD_DIM
    positions = block_index() * ROWS + jnp.arange(ROWS)
    half_dim = HEAD_DIM // 2
    frequency = ROPE_BASE ** (-(jnp.arange(half_dim).astype(F32) * 2.0 / HEAD_DIM))
    angles = positions.astype(F32)[:, None] * frequency[None, :]
    cosine, sine = jnp.cos(angles), jnp.sin(angles)

    x_input = tokens.astype(F32)
    normed_f, norm_back = jax.vjp(rms_norm, x_input, norm1_gain)
    normed = normed_f.astype(BF16)
    kv_at = c * (KVHEADS * HEAD_DIM) + zh * HEAD_DIM
    kv_columns = lax.dynamic_slice_in_dim(kv_weight, kv_at, HEAD_DIM, 1)
    kv_raw = dot(normed, kv_columns)
    kv_own = jnp.where(c == 0, rope_turn(kv_raw, cosine, sine), kv_raw).astype(BF16)
    query_raw = dot(normed, query_weight).reshape(ROWS, q_heads, HEAD_DIM)
    queries = rope_turn(query_raw, cosine[:, None, :], sine[:, None, :]).astype(BF16)
    queries = queries.transpose(1, 0, 2).reshape(q_heads * ROWS, HEAD_DIM)
    x_pre = dot(normed, x_weight).astype(BF16)
    bc_pre = dot(normed, bc_weight).astype(BF16)
    z_val = dot(normed, z_weight)
    dt_raw = dot(normed, dt_weight)

    seg_low = segment_ids.astype(BF16)
    own_block = jnp.concatenate(
        [kv_own, jnp.pad(seg_low.reshape(2, HEAD_DIM), ((0, 14), (0, 0)))], 0
    )
    seg_row = jnp.broadcast_to(jnp.tile(segment_ids.astype(F32), q_heads), (8, q_heads * ROWS))
    edge = jnp.concatenate(
        [x_pre[-16:], bc_pre[-16:], jnp.broadcast_to(seg_low[-16:, None], (16, 128))], 1
    )
    attended, lse, kv_all, edge_in = attention_forward(queries, own_block, seg_row, edge)
    edge_in = edge_in[-edge_rows:]
    seg_extended = jnp.concatenate([edge_in[:, inner + 2 * STATE].astype(jnp.int32), segment_ids])
    seg_before = seg_extended[edge_rows - 1]
    x_extended = jnp.concatenate([edge_in[:, :inner], x_pre]).astype(F32)
    bc_extended = jnp.concatenate([edge_in[:, inner : inner + 2 * STATE], bc_pre]).astype(F32)

    def conv_silu(extended, kernel):
        return jax.nn.silu(conv_taps(extended, seg_extended, kernel))

    x_act_f, x_conv_back = jax.vjp(conv_silu, x_extended, x_conv)
    bc_act_f = conv_silu(bc_extended, bc_conv)
    bc_at = head_index * 128
    _, bc_conv_back = jax.vjp(
        conv_silu,
        lax.dynamic_slice_in_dim(bc_extended, bc_at, 128, 1),
        lax.dynamic_slice_in_dim(bc_conv, bc_at, 128, 1),
    )
    x_heads = x_act_f.astype(BF16).astype(F32).reshape(ROWS, heads, SSM_DIM)
    bc_low = bc_act_f.astype(BF16)
    bc_act = bc_low.astype(F32)
    b_matrix, c_matrix = bc_act[:, :STATE], bc_act[:, STATE:]
    cb_product = dot(bc_low[:, STATE:], bc_low[:, :STATE], 1, 1)
    dt_pre = dt_raw + dt_bias
    step_sizes = jax.nn.softplus(dt_pre)

    def state_fn(x_values, step_vals, b_vals, rate_vals):
        return state_part(x_values, step_vals, b_vals, rate_vals, segment_ids, seg_before)

    (local_state, through), state_part_back = jax.vjp(
        state_fn, x_heads, step_sizes, b_matrix, decay_rate
    )
    state_in = scan_states(local_state, through, False, 3)

    def output_fn(x_values, step_vals, cb_vals, c_vals, rate_vals, entry_state):
        return output_part(
            x_values, step_vals, cb_vals, c_vals, rate_vals, segment_ids, seg_before, entry_state
        )

    ssm_core, output_back = jax.vjp(
        output_fn, x_heads, step_sizes, cb_product, c_matrix, decay_rate, state_in
    )
    ssm_out = (ssm_core + skip_gain[None, :, None] * x_heads).reshape(ROWS, inner)
    z_gate = jax.nn.silu(z_val)
    gated = (ssm_out * z_gate).astype(BF16)
    attended_low = (
        attended.astype(BF16).reshape(q_heads, ROWS, HEAD_DIM).transpose(1, 0, 2)
        .reshape(ROWS, q_heads * HEAD_DIM)
    )
    mixer_part = dot(gated, out_weight) + dot(attended_low, attn_weight)
    hidden_in = x_input + head_sum(mixer_part.astype(BF16), 4).astype(F32)

    normed_two_f, norm_two_back = jax.vjp(rms_norm, hidden_in, norm2_gain)
    normed_two = normed_two_f.astype(BF16)
    gate_val = dot(normed_two, gate_weight)
    up_val = dot(normed_two, up_weight)
    gate_sig = jax.nn.sigmoid(gate_val)
    gate_act = gate_val * gate_sig
    hidden = (gate_act * up_val).astype(BF16)
    grad_hidden = dot(cotangent, down_weight, 1, 1)
    grad_gate = (grad_hidden * up_val * gate_sig * (1.0 + gate_val * (1.0 - gate_sig))).astype(BF16)
    grad_up = (grad_hidden * gate_act).astype(BF16)
    ffn_part = dot(hidden, down_weight).astype(BF16)
    back_part = (dot(grad_gate, gate_weight, 1, 1) + dot(grad_up, up_weight, 1, 1)).astype(BF16)
    sums = head_sum(jnp.concatenate([back_part, ffn_part], 0), 5).astype(F32)
    output = (hidden_in + sums[ROWS:]).astype(BF16)
    grad_from_two, grad_gain_two = norm_two_back(sums[:ROWS])
    grad_hidden_in = grad_from_two + cotangent.astype(F32)
    grad_mix = grad_hidden_in.astype(BF16)
    ffn_w = weight_gradients(
        [normed_two.T, cotangent.T], [[grad_gate, grad_up], [hidden]], 6, "ffn_weights"
    )

    grad_gated = dot(grad_mix, out_weight, 1, 1)
    grad_attended = (
        dot(grad_mix, attn_weight, 1, 1).astype(BF16).reshape(ROWS, q_heads, HEAD_DIM)
        .transpose(1, 0, 2).reshape(q_heads * ROWS, HEAD_DIM)
    )
    z_sig = jax.nn.sigmoid(z_val)
    grad_z = (grad_gated * ssm_out * z_sig * (1.0 + z_val * (1.0 - z_sig))).astype(BF16)
    grad_ssm = (grad_gated * z_gate).reshape(ROWS, heads, SSM_DIM)
    grad_skip = jnp.sum(grad_ssm * x_heads, (0, 2))
    out_grads = output_back(grad_ssm)
    state_grad = scan_states(out_grads[5], through, True, 7)
    grad_through = jnp.sum(state_grad * state_in, (1, 2))
    state_grads = state_part_back((state_grad, grad_through))
    grad_cb = out_grads[2]
    grad_b = state_grads[2] + jnp.dot(grad_cb.T, c_matrix, precision=HIGHEST)
    grad_c = out_grads[3] + jnp.dot(grad_cb, b_matrix, precision=HIGHEST)
    grad_x_heads = out_grads[0] + state_grads[0] + skip_gain[None, :, None] * grad_ssm
    grad_rate = out_grads[4] + state_grads[3]
    grad_dt_pre = (out_grads[1] + state_grads[1]) * jax.nn.sigmoid(dt_pre)
    grad_dt_raw = grad_dt_pre.astype(BF16)
    grad_bias = jnp.sum(grad_dt_pre, 0)
    shares = jnp.concatenate([grad_b, grad_c], -1).astype(BF16)
    shares = shares.reshape(ROWS, 4, 128).transpose(1, 0, 2)
    grad_bc_act = head_share(shares, 8)
    grad_x_ext, grad_x_conv = x_conv_back(grad_x_heads.reshape(ROWS, inner))
    grad_bc_ext, grad_bc_conv = bc_conv_back(grad_bc_act)
    edge_back = jnp.pad(
        jnp.concatenate([grad_x_ext[:edge_rows], grad_bc_ext[:edge_rows]], 1),
        ((0, 8 - edge_rows), (0, 0)),
    )
    delta = jnp.sum(grad_attended.astype(F32) * attended, 1)
    delta = jnp.broadcast_to(delta, (8, q_heads * ROWS))
    grad_query, grad_kv, edge_next = attention_backward(
        queries, grad_attended, lse, delta, seg_row, kv_all, edge_back
    )
    edge_next = edge_next[:edge_rows]
    grad_x_pre = grad_x_ext[edge_rows:].at[-edge_rows:].add(edge_next[:, :inner]).astype(BF16)
    grad_bc_low = grad_bc_ext[edge_rows:].at[-edge_rows:].add(edge_next[:, inner:]).astype(BF16)
    score_scale = HEAD_DIM**-0.5
    grad_query = (grad_query * score_scale).reshape(q_heads, ROWS, HEAD_DIM).transpose(1, 0, 2)
    grad_query_raw = (
        rope_turn(grad_query, cosine[:, None, :], -sine[:, None, :]).astype(BF16)
        .reshape(ROWS, q_heads * HEAD_DIM)
    )
    grad_kv_low = jnp.where(
        c == 0, rope_turn(grad_kv * score_scale, cosine, -sine), grad_kv
    ).astype(BF16)
    bc_columns = lax.dynamic_slice_in_dim(bc_weight, bc_at, 128, 1)
    back_part = (
        dot(grad_x_pre, x_weight, 1, 1)
        + dot(grad_z, z_weight, 1, 1)
        + dot(grad_dt_raw, dt_weight, 1, 1)
        + dot(grad_query_raw, query_weight, 1, 1)
        + dot(grad_bc_low, bc_columns, 1, 1)
        + dot(grad_kv_low, kv_columns, 1, 1)
    )
    grad_normed = head_sum(back_part.astype(BF16), 9).astype(F32)
    grad_from_one, grad_gain_one = norm_back(grad_normed)
    grad_tokens = grad_hidden_in + grad_from_one
    dt_wide = jnp.pad(grad_dt_raw, ((0, 0), (0, WIDE - heads)))
    mixer_w = weight_gradients(
        [normed.T, grad_mix.T],
        [
            [grad_x_pre, grad_z, grad_query_raw, grad_bc_low, grad_kv_low, dt_wide],
            [gated, attended_low],
        ],
        10,
        "mixer_weights",
    )
    quarter = MODEL // 4
    small = [
        grad_x_conv, grad_bc_conv, grad_bias, grad_rate, grad_skip,
        lax.dynamic_slice_in_dim(grad_gain_one, head_index * quarter, quarter),
        lax.dynamic_slice_in_dim(grad_gain_two, head_index * quarter, quarter),
    ]
    flat = jnp.concatenate([a.reshape(-1) for a in small])
    flat = jnp.pad(flat, (0, BLOCKS * SMALL - flat.size)).reshape(BLOCKS, 8, 128)
    at = [0, inner, 2 * inner, 2 * inner + 256, 2 * inner + 512, 2 * inner + 768]
    gathered = gather_replicated(mixer_w[:, at[3] : at[4]], flat, 11)
    gathered = gathered.reshape(2, 2, BLOCKS, TAIL, 256).astype(F32)
    bc_w = gathered[:, :, :, :64, :128].transpose(2, 3, 1, 0, 4).reshape(MODEL, 512)
    kv_w = gathered[:, :, :, :64, 128:].transpose(2, 3, 0, 1, 4).reshape(MODEL, 512)
    total = gathered[:, :, :, 64:72, :128].transpose(1, 0, 2, 3, 4).reshape(4, BLOCKS * SMALL)
    pieces, start = [], 0
    for a in small:
        pieces.append(total[:, start : start + a.size].reshape(4, *a.shape))
        start += a.size
    x_conv_sum = pieces[0].transpose(1, 0, 2).reshape(CONV, 4 * inner)
    bc_conv_sum = pieces[1].transpose(1, 0, 2).reshape(CONV, 512)
    bias_sum, rate_sum, skip_sum, gain_one_sum, gain_two_sum = (p.reshape(-1) for p in pieces[2:])
    ff = gate_weight.shape[1]
    return (
        output,
        grad_tokens,
        gain_one_sum,
        mixer_w[:, : at[1]],
        mixer_w[:, at[1] : at[2]],
        bc_w,
        mixer_w[:, at[4] : at[4] + heads],
        x_conv_sum,
        bc_conv_sum,
        bias_sum,
        rate_sum,
        skip_sum,
        mixer_w[:, at[5] : at[5] + inner].T,
        mixer_w[:, at[2] : at[3]],
        kv_w,
        mixer_w[:, at[5] + inner :].T,
        gain_two_sum,
        ffn_w[:, :ff],
        ffn_w[:, ff : 2 * ff],
        ffn_w[:, 2 * ff :].T,
    )


def solution(mesh):
    split = Mesh(mesh.devices.reshape(NZ, NX, NY, 2, 2), (*SEQ, "zh", "c"))
    head = ("zh", "c")
    rows, columns, both, turned = P(SEQ, None), P(None, head), P(SEQ, head), P(head, SEQ)
    return jax.shard_map(
        on_device,
        mesh=split,
        in_specs=(
            rows, P(SEQ), rows, P(), columns, columns, P(), columns, columns, P(), P(head),
            P(head), P(head), P(head, None), columns, P(), P(head, None), P(), columns, columns,
            P(head, None),
        ),
        out_specs=(
            rows, rows, P(), both, both, P(), both, P(), P(), P(), P(), P(), turned, both, P(),
            turned, P(), both, both, turned,
        ),
        check_vma=False,
    )
```

time: 1730 us -> 738 us (0.43)
  the two profiles are of different devices: /device:TPU:0 before, /device:TPU:1 now
where the time goes in v1:
time: 738 us; the launch traced here: 729 us
  Pallas kernels  465 us (63%)
  local copies, waits for them, and re-layouts  118 us (16%)
  other arithmetic  80.4 us (11%)
  matrix products  61.2 us (8%)
    pallas_call x2, Pallas kernels, weight_gradients(): pl.pallas_call(functools.partial(weight_kernel, tuple(first_of)), name=na...  151 us
    pallas_call x3, Pallas kernels, head_sum(): pl.pallas_call(head_sum_kernel, name=f'head_sum_{collective_id}', out_sha...  77 us
    pallas_call x2, Pallas kernels, scan_states(): pl.pallas_call(functools.partial(scan_kernel, reverse), name='scan_back'...  76.6 us
    pallas_call x1, Pallas kernels, gather_replicated(): pl.pallas_call(gather_kernel, name='gather_replicated', out_shape=jax.Sha...  63.4 us
    pallas_call x1, Pallas kernels, attention_backward(): pl.pallas_call(attention_backward_kernel, name='attention_backward', out_...  52.3 us
    dot_general x23, matrix products, dot(): lax.dot_general(a, b, (((left,), (right,)), ((), ())), preferred_element_...  42.3 us
    pallas_call x1, Pallas kernels, attention_forward(): pl.pallas_call(attention_forward_kernel, name='attention_forward', out_sh...  36.1 us
    unnamed x269, local copies, waits for them, and re-layouts  24.4 us

profile of v1, /device:TPU:1, one launch (start us, length us, event | category | flops | bytes accessed | tf_op | source)
XLA Modules:
  0.0 728.8 jit_solution(12812106085706886397)
XLA Ops:
  10.6 2.3 copy.252
  12.9 1.7 fusion.20
  14.6 2.2 fusion.66
  22.3 1.7 copy.313
  26.3 2.7 fusion.99
  31.3 3.5 convolution_convert_fusion.3
  36.2 2.3 copy.277
  38.5 36.1 %attention_forward.1 = (f32[512,128]{1,0:T(8,128)}, f32[8,512]{1,0:T(8,128)}, bf16[2,32,272,128]{3,2,1,0:T(8,128)(2,1)}, bf16[16,1408]{1,0:T(8,128)(2,1)}) custom-call(bf16[512,128]{1,0:T(8,128)(2,1)} %bitcast.312, bf16[272,128]{1,0:T(8,128)(2,1)} %fusion.135.own_ref, f32[8,512]{1,0:T(8,128)} %broadcast_in_dim.179.qseg_ref, ...), custom_call_target="tpu_custom_call" | custom-call | tf_op jit(solution)/shard_map/attention_forward/pallas_call | solution.py:172
  77.9 1.9 slice_compare_fusion.2
  89.5 1.6 copy.262
  92.1 1.6 copy.272
  93.7 2.0 maximum_convert_fusion
  95.6 1.7 mul.804
  97.3 2.3 copy.284
  100.5 2.3 copy.282
  102.8 4.1 fusion.149
  106.9 2.3 copy.283
  109.2 2.2 fusion.68
  111.4 2.3 copy.259
  116.4 48.5 %scan_ahead.1 = bf16[32,32,256]{2,1,0:T(8,128)(2,1)} custom-call(bf16[32,32,256]{2,1,0:T(8,128)(2,1)} %pad_maximum_fusion.5.part_ref), custom_call_target="tpu_custom_call" | custom-call | tf_op jit(solution)/shard_map/scan_ahead/pallas_call | solution.py:386
  167.1 4.6 fusion.44
  171.6 2.3 copy.273
  173.9 4.7 multiply_convert_fusion.5
  179.4 2.1 fusion.11.x_ref
  181.5 23.1 %head_sum_4.1 = bf16[256,2048]{1,0:T(8,128)(2,1)} custom-call(bf16[256,2048]{1,0:T(8,128)(2,1)} %fusion.11.x_ref), custom_call_target="tpu_custom_call" | custom-call | tf_op jit(solution)/shard_map/head_sum_4/pallas_call | solution.py:452
  204.6 2.6 copy.275
  207.3 2.1 multiply_reduce_fusion.2
  211.1 3.9 fusion.172
  217.5 1.6 multiply_convert_fusion.2
  225.8 32.9 %head_sum_5.1 = bf16[512,2048]{1,0:T(8,128)(2,1)} custom-call(bf16[512,2048]{1,0:T(8,128)(2,1)} %pad_maximum_fusion.x_ref), custom_call_target="tpu_custom_call" | custom-call | tf_op jit(solution)/shard_map/head_sum_5/pallas_call | solution.py:452
  258.7 3.9 copy.276
  262.6 2.3 convert_element_type.280
  266.7 1.9 convert_bitcast_fusion
  271.0 1.7 copy.281
  274.4 2.4 copy.308
  276.8 4.8 multiply_reduce_fusion.3
  287.8 4.3 fusion.24
  295.7 28.1 %scan_back.1 = bf16[32,32,256]{2,1,0:T(8,128)(2,1)} custom-call(bf16[32,32,256]{2,1,0:T(8,128)(2,1)} %pad_maximum_fusion.4.part_ref), custom_call_target="tpu_custom_call" | custom-call | tf_op jit(solution)/shard_map/scan_back/pallas_call | solution.py:386
  326.9 1.7 convolution_bitcast_fusion.1
  331.4 9.2 %head_share.1 = f32[256,128]{1,0:T(8,128)} custom-call(bf16[4,256,128]{2,1,0:T(8,128)(2,1)} %maximum_bitcast_fusion.x_ref), custom_call_target="tpu_custom_call" | custom-call | tf_op jit(solution)/shard_map/head_share/pallas_call | solution.py:488
  340.6 1.9 multiply_reduce_fusion.16
  343.5 4.8 multiply_reduce_fusion.11
  348.6 2.5 reduce-window.24
  351.9 2.9 reduce-window.26
  360.1 2.9 multiply_reduce_fusion.7
  363.1 2.7 pad_maximum_fusion.2.l_ref
  365.8 74.4 %ffn_weights.1 = f32[64,3072]{1,0:T(8,128)} custom-call(bf16[2,2048,256]{2,1,0:T(8,128)(2,1)} %pad_maximum_fusion.2.l_ref, bf16[256,3072]{1,0:T(8,128)(2,1)} %pad_maximum_fusion.3.r_ref), custom_call_target="tpu_custom_call" | custom-call | tf_op jit(solution)/shard_map/ffn_weights/pallas_call | solution.py:632
  440.2 2.0 slice_bitcast_fusion.3
  443.3 52.3 %attention_backward.1 = (f32[512,128]{1,0:T(8,128)}, f32[256,128]{1,0:T(8,128)}, f32[8,896]{1,0:T(8,128)}) custom-call(bf16[512,128]{1,0:T(8,128)(2,1)} %bitcast.313, bf16[512,128]{1,0:T(8,128)(2,1)} %bitcast.307, f32[8,512]{1,0:T(8,128)} %get-tuple-element.53.lse_ref, f32[8,512]{1,0:T(8,128)} %broadcast_in_dim.193.delta_ref, ...), custom_call_target="tpu_custom_call" | custom-call | tf_op jit(solution)/shard_map/attention_backward/pallas_call | solution.py:294
  502.9 1.8 constant_dynamic-update-slice_fusion.2
  514.3 21.0 %head_sum_9.1 = bf16[256,2048]{1,0:T(8,128)(2,1)} custom-call(bf16[256,2048]{1,0:T(8,128)(2,1)} %fusion.13.x_ref), custom_call_target="tpu_custom_call" | custom-call | tf_op jit(solution)/shard_map/head_sum_9/pallas_call | solution.py:452
  535.3 2.4 copy.301
  537.7 2.4 fusion.17
  540.2 2.1 fusion.150
  543.9 76.6 %mixer_weights.1 = f32[64,3328]{1,0:T(8,128)} custom-call(bf16[2,2048,256]{2,1,0:T(8,128)(2,1)} %pad_maximum_fusion.1.l_ref, bf16[256,3328]{1,0:T(8,128)(2,1)} %copy-done.33), custom_call_target="tpu_custom_call" | custom-call | tf_op jit(solution)/shard_map/mixer_weights/pallas_call | solution.py:632
  624.3 1.9 slice_bitcast_fusion.4
  626.3 1.8 copy.309
  628.1 63.4 %gather_replicated.1 = bf16[2,64,80,256]{3,2,1,0:T(8,128)(2,1)} custom-call(f32[64,256]{1,0:T(8,128)} %get-tuple-element.208.w_ref, f32[32,8,128]{2,1,0:T(8,128)} %pad_bitcast_fusion.e_ref), custom_call_target="tpu_custom_call" | custom-call | tf_op jit(solution)/shard_map/gather_replicated/pallas_call | solution.py:718
  691.5 3.9 convert.27
  695.5 2.7 slice_bitcast_fusion
  698.3 5.2 copy.306
  703.5 6.4 reshape.578
  714.6 7.5 %copy.303 = f32[32,64,2,2,128]{4,3,2,1,0:T(2,128)} copy(f32[32,64,2,2,128]{4,1,0,2,3:T(8,128)} %get-tuple-element.198) | data formatting | bytes 8388608 | tf_op jit(solution)/shard_map/transpose | solution.py:975
  722.1 6.6 reshape.570
  (435 shorter events, 107.2 us)
Async XLA Ops:
  0.7 178.7 %copy-start = (bf16[768,2048]{1,0:T(8,128)(2,1)S(1)}, bf16[768,2048]{1,0:T(8,128)(2,1)}, u32[]{:S(2)}) copy-start(bf16[768,2048]{1,0:T(8,128)(2,1)} %param.38) | copy-start | bytes 9437188
  0.7 14.0 %copy-start.71 = (f32[2048]{0:T(1024)S(1)}, f32[2048]{0:T(1024)}, u32[]{:S(2)}) copy-start(f32[2048]{0:T(1024)} %param.28) | copy-start | bytes 24580
  2.1 14.7 %copy-start.95 = (f32[256]{0:T(256)}, f32[256]{0:T(256)S(1)}, u32[]{:S(2)}) copy-start(f32[256]{0:T(256)S(1)} %add_convert_fusion.2) | copy-start | bytes 3076
  2.1 14.7 %copy-start.105 = (f32[64]{0:T(128)}, f32[64]{0:T(128)S(1)}, u32[]{:S(2)}) copy-start(f32[64]{0:T(128)S(1)} %negate_power_fusion) | copy-start | bytes 772
  10.6 13.4 %copy-start.42 = (f32[256,64]{1,0:T(8,128)}, f32[256,64]{1,0:T(8,128)S(1)}, u32[]{:S(2)}) copy-start(f32[256,64]{1,0:T(8,128)S(1)} %get-tuple-element.260) | copy-start | bytes 196612
  12.9 5.2 copy-start.62
  14.6 16.7 %copy-start.93 = (f32[256]{0:T(256)}, f32[256]{0:T(256)S(1)}, u32[]{:S(2)}) copy-start(f32[256]{0:T(256)S(1)} %fusion.140) | copy-start | bytes 3076
  35.6 39.8 %copy-start.73 = (s32[256]{0:T(256)S(1)}, s32[256]{0:T(256)}, u32[]{:S(2)}) copy-start(s32[256]{0:T(256)} %param.26) | copy-start | bytes 3076
  79.8 7.9 %copy-start.74 = (pred[256]{0:T(512)(128)(4,1)}, pred[256]{0:T(512)(128)(4,1)S(1)}, u32[]{:S(2)}) copy-start(pred[256]{0:T(512)(128)(4,1)S(1)} %get-tuple-element.251) | copy-start | bytes 772
  79.8 7.9 %copy-start.77 = (pred[256]{0:T(512)(128)(4,1)}, pred[256]{0:T(512)(128)(4,1)S(1)}, u32[]{:S(2)}) copy-start(pred[256]{0:T(512)(128)(4,1)S(1)} %get-tuple-element.252) | copy-start | bytes 772
  79.8 7.9 %copy-start.80 = (pred[256]{0:T(512)(128)(4,1)}, pred[256]{0:T(512)(128)(4,1)S(1)}, u32[]{:S(2)}) copy-start(pred[256]{0:T(512)(128)(4,1)S(1)} %get-tuple-element.253) | copy-start | bytes 772
  79.8 8.9 %copy-start.83 = (f32[256]{0:T(256)}, f32[256]{0:T(256)S(1)}, u32[]{:S(2)}) copy-start(f32[256]{0:T(256)S(1)} %get-tuple-element.262) | copy-start | bytes 3076
  82.9 5.7 copy-start.40
  82.9 5.7 copy-start.97
  82.9 5.7 copy-start.107
  115.4 51.5 %copy-start.25 = (f32[256,768]{0,1:T(8,128)S(1)}, f32[256,768]{0,1:T(8,128)}, u32[]{:S(2)}) copy-start(f32[256,768]{0,1:T(8,128)} %copy.259) | copy-start | bytes 2359300
  115.5 51.5 %copy-start.58 = (f32[256,256]{1,0:T(8,128)S(1)}, f32[256,256]{1,0:T(8,128)}, u32[]{:S(2)}) copy-start(f32[256,256]{1,0:T(8,128)} %fusion.129) | copy-start | bytes 786436
  115.5 51.5 %copy-start.60 = (f32[256,12]{0,1:T(8,128)S(1)}, f32[256,12]{0,1:T(8,128)}, u32[]{:S(2)}) copy-start(f32[256,12]{0,1:T(8,128)} %copy.272) | copy-start | bytes 36868
  115.5 51.5 %copy-start.65 = (pred[256,256]{1,0:T(8,128)(4,1)S(1)}, pred[256,256]{1,0:T(8,128)(4,1)}, u32[]{:S(2)}) copy-start(pred[256,256]{1,0:T(8,128)(4,1)} %fusion.75) | copy-start | bytes 196612
  115.5 51.5 %copy-start.85 = (f32[256,12]{0,1:T(8,128)S(1)}, f32[256,12]{0,1:T(8,128)}, u32[]{:S(2)}) copy-start(f32[256,12]{0,1:T(8,128)} %copy.265) | copy-start | bytes 36868
  115.5 51.5 %copy-start.88 = (f32[256,12]{0,1:T(8,128)S(1)}, f32[256,12]{0,1:T(8,128)}, u32[]{:S(2)}) copy-start(f32[256,12]{0,1:T(8,128)} %copy.262) | copy-start | bytes 36868
  115.5 51.5 %copy-start.123 = (f32[12]{0:T(128)S(1)}, f32[12]{0:T(128)}, u32[]{:S(2)}) copy-start(f32[12]{0:T(128)} %param.37) | copy-start | bytes 148
  276.8 5.7 copy-start.29
  287.8 6.3 copy-start.61
  294.2 29.5 %copy-start.24 = (bf16[32,32,256]{2,1,0:T(8,128)(2,1)S(1)}, bf16[32,32,256]{2,1,0:T(8,128)(2,1)}, u32[]{:S(2)}) copy-start(bf16[32,32,256]{2,1,0:T(8,128)(2,1)} %scan_ahead.1) | copy-start | bytes 1572868
  323.7 6.9 copy-start.55
  325.0 15.6 %copy-start.12 = (f32[259,512]{1,0:T(8,128)S(1)}, f32[259,512]{1,0:T(8,128)}, u32[]{:S(2)}) copy-start(f32[259,512]{1,0:T(8,128)} %copy-done.11) | copy-start | bytes 1591300
  325.0 15.6 %copy-start.75 = (pred[256]{0:T(512)(128)(4,1)S(1)}, pred[256]{0:T(512)(128)(4,1)}, u32[]{:S(2)}) copy-start(pred[256]{0:T(512)(128)(4,1)} %copy-done.74) | copy-start | bytes 772
  325.0 15.6 %copy-start.78 = (pred[256]{0:T(512)(128)(4,1)S(1)}, pred[256]{0:T(512)(128)(4,1)}, u32[]{:S(2)}) copy-start(pred[256]{0:T(512)(128)(4,1)} %copy-done.77) | copy-start | bytes 772
  325.0 15.6 %copy-start.81 = (pred[256]{0:T(512)(128)(4,1)S(1)}, pred[256]{0:T(512)(128)(4,1)}, u32[]{:S(2)}) copy-start(pred[256]{0:T(512)(128)(4,1)} %copy-done.80) | copy-start | bytes 772
  325.0 15.6 %copy-start.109 = (f32[128]{0:T(128)S(1)}, f32[128]{0:T(128)}, u32[]{:S(2)}) copy-start(f32[128]{0:T(128)} %get-tuple-element.254) | copy-start | bytes 1540
  325.0 15.6 %copy-start.110 = (f32[128]{0:T(128)S(1)}, f32[128]{0:T(128)}, u32[]{:S(2)}) copy-start(f32[128]{0:T(128)} %get-tuple-element.255) | copy-start | bytes 1540
  325.0 15.6 %copy-start.111 = (f32[128]{0:T(128)S(1)}, f32[128]{0:T(128)}, u32[]{:S(2)}) copy-start(f32[128]{0:T(128)} %get-tuple-element.256) | copy-start | bytes 1540
  328.6 14.8 %copy-start.87 = (f32[256,12]{0,1:T(8,128)S(1)}, f32[256,12]{0,1:T(8,128)}, u32[]{:S(2)}) copy-start(f32[256,12]{0,1:T(8,128)} %copy.265) | copy-start | bytes 36868
  329.6 13.8 %copy-start.90 = (f32[256,12]{0,1:T(8,128)S(1)}, f32[256,12]{0,1:T(8,128)}, u32[]{:S(2)}) copy-start(f32[256,12]{0,1:T(8,128)} %copy.262) | copy-start | bytes 36868
  329.6 13.8 %copy-start.124 = (f32[12]{0:T(128)S(1)}, f32[12]{0:T(128)}, u32[]{:S(2)}) copy-start(f32[12]{0:T(128)} %param.37) | copy-start | bytes 148
  330.7 12.8 %copy-start.49 = (f32[256,12,64]{0,2,1:T(8,128)S(1)}, f32[256,12,64]{0,2,1:T(8,128)}, u32[]{:S(2)}) copy-start(f32[256,12,64]{0,2,1:T(8,128)} %copy-done.48) | copy-start | bytes 2359300
  343.4 8.2 %copy-start.41 = (f32[256,12]{1,0:T(8,128)S(1)}, f32[256,12]{1,0:T(8,128)}, u32[]{:S(2)}) copy-start(f32[256,12]{1,0:T(8,128)} %get-tuple-element.266) | copy-start | bytes 36868
  343.5 8.2 %copy-start.84 = (f32[256]{0:T(256)S(1)}, f32[256]{0:T(256)}, u32[]{:S(2)}) copy-start(f32[256]{0:T(256)} %copy-done.83) | copy-start | bytes 3076
  343.5 8.2 %copy-start.108 = (f32[12]{0:T(128)S(1)}, f32[12]{0:T(128)}, u32[]{:S(2)}) copy-start(f32[12]{0:T(128)} %slice_bitcast_fusion.13) | copy-start | bytes 148
  343.5 8.3 %copy-start.117 = (f32[1,12]{1,0:T(1,128)S(1)}, f32[1,12]{1,0:T(1,128)}, u32[]{:S(2)}) copy-start(f32[1,12]{1,0:T(1,128)} %bitcast_multiply_fusion.7) | copy-start | bytes 148
  348.3 6.8 copy-start.118
  348.3 8.8 %copy-start.112 = (f32[128]{0:T(128)S(1)}, f32[128]{0:T(128)}, u32[]{:S(2)}) copy-start(f32[128]{0:T(128)} %get-tuple-element.256) | copy-start | bytes 1540
  348.3 8.8 %copy-start.113 = (f32[128]{0:T(128)S(1)}, f32[128]{0:T(128)}, u32[]{:S(2)}) copy-start(f32[128]{0:T(128)} %get-tuple-element.257) | copy-start | bytes 1540
  351.4 7.5 %copy-start.50 = (f32[256,12,64]{0,2,1:T(8,128)S(1)}, f32[256,12,64]{0,2,1:T(8,128)}, u32[]{:S(2)}) copy-start(f32[256,12,64]{0,2,1:T(8,128)} %get-tuple-element.203) | copy-start | bytes 2359300
  365.8 76.4 %copy-start.27 = (f32[256,768]{1,0:T(8,128)S(1)}, f32[256,768]{1,0:T(8,128)}, u32[]{:S(2)}) copy-start(f32[256,768]{1,0:T(8,128)} %get-tuple-element.186) | copy-start | bytes 2359300
  365.8 76.4 %copy-start.67 = (f32[768]{0:T(1024)S(1)}, f32[768]{0:T(1024)}, u32[]{:S(2)}) copy-start(f32[768]{0:T(1024)} %get-tuple-element.177) | copy-start | bytes 9220
  365.8 76.4 %copy-start.68 = (f32[768]{0:T(1024)S(1)}, f32[768]{0:T(1024)}, u32[]{:S(2)}) copy-start(f32[768]{0:T(1024)} %get-tuple-element.178) | copy-start | bytes 9220
  365.8 76.4 %copy-start.69 = (f32[768]{0:T(1024)S(1)}, f32[768]{0:T(1024)}, u32[]{:S(2)}) copy-start(f32[768]{0:T(1024)} %get-tuple-element.179) | copy-start | bytes 9220
  365.8 76.4 %copy-start.70 = (f32[768]{0:T(1024)S(1)}, f32[768]{0:T(1024)}, u32[]{:S(2)}) copy-start(f32[768]{0:T(1024)} %get-tuple-element.180) | copy-start | bytes 9220
  365.8 76.4 %copy-start.76 = (pred[256]{0:T(512)(128)(4,1)S(1)}, pred[256]{0:T(512)(128)(4,1)}, u32[]{:S(2)}) copy-start(pred[256]{0:T(512)(128)(4,1)} %copy-done.74) | copy-start | bytes 772
  365.8 76.4 %copy-start.79 = (pred[256]{0:T(512)(128)(4,1)S(1)}, pred[256]{0:T(512)(128)(4,1)}, u32[]{:S(2)}) copy-start(pred[256]{0:T(512)(128)(4,1)} %copy-done.77) | copy-start | bytes 772
  365.8 76.4 %copy-start.82 = (pred[256]{0:T(512)(128)(4,1)S(1)}, pred[256]{0:T(512)(128)(4,1)}, u32[]{:S(2)}) copy-start(pred[256]{0:T(512)(128)(4,1)} %copy-done.80) | copy-start | bytes 772
  443.3 52.3 %copy-start.35 = (f32[256,128]{1,0:T(8,128)S(1)}, f32[256,128]{1,0:T(8,128)}, u32[]{:S(2)}) copy-start(f32[256,128]{1,0:T(8,128)} %copy-done.34) | copy-start | bytes 393220
  514.3 23.4 %copy-start.5 = (bf16[256,2048]{0,1:T(8,128)(2,1)S(1)}, bf16[256,2048]{0,1:T(8,128)(2,1)}, u32[]{:S(2)}) copy-start(bf16[256,2048]{0,1:T(8,128)(2,1)} %copy.252) | copy-start | bytes 3145732
  514.3 23.4 %copy-start.72 = (f32[2048]{0:T(1024)S(1)}, f32[2048]{0:T(1024)}, u32[]{:S(2)}) copy-start(f32[2048]{0:T(1024)} %param.28) | copy-start | bytes 24580
  514.3 23.4 %copy-start.94 = (f32[256]{0:T(256)S(1)}, f32[256]{0:T(256)}, u32[]{:S(2)}) copy-start(f32[256]{0:T(256)} %copy-done.93) | copy-start | bytes 3076
  543.8 76.7 %copy-start.103 = (f32[512]{0:T(512)S(1)}, f32[512]{0:T(512)}, u32[]{:S(2)}) copy-start(f32[512]{0:T(512)} %dynamic_slice.23) | copy-start | bytes 6148
  543.8 76.7 %copy-start.104 = (f32[512]{0:T(512)S(1)}, f32[512]{0:T(512)}, u32[]{:S(2)}) copy-start(f32[512]{0:T(512)} %add_bitcast_fusion) | copy-start | bytes 6148
  543.8 76.7 %copy-start.115 = (f32[12]{0:T(128)S(1)}, f32[12]{0:T(128)}, u32[]{:S(2)}) copy-start(f32[12]{0:T(128)} %get-tuple-element.230) | copy-start | bytes 148
  543.8 76.7 %copy-start.116 = (f32[12]{0:T(128)S(1)}, f32[12]{0:T(128)}, u32[]{:S(2)}) copy-start(f32[12]{0:T(128)} %reduce_sum.315) | copy-start | bytes 148
  543.8 76.7 %copy-start.119 = (f32[12]{0:T(128)S(1)}, f32[12]{0:T(128)}, u32[]{:S(2)}) copy-start(f32[12]{0:T(128)} %add.314) | copy-start | bytes 148
  543.9 82.4 %copy-start.16 = (f32[256,2048]{0,1:T(8,128)S(1)}, f32[256,2048]{0,1:T(8,128)}, u32[]{:S(2)}) copy-start(f32[256,2048]{0,1:T(8,128)} %get-tuple-element.205) | copy-start | bytes 6291460
  722.1 6.6 copy-start.1
  (62 other events, 175.1 us)

commit v2 on v1

v2 whole, which is shorter than its diff:
```python
import functools

import jax
import jax.numpy as jnp
from jax import lax
from jax.experimental import pallas as pl
from jax.experimental.pallas import tpu as pltpu
from jax.sharding import Mesh
from jax.sharding import PartitionSpec as P

SSM_DIM = 64
STATE = 256
CONV = 4
KVHEADS = 2
HEAD_DIM = 128
NZ, NX, NY = 2, 4, 4
BLOCKS = NZ * NX * NY
CHIPS = 2 * BLOCKS
ROWS = 256
MODEL = 2048
SEQ = ("zl", "x", "y")
EPSILON = 1e-05
ROPE_BASE = 100000000000.0
HIGHEST = lax.Precision.HIGHEST
MESH = pl.DeviceIdType.MESH
BF16, F32 = jnp.bfloat16, jnp.float32
MASKED = -1e30
LOG2E = 1.4426950408889634
VMEM_LIMIT = 56 * 2**20


def block_index():
    return (lax.axis_index("zl") * NX + lax.axis_index("x")) * NY + lax.axis_index("y")


def block_at(s):
    return {"zl": s // (NX * NY), "x": (s // NY) % NX, "y": s % NY}


PLANE = NX * NY


def plane_shift(k):
    o = 1 + (k * 7) % (PLANE - 1)
    return o // NY, o % NY


def plane_peer(k, sign):
    dx, dy = plane_shift(k)
    x, y = lax.axis_index("x"), lax.axis_index("y")
    if sign < 0:
        dx, dy = NX - dx, NY - dy
    x, y = (x + dx) % NX, (y + dy) % NY
    return x * NY + y, {"x": x, "y": y}


def signal(sem, where):
    pl.semaphore_signal(sem, inc=1, device_id=where, device_id_type=MESH)


def remote(src, dst, send, recv, where):
    return pltpu.make_async_remote_copy(src, dst, send, recv, device_id=where, device_id_type=MESH)


def over(start, stop, body):
    def step(i, carry):
        body(i)
        return carry

    lax.fori_loop(start, stop, step, 0)


def dot(a, b, left=1, right=0):
    return lax.dot_general(
        a, b, (((left,), (right,)), ((), ())), preferred_element_type=F32
    )


def vmem(n):
    return [pl.BlockSpec(memory_space=pltpu.VMEM)] * n


def params(collective_id):
    return pltpu.CompilerParams(
        collective_id=collective_id, has_side_effects=True, vmem_limit_bytes=VMEM_LIMIT
    )


HEADS = 12
INNER = HEADS * SSM_DIM
GROUPS = INNER // 128
BC = 2 * STATE
SCAN_ROWS = INNER // BLOCKS
EDGE_WIDE = INNER + BC + 128
GRAD_EDGE = INNER + 128


def two_parts(v):
    high = v.astype(BF16)
    return high, (v - high.astype(F32)).astype(BF16)


def low_lanes(rows):
    return lax.broadcasted_iota(jnp.int32, (rows, 128), 1) < SSM_DIM


def widen(v, g):
    low = low_lanes(v.shape[0])
    return jnp.where(low, v[:, 2 * g : 2 * g + 1], v[:, 2 * g + 1 : 2 * g + 2])


def per_head(v, g):
    lane = lax.broadcasted_iota(jnp.int32, v.shape, 1)
    first = jnp.sum(jnp.where(lane < SSM_DIM, v, 0.0), 1, keepdims=True)
    second = jnp.sum(jnp.where(lane < SSM_DIM, 0.0, v), 1, keepdims=True)
    return jnp.where(lane == 2 * g, first, jnp.where(lane == 2 * g + 1, second, 0.0))


def triangle():
    row = lax.broadcasted_iota(jnp.int32, (ROWS, ROWS), 0)
    col = lax.broadcasted_iota(jnp.int32, (ROWS, ROWS), 1)
    return (col <= row).astype(F32).astype(BF16)


def running(v, lower, side):
    high, low = two_parts(v)
    middle, lowest = two_parts(v - high.astype(F32))
    return (
        dot(lower, high, side, 0) + dot(lower, middle, side, 0) + dot(lower, lowest, side, 0)
    )


def sigmoid(v):
    return 1.0 / (1.0 + jnp.exp(-v))


def softplus(v):
    return jnp.maximum(v, 0.0) + jnp.log(1.0 + jnp.exp(-jnp.abs(v)))


def lane_block(g):
    return pl.ds(pl.multiple_of(g * 128, 128), 128)


def decays(dt_ref, vec_ref, seg_ref, segx_ref, lower):
    pre = dt_ref[...] + vec_ref[0:1, :]
    step = softplus(pre)
    total = running(-step * vec_ref[1:2, :] * LOG2E, lower, 1)
    last = total[ROWS - 1 : ROWS, :]
    seg = seg_ref[...]
    seg_last, before = seg[ROWS - 1 : ROWS, :], segx_ref[7:8, :]
    carry = jnp.where(seg == seg_last, jnp.exp2(last - total), 0.0)
    entry = jnp.where(seg == before, jnp.exp2(total), 0.0)
    through = jnp.where(seg_last == before, jnp.exp2(last), 0.0)
    return pre, step, total, carry, entry, through


def conv_group(ext_ref, segx_ref, seg_ref, taps_ref, cols):
    total, inputs = None, []
    for k in range(CONV):
        same = segx_ref[pl.ds(5 + k, ROWS), :] == seg_ref[...]
        v = jnp.where(same, ext_ref[pl.ds(5 + k, ROWS), cols], 0.0)
        inputs.append(v)
        term = taps_ref[k : k + 1, cols] * v
        total = term if total is None else total + term
    return total, inputs


def scan_message(msg_ref, state_ref, through):
    high = through.astype(BF16)
    rest = through - high.astype(F32)
    middle = rest.astype(BF16)
    low = rest - middle.astype(F32)
    extra = jnp.concatenate([high.astype(F32), middle.astype(F32), low, jnp.zeros((5, 128), F32)], 0)
    extra = jnp.concatenate([extra, jnp.zeros((8, STATE - 128), F32)], 1)

    def fill(b):
        rows = state_ref[pl.ds(pl.multiple_of(b * SCAN_ROWS, 8), SCAN_ROWS), :]
        msg_ref[b] = jnp.concatenate([rows, extra], 0).astype(BF16)

    over(0, BLOCKS, fill)


class Scan:
    def __init__(self, reverse, me, msg, got, back, out, send, recv):
        self.reverse, self.me = reverse, me
        self.msg, self.got, self.back, self.out = msg, got, back, out
        self.send, self.recv = send, recv

    def there(self, o):
        d = (self.me + o) % BLOCKS
        return remote(
            self.msg.at[d], self.got.at[self.me], self.send.at[0, o], self.recv.at[0, o],
            block_at(d),
        )

    def arrived(self, phase, dst, o):
        s = (self.me + BLOCKS - o) % BLOCKS
        return remote(
            dst.at[s], dst.at[s], self.send.at[phase, o], self.recv.at[phase, o], block_at(s)
        )

    def start(self):
        over(1, BLOCKS, lambda o: self.there(o).start())
        self.got[self.me] = self.msg[self.me]

    def turn(self):
        me = self.me
        over(1, BLOCKS, lambda o: self.arrived(0, self.got, o).wait_recv())
        lane = lax.broadcasted_iota(jnp.int32, (SCAN_ROWS, 128), 1)
        row = lax.broadcasted_iota(jnp.int32, (SCAN_ROWS, 128), 0) + me * SCAN_ROWS
        at_head = (row >= lane * SSM_DIM) & (row < lane * SSM_DIM + SSM_DIM)

        def scan(i, state):
            k = BLOCKS - 1 - i if self.reverse else i
            message = self.got[k].astype(F32)
            self.back[k] = jnp.concatenate([state, jnp.zeros((8, STATE), F32)], 0).astype(BF16)

            @pl.when(k != me)
            def _():
                self.returned(k).start()

            factors = message[SCAN_ROWS : SCAN_ROWS + 1, :128]
            factors += message[SCAN_ROWS + 1 : SCAN_ROWS + 2, :128]
            factors += message[SCAN_ROWS + 2 : SCAN_ROWS + 3, :128]
            through = jnp.sum(jnp.where(at_head, factors, 0.0), 1, keepdims=True)
            return through * state + message[:SCAN_ROWS]

        lax.fori_loop(0, BLOCKS, scan, jnp.zeros((SCAN_ROWS, STATE), F32))
        self.out[me] = self.back[me]

    def returned(self, k):
        o = (k + BLOCKS - self.me) % BLOCKS
        return remote(
            self.back.at[k], self.out.at[self.me], self.send.at[1, o], self.recv.at[1, o],
            block_at(k),
        )

    def finish(self, state_ref):
        over(1, BLOCKS, lambda o: self.arrived(1, self.out, o).wait_recv())

        def fill(b):
            rows = self.out[b].astype(F32)
            state_ref[pl.ds(pl.multiple_of(b * SCAN_ROWS, 8), SCAN_ROWS), :] = rows[:SCAN_ROWS]

        over(0, BLOCKS, fill)

    def close(self):
        def sent(o):
            self.there(o).wait_send()
            self.returned((self.me + o) % BLOCKS).wait_send()

        over(1, BLOCKS, sent)


def key_segments(block):
    turned = jnp.transpose(block.astype(F32))
    return jnp.concatenate([turned[:, 0:1], turned[:, 1:2]], 0)


def causal_mask(s):
    row = lax.broadcasted_iota(jnp.int32, (ROWS, 2 * ROWS), 0)
    col = lax.broadcasted_iota(jnp.int32, (ROWS, 2 * ROWS), 1) % ROWS
    return jnp.where(row <= col, s, MASKED)


def mixing_bias(seg_ref, segrow_ref):
    row = lax.broadcasted_iota(jnp.int32, (ROWS, ROWS), 0)
    col = lax.broadcasted_iota(jnp.int32, (ROWS, ROWS), 1)
    same = segrow_ref[0:1, :ROWS] == seg_ref[:, 0:1]
    return jnp.where((col <= row) & same, 0.0, MASKED)


WIDE = 256
LAG = 3
OWN = MODEL // NZ


class Reduce:
    def __init__(self, lefts, n, r_ref, rz, part, gx, half, gy, out_ref, sems):
        self.lefts, self.n = lefts, n
        self.r, self.rz, self.part, self.gx, self.half, self.gy = r_ref, rz, part, gx, half, gy
        self.out = out_ref
        (self.rz_send, self.rz_recv, self.gx_send, self.gx_recv, self.gy_send, self.gy_recv) = sems
        self.zl, self.x, self.y = (lax.axis_index(a) for a in SEQ)
        self.other = {"zl": 1 - self.zl}

    @staticmethod
    def scratch(n):
        v, dma = pltpu.VMEM, pltpu.SemaphoreType.DMA
        return [
            v((n, ROWS, WIDE), BF16),
            v((n, ROWS, WIDE), BF16),
            v((n, 4, 4, 64, WIDE), BF16),
            v((n, 3, 4, 64, WIDE), BF16),
            v((n, 4, 64, WIDE), BF16),
            v((n, 3, 64, WIDE), BF16),
            *[dma((n,))] * 6,
        ]

    def fill(self, arrays):
        c = 0
        for ref in arrays:
            for k in range(ref.shape[1] // WIDE):
                self.r[c] = ref[:, k * WIDE : (k + 1) * WIDE]
                c += 1

    def right(self, c):
        return remote(
            self.r.at[c], self.rz.at[c], self.rz_send.at[c], self.rz_recv.at[c], self.other
        )

    def start(self):
        over(0, self.n, lambda c: self.right(c).start())

    def spread(self, c, phase, o):
        along_x = c % 2 == phase
        x_to = jnp.where(along_x, (self.x + o) % NX, self.x)
        y_to = jnp.where(along_x, self.y, (self.y + o) % NY)
        return {"x": x_to, "y": y_to}, jnp.where(along_x, x_to, y_to)

    def send_first(self, c, o):
        where, d = self.spread(c, 0, o)
        return remote(
            self.part.at[c, d], self.gx.at[c, o - 1], self.gx_send.at[c], self.gx_recv.at[c], where
        )

    def send_second(self, c, o):
        where, d = self.spread(c, 1, o)
        return remote(
            self.half.at[c, d], self.gy.at[c, o - 1], self.gy_send.at[c], self.gy_recv.at[c], where
        )

    def whole(self, got, send, recv, c):
        return remote(got.at[c], got.at[c], send.at[c], recv.at[c], self.other)

    def product(self, c):
        self.right(c).wait_recv()
        mine, theirs = self.r[c], self.rz[c]
        even = c % 2 == 0
        ends = [first for _, _, first in self.lefts[1:]] + [self.n]
        for (own, near, first), end in zip(self.lefts, ends):
            @pl.when((c >= first) & (c < end))
            def _():
                for i in range(NX):
                    a = own[pl.ds(pl.multiple_of(self.zl * OWN + i * 256, 256), 256), :]
                    b = near[pl.ds(i * 256, 256), :]
                    tile = (dot(a, mine) + dot(b, theirs)).astype(BF16)
                    for j in range(NY):
                        self.part[c, jnp.where(even, i, j), jnp.where(even, j, i)] = (
                            tile[j * 64 : (j + 1) * 64]
                        )
        for o in range(1, 4):
            self.send_first(c, o).start()

    def middle(self, c):
        self.whole(self.gx, self.gx_send, self.gx_recv, c).wait_recv()
        mine = jnp.where(c % 2 == 0, self.x, self.y)
        for j in range(4):
            total = self.part[c, mine, j].astype(F32)
            for o in range(3):
                total += self.gx[c, o, j].astype(F32)
            self.half[c, j] = total.astype(BF16)
        for o in range(1, 4):
            self.send_second(c, o).start()

    def last(self, c):
        self.whole(self.gy, self.gy_send, self.gy_recv, c).wait_recv()
        mine = jnp.where(c % 2 == 0, self.y, self.x)
        total = self.half[c, mine].astype(F32)
        for o in range(3):
            total += self.gy[c, o].astype(F32)
        self.out[:, pl.ds(pl.multiple_of(c * WIDE, WIDE), WIDE)] = total

    @property
    def steps(self):
        return self.n + 2 * LAG

    def step(self, i):
        @pl.when(i < self.n)
        def _():
            self.product(i)

        @pl.when((i >= LAG) & (i < self.n + LAG))
        def _():
            self.middle(i - LAG)

        @pl.when(i >= 2 * LAG)
        def _():
            self.last(i - 2 * LAG)

    def close(self):
        def sent(c):
            self.right(c).wait_send()
            self.whole(self.gx, self.gx_send, self.gx_recv, c).wait_send()
            self.whole(self.gy, self.gy_send, self.gy_recv, c).wait_send()

        over(0, self.n, sent)


class Left:
    def __init__(self, l_ref, lz, sems):
        zl, c = lax.axis_index("zl"), lax.axis_index("c")
        half = OWN // 2
        there = pl.ds(pl.multiple_of((1 - zl) * OWN + c * half, half), half)
        near, other = (pl.ds(pl.multiple_of(k * half, half), half) for k in (c, 1 - c))
        sem = [sems.at[k] for k in range(4)]
        self.out = remote(l_ref.at[there], lz.at[near], sem[0], sem[1], {"zl": 1 - zl})
        self.on = remote(lz.at[near], lz.at[near], sem[2], sem[3], {"c": 1 - c})
        self.back = remote(lz.at[other], lz.at[other], sem[2], sem[3], {"c": 1 - c})

    def start(self):
        self.out.start()

    def pass_on(self):
        self.out.wait_recv()
        self.on.start()

    def finish(self):
        self.back.wait_recv()

    def close(self):
        self.out.wait_send()
        self.on.wait_send()


HEAD_CHUNKS = 4


class HeadSum:
    def __init__(self, x, out, near, pair, far, sems):
        self.x, self.out, self.near, self.pair, self.far = x, out, near, pair, far
        self.near_send, self.near_recv, self.far_send, self.far_recv, self.end_send, self.end_recv = sems
        self.c, zh = lax.axis_index("c"), lax.axis_index("zh")
        self.sibling, self.opposite = {"c": 1 - self.c}, {"zh": 1 - zh}
        self.half = x.shape[0] // 2
        self.rows_each = self.half // HEAD_CHUNKS

    @staticmethod
    def scratch():
        v, dma = pltpu.VMEM, pltpu.SemaphoreType.DMA
        return [*[v((ROWS // 2, MODEL), BF16)] * 3, *[dma((HEAD_CHUNKS,))] * 6]

    def rows(self, core, k):
        return pl.ds(pl.multiple_of(core * self.half + k * self.rows_each, 16), self.rows_each)

    def local(self, k):
        return pl.ds(k * self.rows_each, self.rows_each)

    def first(self, k):
        return remote(
            self.x.at[self.rows(1 - self.c, k)], self.near.at[self.local(k)],
            self.near_send.at[k], self.near_recv.at[k], self.sibling,
        )

    def second(self, k):
        return remote(
            self.pair.at[self.local(k)], self.far.at[self.local(k)],
            self.far_send.at[k], self.far_recv.at[k], self.opposite,
        )

    def third(self, k, core):
        rows = self.rows(core, k)
        return remote(
            self.out.at[rows], self.out.at[rows], self.end_send.at[k], self.end_recv.at[k],
            self.sibling,
        )

    def start(self):
        for k in range(HEAD_CHUNKS):
            self.first(k).start()

    def across(self):
        for k in range(HEAD_CHUNKS):
            self.first(k).wait_recv()
            own = self.x[self.rows(self.c, k)].astype(F32)
            self.pair[self.local(k)] = (own + self.near[self.local(k)].astype(F32)).astype(BF16)
            self.second(k).start()

    def join(self):
        for k in range(HEAD_CHUNKS):
            self.second(k).wait_recv()
            total = self.pair[self.local(k)].astype(F32) + self.far[self.local(k)].astype(F32)
            self.out[self.rows(self.c, k)] = total.astype(BF16)
            self.third(k, self.c).start()

    def finish(self):
        for k in range(HEAD_CHUNKS):
            self.third(k, 1 - self.c).wait_recv()

    def close(self):
        for k in range(HEAD_CHUNKS):
            self.first(k).wait_send()
            self.second(k).wait_send()
            self.third(k, self.c).wait_send()


def head_sum_kernel(x_ref, out_ref, *scratch):
    total = HeadSum(x_ref, out_ref, *scratch[:3], scratch[3:])
    barrier = pltpu.get_barrier_semaphore()
    signal(barrier, total.sibling)
    signal(barrier, total.opposite)
    pl.semaphore_wait(barrier, 2)
    total.start()
    total.across()
    total.join()
    total.finish()
    total.close()


def head_sum(x, collective_id):
    return pl.pallas_call(
        head_sum_kernel,
        name=f"head_sum_{collective_id}",
        out_shape=jax.ShapeDtypeStruct(x.shape, BF16),
        in_specs=vmem(1),
        out_specs=vmem(1)[0],
        scratch_shapes=HeadSum.scratch(),
        compiler_params=params(collective_id),
    )(x)


EARLY = 6


def mixer_forward_kernel(
    q_ref, own_ref, edge_ref, x_ref, bc_ref, dt_ref, z_ref, seg_ref, segrow_ref, xtaps_ref,
    bctaps_ref, vec_ref, skip_ref, nt_ref, ct_ref,
    att_ref, lse_ref, kv_ref, edge_out, gated_ref, core_ref, xact_ref, bcact_ref, state_ref,
    ntz_ref, ctz_ref,
    m_ref, l_ref, acc_ref, xext, bcext, segx, local, msg, got, back, result, bias_ref, cb_ref,
    cumt_ref,
    send_sem, recv_sem, sib_send, sib_recv, edge_sem, scan_send, scan_recv, left_sem,
):
    me, c, zl = block_index(), lax.axis_index("c"), lax.axis_index("zl")
    at = me % PLANE
    sibling = {"c": 1 - c}
    barrier = pltpu.get_barrier_semaphore()
    over(1, BLOCKS, lambda o: signal(barrier, block_at((me + o) % BLOCKS)))
    signal(barrier, sibling)
    pl.semaphore_wait(barrier, BLOCKS)

    def block_copy(src, j, send, where):
        return remote(src, kv_ref.at[c, j], send_sem.at[send], recv_sem.at[j], where)

    def arrival(j):
        return block_copy(own_ref, j, 0, sibling)

    to_sibling = lambda j, src: remote(
        src, kv_ref.at[c, j], sib_send.at[j], sib_recv.at[j], sibling
    )
    from_sibling = lambda j: remote(
        kv_ref.at[1 - c, j], kv_ref.at[1 - c, j], sib_send.at[j], sib_recv.at[j], sibling
    )
    across = block_copy(own_ref, me, PLANE - 1, {"zl": 1 - zl})

    def own_copy(k, wait):
        d, where = plane_peer(k, 1)

        @pl.when(d > at)
        def _():
            copy = block_copy(own_ref, me, k, where)
            copy.wait_send() if wait else copy.start()

    def relay_copy(k, wait):
        copy = block_copy(kv_ref.at[c, at], at, PLANE + k, plane_peer(k, 1)[1])
        copy.wait_send() if wait else copy.start()

    edge_copy = remote(
        edge_ref, edge_out, edge_sem.at[0], edge_sem.at[1], block_at((me + 1) % BLOCKS)
    )
    states = Scan(False, me, msg, got, back, result, scan_send, scan_recv)

    @pl.when(me < BLOCKS - 1)
    def _():
        edge_copy.start()

    @pl.when(zl == 0)
    def _():
        across.start()

    to_sibling(me, own_ref).start()
    over(0, EARLY, lambda k: own_copy(k, False))
    lefts = [Left(ct_ref, ctz_ref, left_sem.at[0]), Left(nt_ref, ntz_ref, left_sem.at[1])]

    kv_ref[c, me] = own_ref[...]
    xext[8:, :] = x_ref[...].astype(F32)
    bcext[8:, :] = bc_ref[...].astype(F32)
    segx[8:, :] = seg_ref[...]
    lower = triangle()
    bias_ref[...] = mixing_bias(seg_ref, segrow_ref)

    @pl.when(me > 0)
    def _():
        edge_copy.wait_recv()

    @pl.when(me == 0)
    def _():
        edge_out[...] = jnp.zeros_like(edge_out)

    edge = edge_out[...].astype(F32)[8:]
    xext[:8, :] = edge[:, :INNER]
    bcext[:8, :] = edge[:, INNER : INNER + BC]
    segx[:8, :] = edge[:, INNER + BC :]

    def activate(ext, taps, out):
        def group(g):
            pre, _ = conv_group(ext, segx, seg_ref, taps, lane_block(g))
            out[:, lane_block(g)] = (pre * sigmoid(pre)).astype(BF16)

        over(0, out.shape[1] // 128, group)

    activate(bcext, bctaps_ref, bcact_ref)
    activate(xext, xtaps_ref, xact_ref)

    _, step, total, carry, entry, through = decays(dt_ref, vec_ref, seg_ref, segx, lower)
    cumt_ref[...] = jnp.transpose(total)
    weight = step * carry
    b_low, c_low = bcact_ref[:, :STATE], bcact_ref[:, STATE:]
    for g in range(GROUPS):
        moved = xact_ref[:, g * 128 : (g + 1) * 128].astype(F32) * widen(weight, g)
        local[g * 128 : (g + 1) * 128, :] = dot(moved.astype(BF16), b_low, 0, 0)
    scan_message(msg, local, through)
    states.start()
    over(EARLY, PLANE - 1, lambda k: own_copy(k, False))

    @pl.when(zl == 1)
    def _():
        arrival(at).wait_recv()
        to_sibling(at, kv_ref.at[c, at]).start()
        over(0, PLANE - 1, lambda k: relay_copy(k, False))

    cb_ref[...] = dot(c_low, b_low, 1, 1)
    low_lane = lax.broadcasted_iota(jnp.int32, (ROWS, 128), 1) < SSM_DIM
    for g in range(GROUPS):
        cols = slice(g * 128, (g + 1) * 128)
        u = (xact_ref[:, cols].astype(F32) * widen(step, g)).astype(BF16)
        made = []
        for h in (2 * g, 2 * g + 1):
            gap = total[:, h : h + 1] - cumt_ref[h : h + 1, :] + bias_ref[...]
            made.append(dot((jnp.exp2(gap) * cb_ref[...]).astype(BF16), u))
        core_ref[:, cols] = jnp.where(low_lane, made[0], made[1])

    scale = LOG2E * HEAD_DIM**-0.5
    queries = q_ref[...]
    qseg = segrow_ref[0:1, :]

    def scores_of(j):
        s = dot(kv_ref[0, j, :ROWS], queries, 1, 1) * scale
        return jnp.where(key_segments(kv_ref[0, j, ROWS:]) == qseg, s, MASKED)

    from_sibling(me).wait_recv()
    s = causal_mask(scores_of(me))
    m = jnp.max(s, 0, keepdims=True)
    p = jnp.exp2(s - m)
    m_ref[...] = m
    l_ref[...] = jnp.sum(p, 0, keepdims=True)
    acc_ref[...] = dot(kv_ref[1, me, :ROWS], p.astype(BF16), 0, 0)

    states.turn()
    for left in lefts:
        left.start()

    def forward(k):
        q, _ = plane_peer(k, -1)

        def one(j):
            arrival(j).wait_recv()
            to_sibling(j, kv_ref.at[c, j]).start()

        pl.when(q < at)(lambda: one(zl * PLANE + q))
        pl.when(zl == 1)(lambda: one(q))

    def attend(j):
        from_sibling(j).wait_recv()
        s = scores_of(j)
        m_old = m_ref[...]
        m = jnp.maximum(m_old, jnp.max(s, 0, keepdims=True))
        p = jnp.exp2(s - m)
        alpha = jnp.exp2(m_old - m)
        m_ref[...] = m
        l_ref[...] = l_ref[...] * alpha + jnp.sum(p, 0, keepdims=True)
        acc_ref[...] = acc_ref[...] * alpha + dot(kv_ref[1, j, :ROWS], p.astype(BF16), 0, 0)

    forward(0)

    @pl.when(zl == 1)
    def _():
        attend(at)

    def step_over(k):
        @pl.when(k + 1 < PLANE - 1)
        def _():
            forward(k + 1)

        q, _ = plane_peer(k, -1)
        pl.when(q < at)(lambda: attend(zl * PLANE + q))
        pl.when(zl == 1)(lambda: attend(q))

    over(0, PLANE - 1, step_over)
    for left in lefts:
        left.pass_on()
    att_ref[...] = jnp.transpose(acc_ref[...] / l_ref[...])
    lse_ref[...] = jnp.broadcast_to(m_ref[...] + jnp.log2(l_ref[...]), lse_ref.shape)

    states.finish(state_ref)
    for g in range(GROUPS):
        cols = slice(g * 128, (g + 1) * 128)
        outer = dot(c_low, state_ref[cols, :].astype(BF16), 1, 1) * widen(entry, g)
        core = core_ref[:, cols] + outer
        core_ref[:, cols] = core
        out = core + skip_ref[0:1, cols] * xact_ref[:, cols].astype(F32)
        z = z_ref[:, cols]
        gated_ref[:, cols] = (out * z * sigmoid(z)).astype(BF16)

    states.close()
    for left in lefts:
        left.finish()
        left.close()
    to_sibling(me, own_ref).wait_send()
    over(0, PLANE - 1, lambda k: own_copy(k, True))

    @pl.when(zl == 0)
    def _():
        across.wait_send()

    @pl.when(zl == 1)
    def _():
        over(0, PLANE - 1, lambda k: relay_copy(k, True))
        over(0, PLANE, lambda j: to_sibling(j, own_ref).wait_send())

    over(0, at, lambda q: to_sibling(zl * PLANE + q, own_ref).wait_send())

    @pl.when(me < BLOCKS - 1)
    def _():
        edge_copy.wait_send()


def mixer_forward(*args):
    wide = 2 * ROWS
    s = jax.ShapeDtypeStruct
    dma = pltpu.SemaphoreType.DMA
    return pl.pallas_call(
        mixer_forward_kernel,
        name="mixer_forward",
        out_shape=(
            s((wide, HEAD_DIM), F32),
            s((8, wide), F32),
            s((2, BLOCKS, ROWS + 16, HEAD_DIM), BF16),
            s((16, EDGE_WIDE), BF16),
            s((ROWS, INNER), BF16),
            s((ROWS, INNER), F32),
            s((ROWS, INNER), BF16),
            s((ROWS, BC), BF16),
            s((INNER, STATE), F32),
            s((OWN, ROWS), BF16),
            s((OWN, ROWS), BF16),
        ),
        in_specs=vmem(len(args)),
        out_specs=tuple(vmem(11)),
        scratch_shapes=[
            pltpu.VMEM((1, wide), F32),
            pltpu.VMEM((1, wide), F32),
            pltpu.VMEM((HEAD_DIM, wide), F32),
            pltpu.VMEM((ROWS + 8, INNER), F32),
            pltpu.VMEM((ROWS + 8, BC), F32),
            pltpu.VMEM((ROWS + 8, 128), F32),
            pltpu.VMEM((INNER, STATE), F32),
            *[pltpu.VMEM((BLOCKS, SCAN_ROWS + 8, STATE), BF16)] * 4,
            pltpu.VMEM((ROWS, ROWS), F32),
            pltpu.VMEM((ROWS, ROWS), F32),
            pltpu.VMEM((128, ROWS), F32),
            *[dma((BLOCKS,))] * 4,
            dma((2,)),
            dma((2, BLOCKS)),
            dma((2, BLOCKS)),
            dma((2, 4)),
        ],
        compiler_params=params(1),
    )(*args)


def mixer_backward_kernel(
    q_ref, do_ref, att_ref, lse_ref, segrow_ref, kv_ref, gg_ref, z_ref, core_ref, xact_ref,
    bcact_ref, x_ref, bcown_ref, edge_in, dt_ref, state_ref, seg_ref, xtaps_ref, bctaps_ref,
    vec_ref, skip_ref, dgate_ref, dup_ref, hidden_ref, ft_ref, ct_ref, ctz_ref, mt_ref,
    dq_ref, dkv_ref, dz_ref, dx_ref, dbc_ref, ddt_ref, dxtaps_ref, dbctaps_ref, dvec_ref,
    w_ref, mtz_ref,
    dqt_ref, mine, theirs, sib, kvgot, relay_ref, total_ref, xext, bcext, segx, local, msg, got, back, result,
    bias_ref, cb_ref, cumt_ref, g_ref, du_ref, dbc_all, shares, share_got, edge_ref,
    edge_out, enter_ref, gext, dcum_ref, ddtx_ref,
    send_sem, recv_sem, sib_send, sib_recv, edge_sem, scan_send, scan_recv, share_send, share_recv,
    ftz_ref, left_sem, *reduce,
):
    me, c, zh, zl = block_index(), *(lax.axis_index(a) for a in ("c", "zh", "zl"))
    head_at = zh * 2 + c
    sibling = {"c": 1 - c}
    at_head = lambda d: {"zh": d // 2, "c": d % 2}
    barrier = pltpu.get_barrier_semaphore()
    over(1, BLOCKS, lambda o: signal(barrier, block_at((me + o) % BLOCKS)))
    for o in range(1, 4):
        signal(barrier, at_head((head_at + o) % 4))
    pl.semaphore_wait(barrier, BLOCKS + 2)

    at = me % PLANE
    to_sibling = lambda j: remote(
        theirs.at[j], sib.at[j], sib_send.at[j], sib_recv.at[j], sibling
    )

    def to_owner(k, kind):
        q, where = plane_peer(k, -1)
        j = q if kind else zl * PLANE + q
        return remote(
            mine.at[j], kvgot.at[kind, at], send_sem.at[kind, k], recv_sem.at[kind, at], where
        )

    def from_plane(kind, q):
        return remote(
            kvgot.at[kind, q], kvgot.at[kind, q], send_sem.at[kind, 0], recv_sem.at[kind, q],
            sibling,
        )

    across = remote(
        relay_ref, kvgot.at[1, 0], send_sem.at[0, PLANE - 1], recv_sem.at[1, 0], {"zl": 1 - zl}
    )
    states = Scan(True, me, msg, got, back, result, scan_send, scan_recv)
    rs = Reduce(
        [(ft_ref, ftz_ref, 0), (ct_ref, ctz_ref, 8)], 12, *reduce[:6], w_ref, reduce[6:]
    )
    lefts = [Left(ft_ref, ftz_ref, left_sem.at[0]), Left(mt_ref, mtz_ref, left_sem.at[1])]
    rs.fill([dgate_ref, dup_ref, hidden_ref])

    lower = triangle()
    edge = edge_in[...].astype(F32)[8:]
    xext[:8, :] = edge[:, :INNER]
    segx[:8, :] = edge[:, INNER + BC :]
    xext[8:, :] = x_ref[...].astype(F32)
    segx[8:, :] = seg_ref[...]
    bcext[...] = bcown_ref[...].astype(F32)[8:]
    bias_ref[...] = mixing_bias(seg_ref, segrow_ref)
    pre_dt, step, total, carry, entry, through = decays(dt_ref, vec_ref, seg_ref, segx, lower)
    cumt_ref[...] = jnp.transpose(total)
    b_low, c_low = bcact_ref[:, :STATE], bcact_ref[:, STATE:]
    dcum = jnp.zeros((ROWS, 128), F32)
    dskip = jnp.zeros((8, 128), F32)
    dc = jnp.zeros((ROWS, STATE), F32)
    for g in range(GROUPS):
        cols = slice(g * 128, (g + 1) * 128)
        z, core, x = z_ref[:, cols], core_ref[:, cols], xact_ref[:, cols].astype(F32)
        sig = sigmoid(z)
        gg = gg_ref[:, cols]
        out = core + skip_ref[0:1, cols] * x
        dz_ref[:, cols] = (gg * out * sig * (1.0 + z * (1.0 - sig))).astype(BF16)
        grad = gg * z * sig
        g_ref[:, cols] = grad
        dcum += per_head(grad * core, g)
        dskip += per_head(jnp.broadcast_to(jnp.sum(grad * x, 0, keepdims=True), (8, 128)), g)
        entered = (grad * widen(entry, g)).astype(BF16)
        local[cols, :] = dot(entered, c_low, 0, 0)
        dc += dot(entered, state_ref[cols, :].astype(BF16))
    scan_message(msg, local, through)
    states.start()
    lefts[0].start()
    rs.start()
    lefts[1].start()
    dbc_all[:, STATE:] = dc

    cb_ref[...] = dot(c_low, b_low, 1, 1)
    low_lane = lax.broadcasted_iota(jnp.int32, (ROWS, 128), 1) < SSM_DIM
    dcb = jnp.zeros((ROWS, ROWS), F32)
    for g in range(GROUPS):
        cols = slice(g * 128, (g + 1) * 128)
        u = xact_ref[:, cols].astype(F32) * widen(step, g)
        u_low, grad = u.astype(BF16), g_ref[:, cols]
        grad_low = grad.astype(BF16)
        made = []
        for i in range(2):
            h = 2 * g + i
            decay = jnp.exp2(total[:, h : h + 1] - cumt_ref[h : h + 1, :] + bias_ref[...])
            mixing = (decay * cb_ref[...]).astype(BF16)
            made.append(dot(mixing, grad_low, 0, 0))
            half = jnp.where(low_lane if i == 0 else ~low_lane, grad, 0.0).astype(BF16)
            dcb += decay * dot(half, u_low, 1, 1)
        du = jnp.where(low_lane, made[0], made[1])
        du_ref[:, cols] = du
        dcum -= per_head(u * du, g)
    dcum_ref[...] = dcum
    dcb_low = dcb.astype(BF16)
    dbc_all[:, :STATE] = dot(dcb_low, c_low, 0, 0)
    dbc_all[:, STATE:] += dot(dcb_low, b_low)

    scale = LOG2E * HEAD_DIM**-0.5
    queries, grads = q_ref[...], do_ref[...]
    lse, qseg = lse_ref[0:1, :], segrow_ref[0:1, :]
    high, low = two_parts(grads.astype(F32) * att_ref[...])
    ones = jnp.ones((8, HEAD_DIM), BF16)
    delta = (dot(ones, high, 1, 1) + dot(ones, low, 1, 1))[0:1, :]

    def block(t, own):
        keys = kv_ref[0, t, :ROWS]
        s = dot(keys, queries, 1, 1) * scale
        s = jnp.where(key_segments(kv_ref[0, t, ROWS:]) == qseg, s, MASKED)
        if own:
            s = causal_mask(s)
        p = jnp.exp2(s - lse)
        ds = (p * (dot(kv_ref[1, t, :ROWS], grads, 1, 1) - delta)).astype(BF16)
        dk = dot(ds, queries)
        dv = dot(p.astype(BF16), grads)
        change = dot(keys, ds, 0, 0)
        dqt_ref[...] = change if own else dqt_ref[...] + change
        mine[t] = jnp.where(c == 0, dk, dv).astype(BF16)
        theirs[t] = jnp.where(c == 0, dv, dk).astype(BF16)
        to_sibling(t).start()

    def pair(t):
        to_sibling(t).wait_recv()
        return mine[t].astype(F32) + sib[t].astype(F32)

    block(me, True)
    lefts[0].pass_on()
    states.turn()
    lefts[0].finish()

    @pl.when(zl == 1)
    def _():
        block(at, False)

    def give(k):
        q, _ = plane_peer(k, -1)

        @pl.when(q < at)
        def _():
            j = zl * PLANE + q
            mine[j] = pair(j).astype(BF16)
            to_owner(k, 0).start()

        @pl.when(zl == 1)
        def _():
            mine[q] = pair(q).astype(BF16)
            to_owner(k, 1).start()

    def step_over(k):
        q, _ = plane_peer(k, -1)
        pl.when(q < at)(lambda: block(zl * PLANE + q, False))
        pl.when(zl == 1)(lambda: block(q, False))

        @pl.when(k >= 1)
        def _():
            give(k - 1)

        rs.step(k)

    over(0, PLANE - 1, step_over)
    give(PLANE - 2)
    over(PLANE - 1, rs.steps, rs.step)
    lefts[1].pass_on()
    dkv_ref[...] = pair(me)

    @pl.when(zl == 1)
    def _():
        total_ref[...] = pair(at)

    dq_ref[...] = jnp.transpose(dqt_ref[...])

    states.finish(enter_ref)
    dcum = dcum_ref[...]
    dstep = jnp.zeros((ROWS, 128), F32)
    dlast = jnp.zeros((8, 128), F32)
    db = jnp.zeros((ROWS, STATE), F32)
    for g in range(GROUPS):
        cols = slice(g * 128, (g + 1) * 128)
        entering = enter_ref[cols, :]
        entering_low = entering.astype(BF16)
        x = xact_ref[:, cols].astype(F32)
        steps, carries = widen(step, g), widen(carry, g)
        v = x * steps * carries
        dv = dot(b_low, entering_low, 1, 1)
        db += dot(v.astype(BF16), entering_low)
        dcarry = per_head(v * dv, g)
        dcum -= dcarry
        dlast += jnp.broadcast_to(jnp.sum(dcarry, 0, keepdims=True), (8, 128))
        du = du_ref[:, cols] + carries * dv
        dstep += per_head(x * du, g)
        pieces = jnp.sum(entering * state_ref[cols, :], 1, keepdims=True)
        both = jnp.sum(jnp.broadcast_to(pieces, (128, 128)) * head_of_lane_f32(g), 0, keepdims=True)
        dlast += through * both
        g_ref[:, cols] = steps * du + skip_ref[0:1, cols] * g_ref[:, cols]
    dbc_all[:, :STATE] += db
    last_row = lax.broadcasted_iota(jnp.int32, (ROWS, 128), 0) == ROWS - 1
    dcum += jnp.where(last_row, dlast[0:1, :], 0.0)
    da = running(dcum, lower, 0)
    rate = vec_ref[1:2, :]
    drate = -jnp.sum(step * da, 0, keepdims=True)
    ddt = (dstep - rate * da) * sigmoid(pre_dt)
    ddt_ref[...] = ddt.astype(BF16)
    dbias = jnp.sum(ddt, 0, keepdims=True)
    dvec_ref[...] = jnp.concatenate([dbias, drate, dskip[0:1, :], jnp.zeros((5, 128), F32)], 0)

    for d in range(4):
        shares[d] = dbc_all[:, d * 128 : (d + 1) * 128].astype(BF16)
    share = lambda o: remote(
        shares.at[(head_at + o) % 4], share_got.at[o], share_send.at[o], share_recv.at[o],
        at_head((head_at + o) % 4),
    )
    for o in range(1, 4):
        share(o).start()

    def conv_back(ext, taps, grad, cols, out_taps, out_grad):
        pre, inputs = conv_group(ext, segx, seg_ref, taps, cols)
        sig = sigmoid(pre)
        dpre = grad * sig * (1.0 + pre * (1.0 - sig))
        gext[...] = jnp.zeros_like(gext)
        rows = []
        for k in range(CONV):
            rows.append(jnp.sum(dpre * inputs[k], 0, keepdims=True))
            same = segx[pl.ds(5 + k, ROWS), :] == seg_ref[...]
            gext[pl.ds(5 + k, ROWS), :] += jnp.where(same, taps[k : k + 1, cols] * dpre, 0.0)
        out_taps[:, cols] = jnp.concatenate([*rows, jnp.zeros((4, 128), F32)], 0)
        out_grad[...] = gext[...]

    def x_group(g):
        cols = lane_block(g)
        conv_back(xext, xtaps_ref, g_ref[:, cols], cols, dxtaps_ref, ddtx_ref)
        edge_ref[:, cols] = ddtx_ref[:8, :]
        g_ref[:, cols] = ddtx_ref[8:, :]

    over(0, GROUPS, x_group)
    grad_bc = shares[head_at].astype(F32)
    for o in range(1, 4):
        share(o).wait_recv()
        grad_bc += share_got[o].astype(F32)
    conv_back(bcext, bctaps_ref, grad_bc, slice(0, 128), dbctaps_ref, ddtx_ref)
    edge_ref[:, INNER:] = ddtx_ref[:8, :]
    edge_copy = remote(
        edge_ref, edge_out, edge_sem.at[0], edge_sem.at[1], block_at((me + BLOCKS - 1) % BLOCKS)
    )

    @pl.when(me > 0)
    def _():
        edge_copy.start()

    def collect(q):
        @pl.when((zl == 1) & (q != at))
        def _():
            from_plane(1, q).wait_recv()
            total_ref[...] += kvgot[1, q].astype(F32)

    over(0, PLANE, collect)

    @pl.when(zl == 1)
    def _():
        relay_ref[...] = total_ref[...].astype(BF16)
        across.start()

    def collect_own(q):
        from_plane(0, q).wait_recv()
        dkv_ref[...] += kvgot[0, q].astype(F32)

    over(at + 1, PLANE, collect_own)

    @pl.when(zl == 0)
    def _():
        from_plane(1, 0).wait_recv()
        dkv_ref[...] += kvgot[1, 0].astype(F32)

    @pl.when(me < BLOCKS - 1)
    def _():
        edge_copy.wait_recv()

    @pl.when(me == BLOCKS - 1)
    def _():
        edge_out[...] = jnp.zeros_like(edge_out)

    tail = pl.ds(ROWS - 8, 8)
    g_ref[tail, :] += edge_out[:, :INNER]
    ddtx_ref[pl.ds(ROWS, 8), :] += edge_out[:, INNER:]
    dx_ref[...] = g_ref[...].astype(BF16)
    dbc_ref[...] = ddtx_ref[8:, :].astype(BF16)

    @pl.when(me > 0)
    def _():
        edge_copy.wait_send()

    states.close()
    rs.close()
    lefts[0].close()
    lefts[1].finish()
    lefts[1].close()
    for o in range(1, 4):
        share(o).wait_send()
    to_sibling(me).wait_send()

    def given(k):
        q, _ = plane_peer(k, -1)

        @pl.when(q < at)
        def _():
            to_sibling(zl * PLANE + q).wait_send()
            to_owner(k, 0).wait_send()

        @pl.when(zl == 1)
        def _():
            to_sibling(q).wait_send()
            to_owner(k, 1).wait_send()

    over(0, PLANE - 1, given)

    @pl.when(zl == 1)
    def _():
        to_sibling(at).wait_send()
        across.wait_send()


def head_of_lane_f32(g):
    row = lax.broadcasted_iota(jnp.int32, (128, 128), 0)
    lane = lax.broadcasted_iota(jnp.int32, (128, 128), 1)
    return (lane == 2 * g + (row >= SSM_DIM).astype(jnp.int32)).astype(F32)


def mixer_backward(*args):
    wide = 2 * ROWS
    s = jax.ShapeDtypeStruct
    dma = pltpu.SemaphoreType.DMA
    v = pltpu.VMEM
    piece = (BLOCKS, ROWS, HEAD_DIM)
    return pl.pallas_call(
        mixer_backward_kernel,
        name="mixer_backward",
        out_shape=(
            s((wide, HEAD_DIM), F32),
            s((ROWS, HEAD_DIM), F32),
            s((ROWS, INNER), BF16),
            s((ROWS, INNER), BF16),
            s((ROWS, 128), BF16),
            s((ROWS, 128), BF16),
            s((8, INNER), F32),
            s((8, 128), F32),
            s((8, 128), F32),
            s((64, 12 * WIDE), F32),
            s((OWN, ROWS), BF16),
        ),
        in_specs=vmem(len(args)),
        out_specs=tuple(vmem(11)),
        scratch_shapes=[
            v((HEAD_DIM, wide), F32),
            *[v(piece, BF16)] * 3,
            v((2, PLANE, ROWS, HEAD_DIM), BF16),
            v((ROWS, HEAD_DIM), BF16),
            v((ROWS, HEAD_DIM), F32),
            v((ROWS + 8, INNER), F32),
            v((ROWS + 8, 128), F32),
            v((ROWS + 8, 128), F32),
            v((INNER, STATE), F32),
            *[v((BLOCKS, SCAN_ROWS + 8, STATE), BF16)] * 4,
            v((ROWS, ROWS), F32),
            v((ROWS, ROWS), F32),
            v((128, ROWS), F32),
            v((ROWS, INNER), F32),
            v((ROWS, INNER), F32),
            v((ROWS, BC), F32),
            v((4, ROWS, 128), BF16),
            v((4, ROWS, 128), BF16),
            v((8, GRAD_EDGE), F32),
            v((8, GRAD_EDGE), F32),
            v((INNER, STATE), F32),
            v((ROWS + 8, 128), F32),
            v((ROWS, 128), F32),
            v((ROWS + 8, 128), F32),
            dma((2, PLANE)),
            dma((2, PLANE)),
            dma((BLOCKS,)),
            dma((BLOCKS,)),
            dma((2,)),
            dma((2, BLOCKS)),
            dma((2, BLOCKS)),
            dma((4,)),
            dma((4,)),
            v((OWN, ROWS), BF16),
            dma((2, 4)),
            *Reduce.scratch(12),
        ],
        compiler_params=params(2),
    )(*args)


SMALL = 8 * 128
SMALL_AT = 5
CHUNKS = 13
GATHER_FROM = CHUNKS


def finish_kernel(
    misc_ref, dx_ref, dz_ref, dq_ref, ddt_ref, gated_ref, att_ref, nt_ref, ntz_ref, mt_ref,
    mtz_ref, back_ref, ffn_ref, tok_ref, gain_ref, ghid_ref, hid_ref, small_ref,
    out_ref, dtok_ref, w_ref, all_ref, alls_ref,
    own_small, back_sum, ffn_sum, mine, esum, egot, e_send, e_recv, z_send, z_recv, w_send, w_recv, sib_send, sib_recv,
    s_send, s_recv, t_send, t_recv, part_ref, *rest,
):
    me, c, zh = block_index(), lax.axis_index("c"), lax.axis_index("zh")
    chip = zh * BLOCKS + me
    sibling = {"c": 1 - c}

    def chip_at(p):
        return {"zh": p // BLOCKS, **block_at(p % BLOCKS)}

    n_rs = len(Reduce.scratch(CHUNKS))
    rs = Reduce(
        [(nt_ref, ntz_ref, 0), (mt_ref, mtz_ref, 9)], CHUNKS, *rest[:6], w_ref, rest[6:n_rs]
    )
    rest = rest[n_rs:]
    n_sum = len(HeadSum.scratch())
    back = HeadSum(back_ref, back_sum, *rest[:3], rest[3:n_sum])
    rest = rest[n_sum:]
    ffn = HeadSum(ffn_ref, ffn_sum, *rest[:3], rest[3:])

    barrier = pltpu.get_barrier_semaphore()
    over(1, CHIPS, lambda o: signal(barrier, chip_at((chip + o) % CHIPS)))
    signal(barrier, sibling)
    pl.semaphore_wait(barrier, CHIPS)

    back.start()
    rs.fill([misc_ref, dx_ref, dz_ref, dq_ref, ddt_ref, gated_ref, att_ref])
    rs.right(0).start()
    back.across()
    over(1, CHUNKS, lambda k: rs.right(k).start())
    ffn.start()

    at, level = me % PLANE, zh * NZ + lax.axis_index("zl")

    def along_z(o):
        d = (level + o) % 4
        where = {"zh": d // NZ, "zl": d % NZ}
        return remote(mine, all_ref.at[c, at, level], z_send.at[o], z_recv.at[o], where)

    def column(k):
        return remote(
            all_ref.at[c, at], all_ref.at[c, at], w_send.at[k], w_recv.at[at], plane_peer(k, 1)[1]
        )

    def to_sibling(q, core):
        return remote(
            all_ref.at[core, q], all_ref.at[core, q], sib_send.at[q], sib_recv.at[q], sibling
        )

    def pass_on(k):
        q, where = plane_peer(k, -1)
        remote(
            all_ref.at[c, q], all_ref.at[c, q], w_send.at[k], w_recv.at[q], where
        ).wait_recv()
        to_sibling(q, c).start()

    def columns_out():
        for o in range(1, 4):
            along_z(o).wait_recv()
        over(0, PLANE - 1, lambda k: column(k).start())
        to_sibling(at, c).start()

    def share(d):
        return remote(own_small.at[d], egot.at[me], e_send.at[d], e_recv.at[me], block_at(d))

    def shared(s):
        return remote(egot.at[s], egot.at[s], e_send.at[0], e_recv.at[s], block_at(s))

    def small_spread(o):
        d = (chip + o) % CHIPS
        slot = zh * SMALL_AT + me
        return remote(esum, alls_ref.at[c, slot], s_send.at[o], s_recv.at[slot], chip_at(d))

    def small_sibling(slot, core):
        return remote(
            alls_ref.at[core, slot], alls_ref.at[core, slot], t_send.at[slot], t_recv.at[slot],
            sibling,
        )

    def gradient():
        for r in range(0, ROWS, 32):
            rows = pl.ds(r, 32)
            x = tok_ref[rows, :].astype(F32)
            scale = lax.rsqrt(jnp.mean(x * x, 1, keepdims=True) + EPSILON)
            n = x * scale
            grad = back_sum[rows, :].astype(F32)
            scaled = grad * gain_ref[0:1, :]
            along = jnp.mean(n * scaled, 1, keepdims=True)
            dtok_ref[rows, :] = ghid_ref[rows, :] + scale * (scaled - n * along)
            gains = jnp.sum(grad * n, 0, keepdims=True)
            for k in range(MODEL // 128):
                piece = gains[:, k * 128 : (k + 1) * 128]
                part_ref[k : k + 1, :] = piece if r == 0 else part_ref[k : k + 1, :] + piece
        quarter = MODEL // 4 // 128
        own_small[...] = small_ref[...]
        own_small[0, :quarter] = part_ref[pl.ds((zh * 2 + c) * quarter, quarter), :]

        def give(d):
            @pl.when(d != me)
            def _():
                share(d).start()

        over(0, SMALL_AT, give)

    def small_sums():
        @pl.when(me < SMALL_AT)
        def _():
            egot[me] = own_small[me]

            def take(s):
                @pl.when(s != me)
                def _():
                    shared(s).wait_recv()

            over(0, BLOCKS, take)
            total = lax.fori_loop(0, BLOCKS, lambda s, t: t + egot[s], jnp.zeros((8, 128), F32))
            esum[...] = jnp.concatenate([total, jnp.zeros_like(total)], 0).astype(BF16)
            slot = zh * SMALL_AT + me
            alls_ref[c, slot] = esum[...]
            over(1, CHIPS, lambda o: small_spread(o).start())
            small_sibling(slot, c).start()

    def small_pass():
        def one(slot):
            @pl.when(slot != zh * SMALL_AT + me + jnp.where(me < SMALL_AT, 0, CHIPS))
            def _():
                remote(
                    esum, alls_ref.at[c, slot], s_send.at[0], s_recv.at[slot], sibling
                ).wait_recv()
                small_sibling(slot, c).start()

        over(0, 2 * SMALL_AT, one)

    def weights_out():
        mine[...] = w_ref[:, :WIDE].astype(BF16)
        all_ref[c, at, level] = mine[...]
        for o in range(1, 4):
            along_z(o).start()

    batch, first_pass = 3, rs.steps - 5

    def step(i):
        rs.step(i)

        @pl.when(i == 2)
        def _():
            ffn.across()

        @pl.when(i == 4)
        def _():
            back.join()

        @pl.when(i == 2 * LAG)
        def _():
            weights_out()
            back.finish()
            gradient()

        @pl.when(i == 9)
        def _():
            columns_out()
            ffn.join()

        @pl.when(i == 11)
        def _():
            small_sums()

        @pl.when(i == 12)
        def _():
            ffn.finish()
            out_ref[...] = (hid_ref[...] + ffn_sum[...].astype(F32)).astype(BF16)

        @pl.when(i >= first_pass)
        def _():
            k = i - first_pass
            over(k * batch, (k + 1) * batch, pass_on)

    over(0, rs.steps, step)
    small_pass()

    over(0, PLANE, lambda q: to_sibling(q, 1 - c).wait_recv())
    over(0, 2 * SMALL_AT, lambda s: small_sibling(s, 1 - c).wait_recv())
    rs.close()
    back.close()
    ffn.close()
    over(0, PLANE, lambda q: to_sibling(q, c).wait_send())
    over(0, 2 * SMALL_AT, lambda s: small_sibling(s, c).wait_send())
    over(0, PLANE - 1, lambda k: column(k).wait_send())
    for o in range(1, 4):
        along_z(o).wait_send()

    @pl.when(me < SMALL_AT)
    def _():
        over(1, CHIPS, lambda o: small_spread(o).wait_send())

    def given(d):
        @pl.when(d != me)
        def _():
            share(d).wait_send()

    over(0, SMALL_AT, given)


def finish(*args):
    s = jax.ShapeDtypeStruct
    v, dma = pltpu.VMEM, pltpu.SemaphoreType.DMA
    return pl.pallas_call(
        finish_kernel,
        name="finish",
        out_shape=(
            s((ROWS, MODEL), BF16),
            s((ROWS, MODEL), F32),
            s((64, CHUNKS * WIDE), F32),
            s((2, PLANE, 4, 64, WIDE), BF16),
            s((2, 2 * SMALL_AT, 16, 128), BF16),
        ),
        in_specs=vmem(len(args)),
        out_specs=tuple(vmem(5)),
        scratch_shapes=[
            v((SMALL_AT, 8, 128), F32),
            v((ROWS, MODEL), BF16),
            v((ROWS, MODEL), BF16),
            v((64, WIDE), BF16),
            v((16, 128), BF16),
            v((BLOCKS, 8, 128), F32),
            dma((SMALL_AT,)), dma((BLOCKS,)),
            dma((4,)), dma((4,)),
            *[dma((PLANE,))] * 4,
            dma((CHIPS,)), dma((2 * SMALL_AT,)),
            dma((2 * SMALL_AT,)), dma((2 * SMALL_AT,)),
            v((16, 128), F32),
            *Reduce.scratch(CHUNKS),
            *HeadSum.scratch(),
            *HeadSum.scratch(),
        ],
        compiler_params=params(3),
    )(*args)


def format_kernel(all_ref, bc_ref, kv_ref):
    for c in range(2):
        for p in range(all_ref.shape[1]):
            for zh in range(2):
                rows = slice(p * 64, (p + 1) * 64)
                at, turned = (zh * 2 + c) * 128, (c * 2 + zh) * 128
                bc_ref[rows, at : at + 128] = all_ref[c, p, zh, 0, :, :128].astype(F32)
                kv_ref[rows, turned : turned + 128] = all_ref[c, p, zh, 0, :, 128:].astype(F32)


def format_replicated(gathered):
    step = 8
    steps = PLANE // step
    block = pl.BlockSpec((64 * step, 512), lambda i: (i, 0))
    return pl.pallas_call(
        format_kernel,
        name="format_replicated",
        out_shape=(jax.ShapeDtypeStruct((MODEL, 512), F32),) * 2,
        grid=(NZ * steps,),
        in_specs=[
            pl.BlockSpec(
                (2, step, 2, 1, 64, WIDE), lambda i: (0, i % steps, 0, i // steps, 0, 0)
            )
        ],
        out_specs=(block, block),
    )(gathered.reshape(2, PLANE, 2, NZ, 64, WIDE))


def rms_norm(values, scales):
    return values * lax.rsqrt(jnp.mean(values * values, -1, keepdims=True) + EPSILON) * scales


def rope_turn(values, cosine, sine):
    half = values.shape[-1] // 2
    first, second = values[..., :half], values[..., half:]
    return jnp.concatenate([first * cosine - second * sine, second * cosine + first * sine], -1)


def on_device(
    tokens, segment_ids, cotangent, norm1_gain, x_weight, z_weight, bc_weight, dt_weight,
    x_conv, bc_conv, dt_bias, decay_rate, skip_gain, out_weight, query_weight, kv_weight,
    attn_weight, norm2_gain, gate_weight, up_weight, down_weight,
):
    zh, c = lax.axis_index("zh"), lax.axis_index("c")
    head_index = zh * 2 + c
    heads = decay_rate.shape[0]
    inner = x_weight.shape[1]
    q_heads = query_weight.shape[1] // HEAD_DIM
    positions = block_index() * ROWS + jnp.arange(ROWS)
    half_dim = HEAD_DIM // 2
    frequency = ROPE_BASE ** (-(jnp.arange(half_dim).astype(F32) * 2.0 / HEAD_DIM))
    angles = positions.astype(F32)[:, None] * frequency[None, :]
    cosine, sine = jnp.cos(angles), jnp.sin(angles)

    x_input = tokens.astype(F32)
    normed_f, norm_back = jax.vjp(rms_norm, x_input, norm1_gain)
    normed = normed_f.astype(BF16)
    kv_at = c * (KVHEADS * HEAD_DIM) + zh * HEAD_DIM
    kv_columns = lax.dynamic_slice_in_dim(kv_weight, kv_at, HEAD_DIM, 1)
    kv_raw = dot(normed, kv_columns)
    kv_own = jnp.where(c == 0, rope_turn(kv_raw, cosine, sine), kv_raw).astype(BF16)
    query_raw = dot(normed, query_weight).reshape(ROWS, q_heads, HEAD_DIM)
    queries = rope_turn(query_raw, cosine[:, None, :], sine[:, None, :]).astype(BF16)
    queries = queries.transpose(1, 0, 2).reshape(q_heads * ROWS, HEAD_DIM)
    x_pre = dot(normed, x_weight).astype(BF16)
    bc_pre = dot(normed, bc_weight).astype(BF16)
    z_val = dot(normed, z_weight)
    dt_wide = jnp.pad(dt_weight, ((0, 0), (0, 128 - heads)))
    dt_raw = dot(normed, dt_wide)

    seg_low = segment_ids.astype(BF16)
    own_block = jnp.concatenate(
        [kv_own, jnp.pad(seg_low.reshape(2, HEAD_DIM), ((0, 14), (0, 0)))], 0
    )
    seg = segment_ids.astype(F32)
    seg_row = jnp.broadcast_to(jnp.tile(seg, q_heads), (8, q_heads * ROWS))
    seg_column = jnp.broadcast_to(seg[:, None], (ROWS, 128))
    edge = jnp.concatenate(
        [x_pre[-16:], bc_pre[-16:], jnp.broadcast_to(seg_low[-16:, None], (16, 128))], 1
    )
    vectors = jnp.pad(jnp.stack([dt_bias, decay_rate]), ((0, 6), (0, 128 - heads)))
    skip = jnp.broadcast_to(jnp.repeat(skip_gain, SSM_DIM), (8, inner))
    attended, lse, kv_all, edge_in, gated, core, x_act, bc_act, state_in, normed_near, cot_near = mixer_forward(
        queries, own_block, edge, x_pre, bc_pre, dt_raw, z_val, seg_column, seg_row, x_conv,
        bc_conv, vectors, skip, normed.T, cotangent.T,
    )
    attended_low = (
        attended.astype(BF16).reshape(q_heads, ROWS, HEAD_DIM).transpose(1, 0, 2)
        .reshape(ROWS, q_heads * HEAD_DIM)
    )
    mixer_part = dot(gated, out_weight) + dot(attended_low, attn_weight)
    hidden_in = x_input + head_sum(mixer_part.astype(BF16), 4).astype(F32)

    normed_two_f, norm_two_back = jax.vjp(rms_norm, hidden_in, norm2_gain)
    normed_two = normed_two_f.astype(BF16)
    gate_val = dot(normed_two, gate_weight)
    up_val = dot(normed_two, up_weight)
    gate_sig = jax.nn.sigmoid(gate_val)
    gate_act = gate_val * gate_sig
    hidden = (gate_act * up_val).astype(BF16)
    grad_hidden = dot(cotangent, down_weight, 1, 1)
    grad_gate = (grad_hidden * up_val * gate_sig * (1.0 + gate_val * (1.0 - gate_sig))).astype(BF16)
    grad_up = (grad_hidden * gate_act).astype(BF16)
    ffn_part = dot(hidden, down_weight).astype(BF16)
    back_part = (dot(grad_gate, gate_weight, 1, 1) + dot(grad_up, up_weight, 1, 1)).astype(BF16)
    grad_from_two, grad_gain_two = norm_two_back(head_sum(back_part, 5).astype(F32))
    grad_hidden_in = grad_from_two + cotangent.astype(F32)
    grad_mix = grad_hidden_in.astype(BF16)
    grad_gated = dot(grad_mix, out_weight, 1, 1)
    grad_attended = (
        dot(grad_mix, attn_weight, 1, 1).astype(BF16).reshape(ROWS, q_heads, HEAD_DIM)
        .transpose(1, 0, 2).reshape(q_heads * ROWS, HEAD_DIM)
    )
    bc_at = head_index * 128
    bc_own = jnp.concatenate(
        [
            lax.dynamic_slice_in_dim(edge_in, inner + bc_at, 128, 1),
            lax.dynamic_slice_in_dim(bc_pre, bc_at, 128, 1),
        ]
    )
    (
        grad_query, grad_kv, grad_z, grad_x_pre, grad_bc_low, grad_dt_raw, grad_x_conv,
        grad_bc_conv, grad_vectors, ffn_w, mix_near,
    ) = mixer_backward(
        queries, grad_attended, attended, lse, seg_row, kv_all, grad_gated, z_val, core, x_act,
        bc_act, x_pre, bc_own, edge_in, dt_raw, state_in, seg_column, x_conv,
        lax.dynamic_slice_in_dim(bc_conv, bc_at, 128, 1), vectors, skip, grad_gate, grad_up,
        hidden, normed_two.T, cotangent.T, cot_near, grad_mix.T,
    )
    score_scale = HEAD_DIM**-0.5
    grad_query = (grad_query * score_scale).reshape(q_heads, ROWS, HEAD_DIM).transpose(1, 0, 2)
    grad_query_raw = (
        rope_turn(grad_query, cosine[:, None, :], -sine[:, None, :]).astype(BF16)
        .reshape(ROWS, q_heads * HEAD_DIM)
    )
    grad_kv_low = jnp.where(
        c == 0, rope_turn(grad_kv * score_scale, cosine, -sine), grad_kv
    ).astype(BF16)
    bc_columns = lax.dynamic_slice_in_dim(bc_weight, bc_at, 128, 1)
    back_part = (
        dot(grad_x_pre, x_weight, 1, 1)
        + dot(grad_z, z_weight, 1, 1)
        + dot(grad_dt_raw, dt_wide, 1, 1)
        + dot(grad_query_raw, query_weight, 1, 1)
        + dot(grad_bc_low, bc_columns, 1, 1)
        + dot(grad_kv_low, kv_columns, 1, 1)
    )
    quarter = MODEL // 4
    small = [
        jnp.zeros((quarter,), F32), grad_x_conv[:CONV], grad_bc_conv[:CONV],
        grad_vectors[0, :heads], grad_vectors[1, :heads], grad_vectors[2, :heads],
        lax.dynamic_slice_in_dim(grad_gain_two, head_index * quarter, quarter),
    ]
    flat = jnp.concatenate([a.reshape(-1) for a in small])
    flat = jnp.pad(flat, (0, SMALL_AT * SMALL - flat.size)).reshape(SMALL_AT, 8, 128)
    output, grad_tokens, mixer_w, gathered, small_sums = finish(
        jnp.concatenate([grad_bc_low, grad_kv_low], 1), grad_x_pre, grad_z, grad_query_raw,
        jnp.pad(grad_dt_raw, ((0, 0), (0, 128))), gated, attended_low, normed.T, normed_near,
        grad_mix.T, mix_near, back_part.astype(BF16), ffn_part, tokens,
        jnp.broadcast_to(norm1_gain, (8, MODEL)), grad_hidden_in, hidden_in, flat,
    )
    bc_w, kv_w = format_replicated(gathered)
    total = small_sums.reshape(2, 2, SMALL_AT, 16, 128)[:, :, :, :8].astype(F32)
    total = total.transpose(1, 0, 2, 3, 4).reshape(4, SMALL_AT * SMALL)
    at = [WIDE, WIDE + inner, WIDE + 2 * inner, 2 * WIDE + 2 * inner, 3 * WIDE + 2 * inner]
    pieces, start = [], 0
    for a in small:
        pieces.append(total[:, start : start + a.size].reshape(4, *a.shape))
        start += a.size
    x_conv_sum = pieces[1].transpose(1, 0, 2).reshape(CONV, 4 * inner)
    bc_conv_sum = pieces[2].transpose(1, 0, 2).reshape(CONV, 512)
    bias_sum, rate_sum, skip_sum, gain_two_sum = (p.reshape(-1) for p in pieces[3:])
    gain_one_sum = pieces[0].reshape(-1)
    ff = gate_weight.shape[1]
    return (
        output,
        grad_tokens,
        gain_one_sum,
        mixer_w[:, at[0] : at[1]],
        mixer_w[:, at[1] : at[2]],
        bc_w,
        mixer_w[:, at[3] : at[3] + heads],
        x_conv_sum,
        bc_conv_sum,
        bias_sum,
        rate_sum,
        skip_sum,
        mixer_w[:, at[4] : at[4] + inner].T,
        mixer_w[:, at[2] : at[3]],
        kv_w,
        mixer_w[:, at[4] + inner :].T,
        gain_two_sum,
        ffn_w[:, :ff],
        ffn_w[:, ff : 2 * ff],
        ffn_w[:, 2 * ff :].T,
    )


def solution(mesh):
    split = Mesh(mesh.devices.reshape(NZ, NX, NY, 2, 2), (*SEQ, "zh", "c"))
    head = ("zh", "c")
    rows, columns, both, turned = P(SEQ, None), P(None, head), P(SEQ, head), P(head, SEQ)
    return jax.shard_map(
        on_device,
        mesh=split,
        in_specs=(
            rows, P(SEQ), rows, P(), columns, columns, P(), columns, columns, P(), P(head),
            P(head), P(head), P(head, None), columns, P(), P(head, None), P(), columns, columns,
            P(head, None),
        ),
        out_specs=(
            rows, rows, P(), both, both, P(), both, P(), P(), P(), P(), P(), turned, both, P(),
            turned, P(), both, both, turned,
        ),
        check_vma=False,
    )
```

time: 738 us -> 486 us (0.66)
  Pallas kernels: 465 us -> 363 us
  local copies, waits for them, and re-layouts: 118 us -> 50.1 us
  other arithmetic: 80.4 us -> 20.8 us
  matrix products: 61.2 us -> 40.4 us
    pallas_call x8 -> x4, Pallas kernels: 389 us -> 319 us  [the longest x1 138 us: mixer_backward(): pl.pallas_call(mixer_backward_kernel, name='mixer_backward', out_shape=(s...]
    pallas_call x3 -> x2, Pallas kernels: 77 us -> 44 us  [head_sum(): pl.pallas_call(head_sum_kernel, name=f'head_sum_{collective_id}', out_sha...]
    dot_general x11 -> x0, matrix products: 18.9 us -> none  [the longest x3 13.7 us: output_part(): inner = jnp.einsum('ijh,jhp->ihp', mixing, moved, precision=HIGHEST)]
    reshape x10 -> x4, local copies, waits for them, and re-layouts: 17.4 us -> 0.72 us  [the longest x1 0.61 us: on_device(): jnp.pad(flat, (0, SMALL_AT * SMALL - flat.size)).reshape(SMALL_AT, 8, 128)]
    mul x11 -> x0, local copies, waits for them, and re-layouts: 15.7 us -> none  [the longest x4 6.51 us: state_part(): moved = x_values * (step_sizes * carry_weight)[:, :, None]]
    another operation x16 -> x3, other arithmetic: 18 us -> 2.33 us
    convert_element_type x10 -> x2, other arithmetic: 14.8 us -> 0.1 us  [the longest x1 0.1 us: on_device(): grad_kv_low = jnp.where(c == 0, rope_turn(grad_kv * score_scale, cosine,...]
    slice x11 -> x2, local copies, waits for them, and re-layouts: 10.5 us -> 0.74 us  [the longest x1 0.74 us: on_device(): grad_x_conv[:CONV]]
where the time goes in v2:
time: 486 us; the launch traced here: 477 us
  Pallas kernels  363 us (75%)
  local copies, waits for them, and re-layouts  50.1 us (10%)
  matrix products  40.4 us (8%)
  other arithmetic  20.8 us (4%)
    pallas_call x1, Pallas kernels, mixer_backward(): pl.pallas_call(mixer_backward_kernel, name='mixer_backward', out_shape=(s...  138 us
    pallas_call x1, Pallas kernels, finish(): pl.pallas_call(finish_kernel, name='finish', out_shape=(s((ROWS, MODEL),...  128 us
    pallas_call x1, Pallas kernels, mixer_forward(): pl.pallas_call(mixer_forward_kernel, name='mixer_forward', out_shape=(s((...  48 us
    pallas_call x2, Pallas kernels, head_sum(): pl.pallas_call(head_sum_kernel, name=f'head_sum_{collective_id}', out_sha...  44 us
    dot_general x22, matrix products, dot(): lax.dot_general(a, b, (((left,), (right,)), ((), ())), preferred_element_...  40.4 us
    unnamed x121, local copies, waits for them, and re-layouts  18.1 us
    transpose x2, local copies, waits for them, and re-layouts, on_device(): grad_query, grad_kv, grad_z, grad_x_pre, grad_bc_low, grad_dt_raw, grad_x...  13 us

profile of v2, /device:TPU:1, one launch (start us, length us, event | category | flops | bytes accessed | tf_op | source)
XLA Modules:
  0.0 476.6 jit_solution(5249409460785137977)
XLA Ops:
  0.7 1.7 fusion.7
  2.4 1.9 fusion.17
  5.0 0.6 fusion.33.own_ref
  5.7 1.2 fusion.23
  6.9 2.2 fusion.51
  9.2 0.7 fusion.54
  9.9 1.0 copy.61
  11.0 1.7 copy.62
  12.7 1.3 subtract_convert_fusion.1
  14.3 0.7 copy.43
  15.0 3.4 convolution_convert_fusion.1.x_ref
  18.5 0.7 convolution_convert_fusion.2.bc_ref
  19.3 0.7 copy-done.29
  20.7 1.3 fusion.44
  22.0 2.3 copy.48.nt_ref
  24.3 4.2 fusion.45.z_ref
  28.6 1.1 fusion.13.dt_ref
  29.7 0.8 broadcast_in_dim.17.seg_ref
  31.1 2.3 copy.47
  34.7 48.0 %mixer_forward.1 = (f32[512,128]{1,0:T(8,128)}, f32[8,512]{1,0:T(8,128)}, bf16[2,32,272,128]{3,2,1,0:T(8,128)(2,1)}, bf16[16,1408]{1,0:T(8,128)(2,1)}, bf16[256,...) custom-call(bf16[512,128]{1,0:T(8,128)(2,1)} %bitcast.109, ...), custom_call_target="tpu_custom_call" | custom-call | tf_op jit(solution)/shard_map/mixer_forward/pallas_call | solution.py:743
  82.7 1.0 convert_element_type.106
  84.4 2.0 fusion.x_ref
  86.4 23.6 %head_sum_4.1 = bf16[256,2048]{1,0:T(8,128)(2,1)} custom-call(bf16[256,2048]{1,0:T(8,128)(2,1)} %fusion.x_ref), custom_call_target="tpu_custom_call" | custom-call | tf_op jit(solution)/shard_map/head_sum_4/pallas_call | solution.py:512
  110.0 3.0 convert_add_fusion
  113.7 1.3 fusion.58
  115.3 1.3 copy-done.52
  116.5 1.3 fusion.57
  117.8 0.9 copy-done.51
  118.7 2.5 multiply_convert_fusion.1
  121.2 1.3 fusion.59
  122.6 2.3 fusion.1.x_ref
  124.8 20.5 %head_sum_5.1 = bf16[256,2048]{1,0:T(8,128)(2,1)} custom-call(bf16[256,2048]{1,0:T(8,128)(2,1)} %fusion.1.x_ref), custom_call_target="tpu_custom_call" | custom-call | tf_op jit(solution)/shard_map/head_sum_5/pallas_call | solution.py:512
  145.3 2.3 fusion.6
  147.6 2.7 convert_bitcast_fusion.1
  150.3 11.7 %copy.52.mt_ref = bf16[2048,256]{1,0:T(8,128)(2,1)} copy(bf16[2048,256]{0,1:T(8,128)(2,1)} %get-tuple-element.100) | data formatting | bytes 2097152 | tf_op jit(solution)/shard_map/transpose | solution.py:1562
  162.0 3.7 fusion.38.gg_ref
  166.2 0.8 copy.50
  166.9 1.3 copy.51.ft_ref
  168.3 0.7 constant_dynamic-slice_fusion.2
  168.9 0.8 constant_dynamic-slice_fusion.1
  169.8 0.6 pad_maximum_fusion.2.bcown_ref
  170.4 1.3 constant_dynamic-slice_fusion.bctaps_ref
  171.7 137.6 %mixer_backward.1 = (f32[512,128]{1,0:T(8,128)}, f32[256,128]{1,0:T(8,128)}, bf16[256,768]{1,0:T(8,128)(2,1)}, bf16[256,768]{1,0:T(8,128)(2,1)}, bf16[256,128]{1...) custom-call(bf16[512,128]{1,0:T(8,128)(2,1)} %bitcast.110, ...), custom_call_target="tpu_custom_call" | custom-call | tf_op jit(solution)/shard_map/mixer_backward/pallas_call | solution.py:1126
  309.2 0.7 slice.110
  310.0 0.7 slice_bitcast_fusion.6
  310.7 0.8 slice_bitcast_fusion.7
  312.2 3.2 fusion.60
  315.4 1.0 convolution_add_fusion
  319.4 1.5 convolution_add_fusion.3
  321.7 2.6 fusion.2.back_ref
  324.3 0.7 copy_bitcast_fusion.1
  325.0 0.7 pad_maximum_fusion.misc_ref
  325.7 0.7 pad.23.ddt_ref
  326.4 2.3 convolution_convert_fusion.ffn_ref
  328.7 0.6 broadcast_in_dim.22.gain_ref
  329.3 127.6 %finish.1 = (bf16[256,2048]{1,0:T(8,128)(2,1)}, f32[256,2048]{1,0:T(8,128)}, f32[64,3328]{1,0:T(8,128)}, bf16[2,16,4,64,256]{4,3,2,1,0:T(8,128)(2,1)}, bf16[2,10,16,128]{3,2,1,0:T(8,128)(2,1)}) custom-call(bf16[256,256]{1,0:T(8,128)(2,1)} %pad_maximum_fusion.misc_ref, bf16[256,768]{1,0:T(8,128)(2,1)} %get-tuple-element.61.dx_ref, ...), custom_call_target="tpu_custom_call" | custom-call | tf_op jit(solution)/shard_map/finish/pallas_call | solution.py:1402
  456.9 6.1 %format_replicated.1 = (f32[2048,512]{1,0:T(8,128)}, f32[2048,512]{1,0:T(8,128)}) custom-call(bf16[2,16,2,2,64,256]{5,4,3,2,1,0:T(8,128)(2,1)} %bitcast.106), custom_call_target="tpu_custom_call" | custom-call | tf_op jit(solution)/shard_map/format_replicated/pallas_call | solution.py:1449
  463.1 0.8 slice_bitcast_fusion.1
  464.0 0.6 copy.67
  468.3 0.7 slice_bitcast_fusion.2
  469.0 0.7 copy.59
  469.7 0.9 slice_bitcast_fusion
  470.6 2.5 copy.80
  473.0 3.1 copy.81
  (157 shorter events, 14.0 us)
Async XLA Ops:
  0.7 83.7 %copy-start = (bf16[768,2048]{1,0:T(8,128)(2,1)S(1)}, bf16[768,2048]{1,0:T(8,128)(2,1)}, u32[]{:S(2)}) copy-start(bf16[768,2048]{1,0:T(8,128)(2,1)} %param.34) | copy-start | bytes 9437188
  0.7 4.3 copy-start.46
  2.4 4.6 copy-start.37
  2.4 6.8 %copy-start.41 = (f32[256]{0:T(256)}, f32[256]{0:T(256)S(1)}, u32[]{:S(2)}) copy-start(f32[256]{0:T(256)S(1)} %add_rsqrt_fusion) | copy-start | bytes 3076
  4.3 4.9 %copy-start.39 = (f32[64]{0:T(128)}, f32[64]{0:T(128)S(1)}, u32[]{:S(2)}) copy-start(f32[64]{0:T(128)S(1)} %negate_power_fusion) | copy-start | bytes 772
  5.0 4.9 %copy-start.44 = (bf16[256]{0:T(256)(128)(2,1)}, bf16[256]{0:T(256)(128)(2,1)S(1)}, u32[]{:S(2)}) copy-start(bf16[256]{0:T(256)(128)(2,1)S(1)} %get-tuple-element.138) | copy-start | bytes 1540
  6.9 5.8 %copy-start.19 = (f32[256,64]{1,0:T(8,128)}, f32[256,64]{1,0:T(8,128)S(1)}, u32[]{:S(2)}) copy-start(f32[256,64]{1,0:T(8,128)S(1)} %get-tuple-element.136) | copy-start | bytes 196612
  15.0 3.4 copy-start.2
  15.0 3.4 copy-start.33
  15.0 3.5 copy-start.42
  18.4 0.8 copy-start.14
  18.5 1.5 copy-start.45
  19.3 0.7 copy-start.29
  20.7 3.5 copy-start.43
  24.3 4.3 copy-start.3
  24.3 4.3 copy-start.35
  28.5 4.8 %copy-start.47 = (f32[12]{0:T(128)S(1)}, f32[12]{0:T(128)}, u32[]{:S(2)}) copy-start(f32[12]{0:T(128)} %param.33) | copy-start | bytes 148
  28.5 5.6 %copy-start.48 = (f32[12]{0:T(128)S(1)}, f32[12]{0:T(128)}, u32[]{:S(2)}) copy-start(f32[12]{0:T(128)} %param.32) | copy-start | bytes 148
  28.6 5.6 %copy-start.49 = (f32[12]{0:T(128)S(1)}, f32[12]{0:T(128)}, u32[]{:S(2)}) copy-start(f32[12]{0:T(128)} %param.31) | copy-start | bytes 148
  34.7 49.2 %copy-start.8 = (bf16[256,2048]{1,0:T(8,128)(2,1)S(1)}, bf16[256,2048]{1,0:T(8,128)(2,1)}, u32[]{:S(2)}) copy-start(bf16[256,2048]{1,0:T(8,128)(2,1)} %param.37) | copy-start | bytes 3145732
  82.7 1.6 copy-start.15
  83.9 2.5 copy-start.17
  86.4 23.6 %copy-start.4 = (bf16[256,2048]{1,0:T(8,128)(2,1)S(1)}, bf16[256,2048]{1,0:T(8,128)(2,1)}, u32[]{:S(2)}) copy-start(bf16[256,2048]{1,0:T(8,128)(2,1)} %tok_ref.1) | copy-start | bytes 3145732
  110.0 3.1 copy-start.6
  110.0 3.1 copy-start.34
  110.0 3.6 copy-start.50
  113.6 4.2 copy-start.11
  113.6 1.6 copy-start.10
  113.7 2.9 copy-start.52
  116.5 2.2 copy-start.51
  121.2 1.3 copy-start.25
  121.2 1.4 copy-start.26
  145.3 2.3 copy-start.7
  162.0 3.7 copy-start.5
  162.0 3.7 copy-start.9
  165.7 1.2 copy-start.12
  312.2 3.2 copy-start.13
  312.2 3.2 copy-start.16
  315.4 1.1 copy-start.30
  315.4 1.1 copy-start.36
  316.5 1.0 copy-start.32
  316.5 1.2 copy-start.20
  316.5 1.2 copy-start.28
  316.9 1.6 copy-start.21
  318.6 0.8 copy-start.31
  319.4 1.5 copy-start.27
  319.4 1.6 copy-start.40
  321.6 2.7 copy-start.18
  321.7 4.7 copy-start.24
  321.7 4.7 copy-start.53
  456.9 6.2 %copy-start.23 = (f32[64,3328]{1,0:T(8,128)S(1)}, f32[64,3328]{1,0:T(8,128)}, u32[]{:S(2)}) copy-start(f32[64,3328]{1,0:T(8,128)} %get-tuple-element.73) | copy-start | bytes 2555908
  456.9 7.0 %copy-start.38 = (bf16[2,10,16,128]{3,2,1,0:T(8,128)(2,1)S(1)}, bf16[2,10,16,128]{3,2,1,0:T(8,128)(2,1)}, u32[]{:S(2)}) copy-start(bf16[2,10,16,128]{3,2,1,0:T(8,128)(2,1)} %get-tuple-element.72) | copy-start | bytes 245764
  463.1 6.6 %copy-start.22 = (f32[64,3072]{1,0:T(8,128)S(1)}, f32[64,3072]{1,0:T(8,128)}, u32[]{:S(2)}) copy-start(f32[64,3072]{1,0:T(8,128)} %get-tuple-element.77) | copy-start | bytes 2359300
  470.6 5.6 %copy-start.1 = (bf16[768,2048]{1,0:T(8,128)(2,1)S(1)}, bf16[768,2048]{1,0:T(8,128)(2,1)}, u32[]{:S(2)}) copy-start(bf16[768,2048]{1,0:T(8,128)(2,1)} %param.34) | copy-start | bytes 9437188
